TPU v7x, 256 devices: a whole 4x4x8 slice. The times are simulated.
256 devices in a mesh: dp: 64 (over y, z, core), mp: 4 (over x).
Axes of the slice: x: 4, y: 4, z: 8, core: 2. Of those that a mesh axis runs over, the one named last changes fastest.
Arguments:
- queries: bfloat16 [8192, 4096], P('dp', 'mp'), may hold values from -6 to 6
- cotangent: bfloat16 [8192, 4096], P('dp', 'mp'), may hold values from -6 to 6
- neighbours: bfloat16 [128, 2, 128, 896], P('dp', None, 'mp'), may hold values from -16 to 16
- present: int32 [128, 2], P('dp'), may hold values 0 or 1
- key_weight: bfloat16 [896, 4096], P(None, 'mp'), may hold values from -0.1875 to 0.1875
- value_weight: bfloat16 [896, 4096], P(None, 'mp'), may hold values from -0.1875 to 0.1875
Outputs:
- attended: bfloat16 [8192, 4096], P('dp', 'mp')
- query_grad: bfloat16 [8192, 4096], P('dp', 'mp')
- neighbour_grad: float32 [128, 2, 128, 896], P('dp', None, 'mp')
- key_weight_grad: float32 [896, 4096], P('dp', 'mp')
- value_weight_grad: float32 [896, 4096], P('dp', 'mp')
All inputs are finite; a program needn't handle non-finite values. No bound on the sum of `present` on one device may be relied on, other than what follows from the above.
Results may differ from a plain program's by a relative error of at most 0.014.
Values may be sent and summed in bfloat16 or wider, within the bound.
No kernel may reach another device: no remote copies, remote signals or barrier semaphores. Data moves between devices by JAX's collectives and lax.ppermute only.
A program may use at most 128 MiB of HBM per device.

v0:
```python
import jax
import jax.numpy as jnp
from jax import lax
from jax.sharding import PartitionSpec as P

HEAD = 128


def shards(queries, cotangent, neighbours, present, key_weight, value_weight):
    score_scale = HEAD ** (-0.5)
    gathered = lax.all_gather(neighbours, "mp", axis=2, tiled=True)
    stretch_count, neigh_count, pass_len, enc_width = gathered.shape
    key_span = neigh_count * pass_len
    row_count = stretch_count * key_span
    local_width = key_weight.shape[1]
    head_count = local_width // HEAD
    stretch_len = queries.shape[0] // stretch_count
    flat_rows = gathered.reshape(row_count, enc_width)
    key_rows = jnp.dot(flat_rows, key_weight, preferred_element_type=jnp.float32).astype(
        jnp.bfloat16
    )
    value_rows = jnp.dot(flat_rows, value_weight, preferred_element_type=jnp.float32).astype(
        jnp.bfloat16
    )
    query_heads = queries.reshape(stretch_count, stretch_len, head_count, HEAD)
    grad_heads = cotangent.reshape(stretch_count, stretch_len, head_count, HEAD)
    key_heads = key_rows.reshape(stretch_count, key_span, head_count, HEAD)
    value_heads = value_rows.reshape(stretch_count, key_span, head_count, HEAD)
    scores = (
        jnp.einsum("cthd,crhd->chtr", query_heads, key_heads, preferred_element_type=jnp.float32)
        * score_scale
    )
    live_keys = jnp.repeat(present.astype(jnp.float32), pass_len, axis=1)
    raw_weights = jnp.exp(scores) * live_keys[:, None, None, :]
    no_keys = (jnp.sum(present, axis=1) == 0).astype(jnp.float32)
    weights = raw_weights / (
        jnp.sum(raw_weights, axis=-1, keepdims=True) + no_keys[:, None, None, None]
    )
    weights_low = weights.astype(jnp.bfloat16)
    attended = jnp.einsum(
        "chtr,crhd->cthd", weights_low, value_heads, preferred_element_type=jnp.float32
    )
    attended = attended.astype(jnp.bfloat16).reshape(queries.shape)
    prob_grad = jnp.einsum(
        "cthd,crhd->chtr", grad_heads, value_heads, preferred_element_type=jnp.float32
    )
    row_delta = jnp.sum(weights * prob_grad, axis=-1, keepdims=True)
    score_grad = (weights * (prob_grad - row_delta) * score_scale).astype(jnp.bfloat16)
    value_grad = jnp.einsum(
        "chtr,cthd->crhd", weights_low, grad_heads, preferred_element_type=jnp.float32
    ).astype(jnp.bfloat16)
    query_grad = jnp.einsum(
        "chtr,crhd->cthd", score_grad, key_heads, preferred_element_type=jnp.float32
    ).astype(jnp.bfloat16)
    key_grad = jnp.einsum(
        "chtr,cthd->crhd", score_grad, query_heads, preferred_element_type=jnp.float32
    ).astype(jnp.bfloat16)
    key_grad_rows = key_grad.reshape(row_count, local_width)
    value_grad_rows = value_grad.reshape(row_count, local_width)
    both_grads = jnp.concatenate([key_grad_rows, value_grad_rows], axis=1)
    contract_rows = (((0,), (0,)), ((), ()))
    partial_grads = lax.dot_general(
        flat_rows, both_grads, contract_rows, preferred_element_type=jnp.float32
    )
    summed = lax.psum_scatter(partial_grads, "dp", scatter_dimension=0, tiled=True)
    contract_cols = (((1,), (1,)), ((), ()))
    passage_grad = lax.dot_general(
        key_grad_rows, key_weight, contract_cols, preferred_element_type=jnp.float32
    )
    passage_grad = passage_grad + lax.dot_general(
        value_grad_rows, value_weight, contract_cols, preferred_element_type=jnp.float32
    )
    passage_grad = passage_grad.reshape(stretch_count, neigh_count, pass_len, enc_width)
    neighbour_grad = lax.psum_scatter(
        passage_grad.astype(jnp.bfloat16), "mp", scatter_dimension=2, tiled=True
    ).astype(jnp.float32)
    query_grad = query_grad.reshape(queries.shape)
    return (attended, query_grad, neighbour_grad, summed[:, :local_width], summed[:, local_width:])


def solution(mesh):
    placed = (
        P("dp", "mp"),
        P("dp", "mp"),
        P("dp", None, "mp", None),
        P("dp", None),
        P(None, "mp"),
        P(None, "mp"),
    )
    return jax.shard_map(
        shards,
        mesh=mesh,
        in_specs=placed,
        out_specs=(
            P("dp", "mp"),
            P("dp", "mp"),
            P("dp", None, "mp", None),
            P("dp", "mp"),
            P("dp", "mp"),
        ),
        check_vma=False,
    )
```

profile of v0, /device:TPU:1, one launch (start us, length us, event | category | flops | bytes accessed | tf_op | source)
XLA Modules:
  0.0 274.7 jit_solution(4062452152025861231)
XLA Ops:
  8.1 13.8 %all_gather.3 = bf16[2,2,128,896]{3,2,1,0:T(8,128)(2,1)S(1)} all-gather(bf16[2,2,32,896]{3,2,1,0:T(8,128)(2,1)} %param.8), channel_id=1, replica_groups=mesh['dp'=64,'mp'=4] {'mp'}, dimensions={2}, use_global_device_ids=true | all-gather | bytes 1146880 | tf_op jit(solution)/shard_map/all_gather | solution.py:11
  21.9 3.1 %fusion.4 = bf16[64,8,8,128]{3,1,2,0:T(8,128)(2,1)S(1)} fusion(bf16[512,896]{1,0:T(8,128)(2,1)S(1)} %bitcast.80, bf16[896,1024]{1,0:T(8,128)(2,1)} %param.11), kind=kOutput, calls=%fused_computation.10 | convolution fusion | flops 940048384 | bytes 3801088 | tf_op jit(solution)/shard_map/dot_general | solution.py:22
  25.0 0.3 copy.54
  25.3 0.7 copy-done.8
  26.0 1.3 fusion.5
  27.3 0.3 copy.51
  27.6 0.4 copy-done.10
  28.3 1.5 convolution_bitcast_fusion.1
  29.8 0.6 fusion.41
  30.5 0.9 copy-done.13
  31.4 1.8 fusion.7
  33.2 9.4 %fusion.6 = bf16[2,256,8,128]{3,1,2,0:T(8,128)(2,1)} fusion(f32[2,8,64,256]{3,2,1,0:T(8,128)} %convolution_bitcast_fusion.1, bf16[2,64,8,128]{3,2,1,0:T(8,128)(2,1)S(1)} %bitcast.86, f32[2,8,64,256]{3,2,1,0:T(8,128)} %copy-done.13, f32[2,8,64]{2,1,0:T(8,128)S(1)} %broadcast_add_fusion), kind=kOutput, calls=%fused_computation.12 | convolution fusion | flops 69469440 | bytes 3411968 | tf_op jit(solution)/shard_map/chtr,cthd->crhd/dot_general | solution.py:55
  42.6 1.9 copy.44
  44.5 1.3 fusion.38
  45.8 0.3 copy-done.5
  46.1 0.7 copy.46
  46.8 0.8 copy-done.11
  47.6 2.3 add_convert_fusion
  49.9 0.2 all-reduce.3.cloned.1.call-start
  50.2 1.6 copy.87
  51.8 0.3 copy.88
  52.1 5.4 %convolution_bitcast_fusion = f32[896,2048]{0,1:T(8,128)} fusion(bf16[512,896]{1,0:T(8,128)(2,1)S(1)} %bitcast.82, bf16[512,1024]{1,0:T(8,128)(2,1)S(1)} %bitcast.75, bf16[512,1024]{1,0:T(8,128)(2,1)S(1)} %bitcast.76), kind=kOutput, calls=%fused_computation.1 | convolution fusion | flops 1883242496 | bytes 10354688 | tf_op jit(solution)/shard_map/dot_general | solution.py:62
  57.6 8.0 %fusion.16 = bf16[2,64,8,128]{3,1,2,0:T(8,128)(2,1)S(1)} fusion(f32[2,8,64,256]{3,2,1,0:T(8,128)} %convolution_bitcast_fusion.1, bf16[2,256,8,128]{3,2,1,0:T(8,128)(2,1)} %bitcast.74, f32[2,8,64,256]{3,2,1,0:T(8,128)} %copy-done.13, f32[2,8,64]{2,1,0:T(8,128)S(1)} %broadcast_add_fusion), kind=kOutput, calls=%fused_computation.26 | convolution fusion | flops 69076224 | bytes 3411968 | tf_op jit(solution)/shard_map/chtr,crhd->cthd/dot_general | solution.py:52
  65.8 1.6 fusion.15
  67.6 0.6 dynamic-slice
  68.8 0.9 copy_bitcast_fusion.2
  69.7 9.3 %reduce-scatter.3.cloned.1.call-done = bf16[2,2,32,896]{3,2,1,0:T(8,128)(2,1)} async-done(((bf16[2,2,128,896]{3,2,1,0:T(8,128)(2,1)}), bf16[2,2,32,896]{3,2,1,0:T(8,128)(2,1)}) %reduce-scatter.3.cloned.1.call-update) | async-done | bytes 229392 | tf_op jit(solution)/shard_map/reduce_scatter | solution.py:74
  79.0 1.7 convert_element_type.71
  80.7 183.0 %all-reduce.3.cloned.1.call-done = f32[896,2048]{0,1:T(8,128)} async-done(((f32[896,2048]{0,1:T(8,128)}), f32[896,2048]{0,1:T(8,128)}) %all-reduce.3.cloned.1.call-update) | async-done | bytes 7340048
  263.7 1.9 fusion.39
  265.6 0.8 copy.47
  266.4 0.8 copy.48
  (35 shorter events, 0.9 us)
Async XLA Ops:
  8.0 18.0 %copy-start = (bf16[896,1024]{1,0:T(8,128)(2,1)S(1)}, bf16[896,1024]{1,0:T(8,128)(2,1)}, u32[]{:S(2)}) copy-start(bf16[896,1024]{1,0:T(8,128)(2,1)} %param.10) | copy-start | bytes 5505028
  8.0 71.0 %reduce-scatter.3.cloned.1.call-start = ((), (), s32[]{:S(2)}) async-start(), calls=%async_computation.1 | async-start | bytes 1146880 | tf_op jit(solution)/shard_map/reduce_scatter | solution.py:74
  21.9 4.1 %copy-start.6 = (bf16[2,2,128,896]{3,2,1,0:T(8,128)(2,1)}, bf16[2,2,128,896]{3,2,1,0:T(8,128)(2,1)S(1)}, u32[]{:S(2)}) copy-start(bf16[2,2,128,896]{3,2,1,0:T(8,128)(2,1)S(1)} %all_gather.3) | copy-start | bytes 2752516
  25.0 1.0 copy-start.8
  27.3 0.7 copy-start.10
  27.3 1.0 copy-start.9
  28.0 2.4 copy-start.4
  30.4 1.0 copy-start.13
  44.5 1.3 copy-start.1
  44.5 1.6 copy-start.5
  46.1 1.5 copy-start.11
  46.8 3.1 %copy-start.3 = (bf16[2,256,8,128]{3,2,1,0:T(8,128)(2,1)}, bf16[2,256,8,128]{3,2,1,0:T(8,128)(2,1)S(1)}, u32[]{:S(2)}) copy-start(bf16[2,256,8,128]{3,2,1,0:T(8,128)(2,1)S(1)} %copy.46) | copy-start | bytes 3145732
  49.9 213.7 %all-reduce.3.cloned.1.call-start = ((), (), s32[]{:S(2)}) async-start(), calls=%async_computation.2 | async-start | bytes 14680064
  50.2 1.7 copy-start.2
  50.2 1.9 copy-start.7
  65.7 1.9 copy-start.12
Sparse Core Ops, SparseCore 0:
  50.1 28.8 reduce-scatter.2
Sparse Core Ops, SparseCore 1:
  57.6 206.0 all-reduce.2
where the time goes:
time: 276 us; the launch traced here: 275 us
  waiting for transfers between devices  192 us (70%)
  matrix products  36.3 us (13%)
  between operations  16.4 us (6%)
  blocking collectives  13.8 us (5%)
  local copies, waits for them, and re-layouts  13.7 us (5%)
    unnamed x3, waiting for transfers between devices  183 us
    all_gather x1, blocking collectives, shards(): gathered = lax.all_gather(neighbours, 'mp', axis=2, tiled=True)  13.8 us
    dot_general x1, matrix products, shards(): jnp.einsum('chtr,cthd->crhd', score_grad, query_heads, preferred_element_...  9.38 us
    reduce_scatter x1, waiting for transfers between devices, shards(): lax.psum_scatter(passage_grad.astype(jnp.bfloat16), 'mp', scatter_dimensi...  9.27 us
    unnamed x39, local copies, waits for them, and re-layouts  8.01 us
    dot_general x1, matrix products, shards(): jnp.einsum('chtr,crhd->cthd', score_grad, key_heads, preferred_element_ty...  7.99 us
  transfers between devices with their start and end apart: 2, of which 2 were waited for; matrix products, arithmetic and copies ran while one was open for 7% of the time, Pallas kernels for 0%

commit v1 on v0

v1 whole, which is shorter than its diff:
```python
import jax
import jax.numpy as jnp
from jax import lax
from jax.experimental import pallas as pl
from jax.experimental.pallas import tpu as pltpu
from jax.sharding import Mesh, PartitionSpec as P

HEAD = 128
BF = jnp.bfloat16
F32 = jnp.float32
NT = (((1,), (1,)), ((), ()))
TN = (((0,), (0,)), ((), ()))
VMEM_LIMIT = 48 * 1024 * 1024


def ring(size, step):
    return [(i, (i + step) % size) for i in range(size)]


def dot(a, b, dims=(((1,), (0,)), ((), ()))):
    return lax.dot_general(a, b, dims, preferred_element_type=F32)


def attend_body(
    stretches, span, group, steps,
    flags, rows, key_w, value_w, queries, cotangent,
    attended, query_grad, keep, send, passage, total,
):
    step = pl.program_id(0)
    core = flags[0]
    tokens = queries.shape[0] // stretches
    scale = HEAD ** (-0.5)
    keys = dot(rows[...], key_w[...]).astype(BF)
    values = dot(rows[...], value_w[...]).astype(BF)
    neigh = (lax.broadcasted_iota(jnp.int32, (1, span), 1) // group) % 2
    key_grads, value_grads = [], []
    for c in range(stretches):
        first, second = flags[1 + 2 * c], flags[2 + 2 * c]
        live = jnp.where(neigh == 0, first, second).astype(F32)
        empty = jnp.where(first + second == 0, 1.0, 0.0).astype(F32)
        r = slice(c * span, (c + 1) * span)
        t = slice(c * tokens, (c + 1) * tokens)
        kg_heads, vg_heads = [], []
        for h in range(queries.shape[1] // HEAD):
            w = slice(h * HEAD, (h + 1) * HEAD)
            q, g = queries[t, w], cotangent[t, w]
            k, v = keys[r, w], values[r, w]
            raw = jnp.exp(dot(q, k, NT) * scale) * live
            probs = raw / (jnp.sum(raw, axis=-1, keepdims=True) + empty)
            low = probs.astype(BF)
            attended[t, w] = dot(low, v).astype(BF)
            prob_grad = dot(g, v, NT)
            delta = jnp.sum(probs * prob_grad, axis=-1, keepdims=True)
            score_grad = (probs * (prob_grad - delta) * scale).astype(BF)
            query_grad[t, w] = dot(score_grad, k).astype(BF)
            vg_heads.append(dot(low, g, TN).astype(BF))
            kg_heads.append(dot(score_grad, q, TN).astype(BF))
        key_grads.append(jnp.concatenate(kg_heads, axis=1))
        value_grads.append(jnp.concatenate(vg_heads, axis=1))
    key_grad = jnp.concatenate(key_grads, axis=0)
    value_grad = jnp.concatenate(value_grads, axis=0)

    @pl.when(core == 0)
    def _():
        keep[...] = key_grad
        send[...] = value_grad

    @pl.when(core != 0)
    def _():
        keep[...] = value_grad
        send[...] = key_grad

    part = dot(key_grad, key_w[...], NT) + dot(value_grad, value_w[...], NT)

    @pl.when(step == 0)
    def _():
        total[...] = part

    @pl.when(step > 0)
    def _():
        total[...] += part

    @pl.when(step == steps - 1)
    def _():
        passage[...] = total[...].astype(BF)


def attend(flags, rows, key_w, value_w, queries, cotangent, stretches, group):
    row_count, enc = rows.shape
    tokens, width = queries.shape
    block = 2 * HEAD
    steps = width // block
    span = row_count // stretches

    def body(*refs):
        attend_body(stretches, span, group, steps, *refs)

    columns = lambda n: pl.BlockSpec((n, block), lambda i: (0, i))
    whole = pl.BlockSpec((row_count, enc), lambda i: (0, 0))
    return pl.pallas_call(
        body,
        grid=(steps,),
        in_specs=[
            pl.BlockSpec(memory_space=pltpu.SMEM),
            whole,
            columns(enc),
            columns(enc),
            columns(tokens),
            columns(tokens),
        ],
        out_specs=[
            columns(tokens),
            columns(tokens),
            columns(row_count),
            columns(row_count),
            whole,
        ],
        out_shape=[
            jax.ShapeDtypeStruct((tokens, width), BF),
            jax.ShapeDtypeStruct((tokens, width), BF),
            jax.ShapeDtypeStruct((row_count, width), BF),
            jax.ShapeDtypeStruct((row_count, width), BF),
            jax.ShapeDtypeStruct((row_count, enc), BF),
        ],
        scratch_shapes=[pltpu.VMEM((row_count, enc), F32)],
        compiler_params=pltpu.CompilerParams(
            vmem_limit_bytes=VMEM_LIMIT, dimension_semantics=("arbitrary",)
        ),
    )(flags, rows, key_w, value_w, queries, cotangent)


def weight_body(place, rows, rows_other, grads, grads_other, mine, away, total):
    pieces, height, _ = away.shape
    total[...] = dot(rows[...], grads[...], TN) + dot(rows_other[...], grads_other[...], TN)
    y = place[0]
    for k in range(pieces + 1):
        start = pl.multiple_of(lax.rem(y + k, pieces + 1) * height, 8)
        piece = total[pl.ds(start, height), :]
        if k == 0:
            mine[...] = piece
        else:
            away[k - 1] = piece.astype(BF)


def weight_grad(place, rows, rows_other, grads, grads_other, parts):
    row_count, enc = rows.shape
    width = grads.shape[1]
    block = 512
    height = enc // parts
    columns = pl.BlockSpec((row_count, block), lambda i: (0, i))
    whole = pl.BlockSpec((row_count, enc), lambda i: (0, 0))
    return pl.pallas_call(
        weight_body,
        grid=(width // block,),
        in_specs=[pl.BlockSpec(memory_space=pltpu.SMEM), whole, whole, columns, columns],
        out_specs=[
            pl.BlockSpec((height, block), lambda i: (0, i)),
            pl.BlockSpec((parts - 1, height, block), lambda i: (0, 0, i)),
        ],
        out_shape=[
            jax.ShapeDtypeStruct((height, width), F32),
            jax.ShapeDtypeStruct((parts - 1, height, width), BF),
        ],
        scratch_shapes=[pltpu.VMEM((enc, block), F32)],
        compiler_params=pltpu.CompilerParams(
            vmem_limit_bytes=VMEM_LIMIT, dimension_semantics=("arbitrary",)
        ),
    )(place, rows, rows_other, grads, grads_other)


def fold_body(place, mine, *refs):
    arrived, (own, away) = refs[:-2], refs[-2:]
    pieces, padded, width = away.shape
    height = own.shape[0]
    z = place[1]
    total = mine[...]
    for a in arrived:
        total = total + a[...].astype(F32)
    pad = jnp.zeros((padded - height, width), F32)
    for j in range(pieces + 1):
        piece = total[j * height : (j + 1) * height]
        slot = lax.rem(j - z + pieces + 1, pieces + 1)

        @pl.when(slot == 0)
        def _():
            own[...] = piece

        @pl.when(slot != 0)
        def _():
            away[slot - 1] = jnp.concatenate([piece, pad], axis=0).astype(BF)


def fold(place, mine, arrived, parts):
    height, width = mine.shape[0] // parts, mine.shape[1]
    vmem = pl.BlockSpec(memory_space=pltpu.VMEM)
    return pl.pallas_call(
        fold_body,
        in_specs=[pl.BlockSpec(memory_space=pltpu.SMEM)] + [vmem] * (1 + len(arrived)),
        out_specs=[vmem, vmem],
        out_shape=[
            jax.ShapeDtypeStruct((height, width), F32),
            jax.ShapeDtypeStruct((parts - 1, 32, width), BF),
        ],
        compiler_params=pltpu.CompilerParams(vmem_limit_bytes=VMEM_LIMIT),
    )(place, mine, *arrived)


def shards(queries, cotangent, neighbours, present, key_weight, value_weight):
    stretch_count, neigh_count, group, enc = neighbours.shape
    ny, nz, nx = 4, 8, 4
    y, z, core = lax.axis_index("y"), lax.axis_index("z"), lax.axis_index("c")
    place = jnp.stack([y, z])
    flags = jnp.concatenate([core[None], present.reshape(-1)]).astype(jnp.int32)
    swap = [(0, 1), (1, 0)]

    slab = neighbours.reshape(stretch_count, neigh_count * group, enc)
    slabs = [slab] + [lax.ppermute(slab, "x", ring(nx, k)) for k in (1, 3, 2)]
    rows = jnp.stack(slabs, axis=1).reshape(-1, enc)
    rows_other = lax.ppermute(rows, "c", swap)

    attended, query_grad, keep, send, passage = attend(
        flags, rows, key_weight, value_weight, queries, cotangent, stretch_count, group
    )
    grads_other = lax.ppermute(send, "c", swap)

    passage = passage.reshape(stretch_count, nx, neigh_count * group, enc)
    returned = [lax.ppermute(passage[:, s], "x", ring(nx, k)) for s, k in ((1, 3), (2, 1), (3, 2))]
    neighbour_grad = passage[:, 0].astype(F32)
    for r in returned:
        neighbour_grad = neighbour_grad + r.astype(F32)
    neighbour_grad = neighbour_grad.reshape(neighbours.shape)

    mine, away = weight_grad(place, rows, rows_other, keep, grads_other, ny)
    arrived = [lax.ppermute(away[k - 1], "y", ring(ny, k)) for k in (2, 1, 3)]
    own, further = fold(place, mine, arrived, nz)
    height = own.shape[0]
    summed = own
    for k in (4, 3, 5, 2, 6, 1, 7):
        summed = summed + lax.ppermute(further[k - 1], "z", ring(nz, k))[:height].astype(F32)
    half = height // 2
    low, high = summed[:half], summed[half:]
    first = core == 0
    other = lax.ppermute(jnp.where(first, high, low), "c", swap)
    stay = jnp.where(first, low, high)
    return (
        attended,
        query_grad,
        neighbour_grad,
        jnp.where(first, stay, other),
        jnp.where(first, other, stay),
    )


def solution(mesh):
    mesh = Mesh(mesh.devices.reshape(4, 8, 2, 4), ("y", "z", "c", "x"))
    dp = ("y", "z", "c")
    placed = (
        P(dp, "x"),
        P(dp, "x"),
        P(dp, None, "x", None),
        P(dp, None),
        P(None, "x"),
        P(None, "x"),
    )
    return jax.shard_map(
        shards,
        mesh=mesh,
        in_specs=placed,
        out_specs=(
            P(dp, "x"),
            P(dp, "x"),
            P(dp, None, "x", None),
            P(dp, "x"),
            P(dp, "x"),
        ),
        check_vma=False,
    )
```

time: 276 us -> 101 us (0.37)
  the two profiles are of different devices: /device:TPU:1 before, /device:TPU:96 now
where the time goes in v1:
time: 101 us
  waiting for transfers between devices  41 us (41%)
  starting transfers between devices  32.3 us (32%)
  Pallas kernels  20.6 us (20%)
  local copies, waits for them, and re-layouts  3.18 us (3%)
  other arithmetic  2.85 us (3%)
    ppermute x3, waiting for transfers between devices, shards(): arrived = [lax.ppermute(away[k - 1], 'y', ring(ny, k)) for k in (2, 1, 3)]  21.1 us
    ppermute x7, starting transfers between devices, shards(): lax.ppermute(further[k - 1], 'z', ring(nz, k))[:height].astype(F32)  17 us
    pallas_call x1, Pallas kernels, attend(): pl.pallas_call(body, grid=(steps,), in_specs=[pl.BlockSpec(memory_space=p...  14.8 us
    ppermute x3, waiting for transfers between devices, shards(): slabs = [slab] + [lax.ppermute(slab, 'x', ring(nx, k)) for k in (1, 3, 2)]  8.22 us
    ppermute x3, waiting for transfers between devices, shards(): lax.ppermute(passage[:, s], 'x', ring(nx, k))  8.08 us
    ppermute x3, starting transfers between devices, shards(): arrived = [lax.ppermute(away[k - 1], 'y', ring(ny, k)) for k in (2, 1, 3)]  5.29 us
    ppermute x3, starting transfers between devices, shards(): slabs = [slab] + [lax.ppermute(slab, 'x', ring(nx, k)) for k in (1, 3, 2)]  5.14 us
    pallas_call x1, Pallas kernels, weight_grad(): pl.pallas_call(weight_body, grid=(width // block,), in_specs=[pl.BlockSpe...  4.84 us
  transfers between devices with their start and end apart: 19, of which 9 were waited for; matrix products, arithmetic and copies ran while one was open for 2% of the time, Pallas kernels for 0%

profile of v1, /device:TPU:96, one launch (start us, length us, event | category | flops | bytes accessed | tf_op | source)
XLA Modules:
  0.0 100.8 jit_solution(15274463098543318427)
XLA Ops:
  0.7 3.1 %collective-permute-start.2 = (bf16[2,64,896]{2,1,0:T(8,128)(2,1)}, bf16[2,64,896]{2,1,0:T(8,128)(2,1)S(1)}, u32[]{:S(2)}, u32[]{:S(2)}) collective-permute-start(bf16[2,64,896]{2,1,0:T(8,128)(2,1)} %bitcast.60), channel_id=1, source_target_pairs={{0,2},{1,3},{2,0},{3,1},{4,6},{5,7},{6,4},{7,5},{8,10},{9,11},{10,... | collective-permute-start | bytes 688136 | tf_op jit(solution)/shard_map/ppermute | solution.py:217
  3.8 1.1 %collective-permute-start.1 = (bf16[2,64,896]{2,1,0:T(8,128)(2,1)}, bf16[2,64,896]{2,1,0:T(8,128)(2,1)S(1)}, u32[]{:S(2)}, u32[]{:S(2)}) collective-permute-start(bf16[2,64,896]{2,1,0:T(8,128)(2,1)} %bitcast.61), channel_id=1, source_target_pairs={{0,3},{1,0},{2,1},{3,2},{4,7},{5,4},{6,5},{7,6},{8,11},{9,8},{10,9... | collective-permute-start | bytes 688136 | tf_op jit(solution)/shard_map/ppermute | solution.py:217
  4.9 0.9 collective-permute-start
  5.8 0.8 reshape.27
  6.6 4.3 %collective-permute-done.2 = bf16[2,64,896]{2,1,0:T(8,128)(2,1)S(1)} collective-permute-done((bf16[2,64,896]{2,1,0:T(8,128)(2,1)}, bf16[2,64,896]{2,1,0:T(8,128)(2,1)S(1)}, u32[]{:S(2)}, u32[]{:S(2)}) %collective-permute-start.2) | collective-permute-done | bytes 229408 | tf_op jit(solution)/shard_map/ppermute | solution.py:217
  10.9 3.9 %collective-permute-done.1 = bf16[2,64,896]{2,1,0:T(8,128)(2,1)S(1)} collective-permute-done((bf16[2,64,896]{2,1,0:T(8,128)(2,1)}, bf16[2,64,896]{2,1,0:T(8,128)(2,1)S(1)}, u32[]{:S(2)}, u32[]{:S(2)}) %collective-permute-start.1) | collective-permute-done | bytes 229408 | tf_op jit(solution)/shard_map/ppermute | solution.py:217
  14.8 1.1 %pad_maximum_fusion = bf16[2,4,64,896]{3,2,1,0:T(8,128)(2,1)S(1)} fusion(bf16[2,1,64,896]{3,2,1,0:T(8,128)(2,1)S(1)} %bitcast.64, bf16[2,1,64,896]{3,2,1,0:T(8,128)(2,1)S(1)} %bitcast.65, bf16[2,1,64,896]{3,2,1,0:T(8,128)(2,1)S(1)} %bitcast.66, bf16[2,1,64,896]{3,2,1,0:T(8,128)(2,1)} %bitcast.63), kind=kLoop, calls=%fused_computation | loop fusion | flops 1376256 | bytes 1835008 | tf_op jit(solution)/shard_map/stack | solution.py:218
  15.9 14.8 %shard_map.101 = (bf16[128,1024]{1,0:T(8,128)(2,1)}, bf16[128,1024]{1,0:T(8,128)(2,1)}, bf16[512,1024]{1,0:T(8,128)(2,1)S(1)}, bf16[512,1024]{1,0:T(8,128)(2,1)}, bf16[512,896]{1,0:T(8,128)(2,1)S(1)}) custom-call(s32[5]{0:T(128)S(1)} %pad_add_fusion.refs_0_, bf16[512,896]{1,0:T(8,128)(2,1)S(1)} %bitcast.54, bf16[896,1024]{1,0:T(8,128)(2,1)} %refs_2_.1, ...), custom_call_target="tpu_custom_call" | custom-call | tf_op jit(solution)/shard_map/pallas_call | solution.py:100
  30.7 0.9 copy-done
  31.7 0.5 collective-permute-start.6
  32.2 3.4 %collective-permute-done.6.rows_other = bf16[512,896]{1,0:T(8,128)(2,1)} collective-permute-done((bf16[512,896]{1,0:T(8,128)(2,1)S(1)}, bf16[512,896]{1,0:T(8,128)(2,1)}, u32[]{:S(2)}, u32[]{:S(2)}) %collective-permute-start.6) | collective-permute-done | bytes 917536 | tf_op jit(solution)/shard_map/ppermute | solution.py:219
  35.8 4.8 %shard_map.102 = (f32[224,1024]{1,0:T(8,128)S(1)}, bf16[3,224,1024]{2,1,0:T(8,128)(2,1)}) custom-call(s32[2]{0:T(128)S(1)} %pad_add_fusion.1.place, bf16[512,896]{1,0:T(8,128)(2,1)S(1)} %bitcast.56, bf16[512,896]{1,0:T(8,128)(2,1)} %collective-permute-done.6.rows_other, bf16[512,1024]{1,0:T(8,128)(2,1)S(1)} %get-tuple-element.17.grads, ...), custom_call_target="tpu_custom_call" | custom-call | tf_op jit(solution)/shard_map/pallas_call | solution.py:152
  40.7 1.4 %slice_bitcast_fusion = (bf16[224,1024]{1,0:T(8,128)(2,1)S(1)}, bf16[224,1024]{1,0:T(8,128)(2,1)S(1)}, bf16[224,1024]{1,0:T(8,128)(2,1)S(1)}) fusion(bf16[3,224,1024]{2,1,0:T(8,128)(2,1)} %get-tuple-element.20), kind=kLoop, calls=%fused_computation.4 | loop fusion | bytes 2752512 | tf_op jit(solution)/shard_map/squeeze | solution.py:234
  42.1 3.1 %collective-permute-start.10 = (bf16[224,1024]{1,0:T(8,128)(2,1)S(1)}, bf16[224,1024]{1,0:T(8,128)(2,1)S(1)}, u32[]{:S(2)}, u32[]{:S(2)}) collective-permute-start(bf16[224,1024]{1,0:T(8,128)(2,1)S(1)} %get-tuple-element.23), channel_id=1, source_target_pairs={{0,192},{64,0},{128,64},{192,128},{1,193},{65,1},{129,65},{193,129... | collective-permute-start | bytes 1376264 | tf_op jit(solution)/shard_map/ppermute | solution.py:234
  45.2 2.2 %collective-permute-start.8 = (bf16[224,1024]{1,0:T(8,128)(2,1)S(1)}, bf16[224,1024]{1,0:T(8,128)(2,1)S(1)}, u32[]{:S(2)}, u32[]{:S(2)}) collective-permute-start(bf16[224,1024]{1,0:T(8,128)(2,1)S(1)} %get-tuple-element.25), channel_id=1, source_target_pairs={{0,128},{64,192},{128,0},{192,64},{1,129},{65,193},{129,1},{193,65... | collective-permute-start | bytes 1376264 | tf_op jit(solution)/shard_map/ppermute | solution.py:234
  47.4 17.7 %collective-permute-done.10.refs_2_ = bf16[224,1024]{1,0:T(8,128)(2,1)S(1)} collective-permute-done((bf16[224,1024]{1,0:T(8,128)(2,1)S(1)}, bf16[224,1024]{1,0:T(8,128)(2,1)S(1)}, u32[]{:S(2)}, u32[]{:S(2)}) %collective-permute-start.10) | collective-permute-done | bytes 458784 | tf_op jit(solution)/shard_map/ppermute | solution.py:234
  65.1 3.4 %collective-permute-done.9.refs_1_ = bf16[224,1024]{1,0:T(8,128)(2,1)S(1)} collective-permute-done((bf16[224,1024]{1,0:T(8,128)(2,1)S(1)}, bf16[224,1024]{1,0:T(8,128)(2,1)S(1)}, u32[]{:S(2)}, u32[]{:S(2)}) %collective-permute-start.9) | collective-permute-done | bytes 458784 | tf_op jit(solution)/shard_map/ppermute | solution.py:234
  68.5 1.0 %shard_map.103 = (f32[28,1024]{1,0:T(8,128)S(1)}, bf16[7,32,1024]{2,1,0:T(8,128)(2,1)S(1)}) custom-call(s32[2]{0:T(128)S(1)} %pad_add_fusion.1.place, f32[224,1024]{1,0:T(8,128)S(1)} %get-tuple-element.19.mine, bf16[224,1024]{1,0:T(8,128)(2,1)S(1)} %collective-permute-done.8.refs_0_, bf16[224,1024]{1,0:T(8,128)(2,1)S(1)} %collective-permute-done.9.refs_1_, ...), custom_call_target="tpu_custom_call" | custom-call | tf_op jit(solution)/shard_map/pallas_call | solution.py:196
  69.6 4.6 %collective-permute-start.11 = (bf16[32,1024]{1,0:T(8,128)(2,1)S(1)}, bf16[32,1024]{1,0:T(8,128)(2,1)S(1)}, u32[]{:S(2)}, u32[]{:S(2)}) collective-permute-start(bf16[32,1024]{1,0:T(8,128)(2,1)S(1)} %get-tuple-element.29), channel_id=1, source_target_pairs={{0,32},{8,40},{16,48},{24,56},{32,0},{40,8},{48,16},{56,24},{1,33}... | collective-permute-start | bytes 196616 | tf_op jit(solution)/shard_map/ppermute | solution.py:239
  74.1 1.0 %collective-permute-start.17 = (bf16[32,1024]{1,0:T(8,128)(2,1)S(1)}, bf16[32,1024]{1,0:T(8,128)(2,1)S(1)}, u32[]{:S(2)}, u32[]{:S(2)}) collective-permute-start(bf16[32,1024]{1,0:T(8,128)(2,1)S(1)} %get-tuple-element.30), channel_id=1, source_target_pairs={{0,56},{8,0},{16,8},{24,16},{32,24},{40,32},{48,40},{56,48},{1,57}... | collective-permute-start | bytes 196616 | tf_op jit(solution)/shard_map/ppermute | solution.py:239
  75.2 2.2 %collective-permute-start.16 = (bf16[32,1024]{1,0:T(8,128)(2,1)S(1)}, bf16[32,1024]{1,0:T(8,128)(2,1)S(1)}, u32[]{:S(2)}, u32[]{:S(2)}) collective-permute-start(bf16[32,1024]{1,0:T(8,128)(2,1)S(1)} %get-tuple-element.31), channel_id=1, source_target_pairs={{0,8},{8,16},{16,24},{24,32},{32,40},{40,48},{48,56},{56,0},{1,9},... | collective-permute-start | bytes 196616 | tf_op jit(solution)/shard_map/ppermute | solution.py:239
  77.4 0.2 collective-permute-start.15
  77.6 3.9 %collective-permute-start.14 = (bf16[32,1024]{1,0:T(8,128)(2,1)S(1)}, bf16[32,1024]{1,0:T(8,128)(2,1)S(1)}, u32[]{:S(2)}, u32[]{:S(2)}) collective-permute-start(bf16[32,1024]{1,0:T(8,128)(2,1)S(1)} %get-tuple-element.33), channel_id=1, source_target_pairs={{0,16},{8,24},{16,32},{24,40},{32,48},{40,56},{48,0},{56,8},{1,17}... | collective-permute-start | bytes 196616 | tf_op jit(solution)/shard_map/ppermute | solution.py:239
  81.5 5.0 %collective-permute-start.12 = (bf16[32,1024]{1,0:T(8,128)(2,1)S(1)}, bf16[32,1024]{1,0:T(8,128)(2,1)S(1)}, u32[]{:S(2)}, u32[]{:S(2)}) collective-permute-start(bf16[32,1024]{1,0:T(8,128)(2,1)S(1)} %get-tuple-element.35), channel_id=1, source_target_pairs={{0,24},{8,32},{16,40},{24,48},{32,56},{40,0},{48,8},{56,16},{1,25}... | collective-permute-start | bytes 196616 | tf_op jit(solution)/shard_map/ppermute | solution.py:239
  86.6 2.6 %collective-permute-start.3 = (bf16[2,64,896]{2,1,0:T(8,128)(2,1)S(1)}, bf16[2,64,896]{2,1,0:T(8,128)(2,1)S(1)}, u32[]{:S(2)}, u32[]{:S(2)}) collective-permute-start(bf16[2,64,896]{2,1,0:T(8,128)(2,1)S(1)} %get-tuple-element.26), channel_id=1, source_target_pairs={{0,3},{1,0},{2,1},{3,2},{4,7},{5,4},{6,5},{7,6},{8,11},{9,8},{10,9... | collective-permute-start | bytes 688136 | tf_op jit(solution)/shard_map/ppermute | solution.py:227
  89.3 0.9 collective-permute-start.5
  90.2 0.8 collective-permute-start.4
  91.2 4.1 %collective-permute-done.3 = bf16[2,64,896]{2,1,0:T(8,128)(2,1)S(1)} collective-permute-done((bf16[2,64,896]{2,1,0:T(8,128)(2,1)S(1)}, bf16[2,64,896]{2,1,0:T(8,128)(2,1)S(1)}, u32[]{:S(2)}, u32[]{:S(2)}) %collective-permute-start.3) | collective-permute-done | bytes 229408 | tf_op jit(solution)/shard_map/ppermute | solution.py:227
  95.3 1.6 %collective-permute-done.5 = bf16[2,64,896]{2,1,0:T(8,128)(2,1)S(1)} collective-permute-done((bf16[2,64,896]{2,1,0:T(8,128)(2,1)S(1)}, bf16[2,64,896]{2,1,0:T(8,128)(2,1)S(1)}, u32[]{:S(2)}, u32[]{:S(2)}) %collective-permute-start.5) | collective-permute-done | bytes 229408 | tf_op jit(solution)/shard_map/ppermute | solution.py:227
  96.9 2.4 %collective-permute-done.4 = bf16[2,64,896]{2,1,0:T(8,128)(2,1)S(1)} collective-permute-done((bf16[2,64,896]{2,1,0:T(8,128)(2,1)S(1)}, bf16[2,64,896]{2,1,0:T(8,128)(2,1)S(1)}, u32[]{:S(2)}, u32[]{:S(2)}) %collective-permute-start.4) | collective-permute-done | bytes 229408 | tf_op jit(solution)/shard_map/ppermute | solution.py:227
  99.3 0.9 fusion.1
  100.1 0.7 broadcast_select_fusion
  (28 shorter events, 0.7 us)
Async XLA Ops:
  0.6 15.3 %copy-start.3 = (bf16[128,1024]{1,0:T(8,128)(2,1)S(1)}, bf16[128,1024]{1,0:T(8,128)(2,1)}, u32[]{:S(2)}) copy-start(bf16[128,1024]{1,0:T(8,128)(2,1)} %refs_5_.1) | copy-start | bytes 786436
  0.6 15.3 %copy-start.2 = (bf16[128,1024]{1,0:T(8,128)(2,1)S(1)}, bf16[128,1024]{1,0:T(8,128)(2,1)}, u32[]{:S(2)}) copy-start(bf16[128,1024]{1,0:T(8,128)(2,1)} %refs_4_.1) | copy-start | bytes 786436
  0.7 10.3 %collective-permute-start.2 = (bf16[2,64,896]{2,1,0:T(8,128)(2,1)}, bf16[2,64,896]{2,1,0:T(8,128)(2,1)S(1)}, u32[]{:S(2)}, u32[]{:S(2)}) collective-permute-start(bf16[2,64,896]{2,1,0:T(8,128)(2,1)} %bitcast.60), channel_id=1, source_target_pairs={{0,2},{1,3},{2,0},{3,1},{4,6},{5,7},{6,4},{7,5},{8,10},{9,11},{10,... | collective-permute-start | bytes 688136 | tf_op jit(solution)/shard_map/ppermute | solution.py:217
  3.8 11.1 %collective-permute-start.1 = (bf16[2,64,896]{2,1,0:T(8,128)(2,1)}, bf16[2,64,896]{2,1,0:T(8,128)(2,1)S(1)}, u32[]{:S(2)}, u32[]{:S(2)}) collective-permute-start(bf16[2,64,896]{2,1,0:T(8,128)(2,1)} %bitcast.61), channel_id=1, source_target_pairs={{0,3},{1,0},{2,1},{3,2},{4,7},{5,4},{6,5},{7,6},{8,11},{9,8},{10,9... | collective-permute-start | bytes 688136 | tf_op jit(solution)/shard_map/ppermute | solution.py:217
  4.9 9.9 %collective-permute-start = (bf16[2,64,896]{2,1,0:T(8,128)(2,1)}, bf16[2,64,896]{2,1,0:T(8,128)(2,1)S(1)}, u32[]{:S(2)}, u32[]{:S(2)}) collective-permute-start(bf16[2,64,896]{2,1,0:T(8,128)(2,1)} %bitcast.62), channel_id=1, source_target_pairs={{0,1},{1,2},{2,3},{3,0},{4,5},{5,6},{6,7},{7,4},{8,9},{9,10},{10,1... | collective-permute-start | bytes 688136 | tf_op jit(solution)/shard_map/ppermute | solution.py:217
  30.7 0.9 copy-start
  31.7 4.2 %collective-permute-start.7 = (bf16[512,1024]{1,0:T(8,128)(2,1)}, bf16[512,1024]{1,0:T(8,128)(2,1)S(1)}, u32[]{:S(2)}, u32[]{:S(2)}) collective-permute-start(bf16[512,1024]{1,0:T(8,128)(2,1)} %get-tuple-element.18), channel_id=1, source_target_pairs={{0,4},{4,0},{1,5},{5,1},{2,6},{6,2},{3,7},{7,3},{8,12},{12,8},{9,1... | collective-permute-start | bytes 3145736 | tf_op jit(solution)/shard_map/ppermute | solution.py:224
  31.7 3.9 %collective-permute-start.6 = (bf16[512,896]{1,0:T(8,128)(2,1)S(1)}, bf16[512,896]{1,0:T(8,128)(2,1)}, u32[]{:S(2)}, u32[]{:S(2)}) collective-permute-start(bf16[512,896]{1,0:T(8,128)(2,1)S(1)} %bitcast.55), channel_id=1, source_target_pairs={{0,4},{4,0},{1,5},{5,1},{2,6},{6,2},{3,7},{7,3},{8,12},{12,8},{9,1... | collective-permute-start | bytes 2752520 | tf_op jit(solution)/shard_map/ppermute | solution.py:219
  42.1 44.5 %copy-start.1 = (bf16[512,896]{1,0:T(8,128)(2,1)S(1)}, bf16[512,896]{1,0:T(8,128)(2,1)}, u32[]{:S(2)}) copy-start(bf16[512,896]{1,0:T(8,128)(2,1)} %copy-done) | copy-start | bytes 2752516
  42.1 23.0 %collective-permute-start.10 = (bf16[224,1024]{1,0:T(8,128)(2,1)S(1)}, bf16[224,1024]{1,0:T(8,128)(2,1)S(1)}, u32[]{:S(2)}, u32[]{:S(2)}) collective-permute-start(bf16[224,1024]{1,0:T(8,128)(2,1)S(1)} %get-tuple-element.23), channel_id=1, source_target_pairs={{0,192},{64,0},{128,64},{192,128},{1,193},{65,1},{129,65},{193,129... | collective-permute-start | bytes 1376264 | tf_op jit(solution)/shard_map/ppermute | solution.py:234
  45.2 23.3 %collective-permute-start.9 = (bf16[224,1024]{1,0:T(8,128)(2,1)S(1)}, bf16[224,1024]{1,0:T(8,128)(2,1)S(1)}, u32[]{:S(2)}, u32[]{:S(2)}) collective-permute-start(bf16[224,1024]{1,0:T(8,128)(2,1)S(1)} %get-tuple-element.24), channel_id=1, source_target_pairs={{0,64},{64,128},{128,192},{192,0},{1,65},{65,129},{129,193},{193,1... | collective-permute-start | bytes 1376264 | tf_op jit(solution)/shard_map/ppermute | solution.py:234
  45.2 23.3 %collective-permute-start.8 = (bf16[224,1024]{1,0:T(8,128)(2,1)S(1)}, bf16[224,1024]{1,0:T(8,128)(2,1)S(1)}, u32[]{:S(2)}, u32[]{:S(2)}) collective-permute-start(bf16[224,1024]{1,0:T(8,128)(2,1)S(1)} %get-tuple-element.25), channel_id=1, source_target_pairs={{0,128},{64,192},{128,0},{192,64},{1,129},{65,193},{129,1},{193,65... | collective-permute-start | bytes 1376264 | tf_op jit(solution)/shard_map/ppermute | solution.py:234
  69.6 12.0 %collective-permute-start.11 = (bf16[32,1024]{1,0:T(8,128)(2,1)S(1)}, bf16[32,1024]{1,0:T(8,128)(2,1)S(1)}, u32[]{:S(2)}, u32[]{:S(2)}) collective-permute-start(bf16[32,1024]{1,0:T(8,128)(2,1)S(1)} %get-tuple-element.29), channel_id=1, source_target_pairs={{0,32},{8,40},{16,48},{24,56},{32,0},{40,8},{48,16},{56,24},{1,33}... | collective-permute-start | bytes 196616 | tf_op jit(solution)/shard_map/ppermute | solution.py:239
  74.1 7.4 %collective-permute-start.17 = (bf16[32,1024]{1,0:T(8,128)(2,1)S(1)}, bf16[32,1024]{1,0:T(8,128)(2,1)S(1)}, u32[]{:S(2)}, u32[]{:S(2)}) collective-permute-start(bf16[32,1024]{1,0:T(8,128)(2,1)S(1)} %get-tuple-element.30), channel_id=1, source_target_pairs={{0,56},{8,0},{16,8},{24,16},{32,24},{40,32},{48,40},{56,48},{1,57}... | collective-permute-start | bytes 196616 | tf_op jit(solution)/shard_map/ppermute | solution.py:239
  75.2 11.5 %collective-permute-start.16 = (bf16[32,1024]{1,0:T(8,128)(2,1)S(1)}, bf16[32,1024]{1,0:T(8,128)(2,1)S(1)}, u32[]{:S(2)}, u32[]{:S(2)}) collective-permute-start(bf16[32,1024]{1,0:T(8,128)(2,1)S(1)} %get-tuple-element.31), channel_id=1, source_target_pairs={{0,8},{8,16},{16,24},{24,32},{32,40},{40,48},{48,56},{56,0},{1,9},... | collective-permute-start | bytes 196616 | tf_op jit(solution)/shard_map/ppermute | solution.py:239
  77.4 11.9 %collective-permute-start.15 = (bf16[32,1024]{1,0:T(8,128)(2,1)S(1)}, bf16[32,1024]{1,0:T(8,128)(2,1)S(1)}, u32[]{:S(2)}, u32[]{:S(2)}) collective-permute-start(bf16[32,1024]{1,0:T(8,128)(2,1)S(1)} %get-tuple-element.32), channel_id=1, source_target_pairs={{0,48},{8,56},{16,0},{24,8},{32,16},{40,24},{48,32},{56,40},{1,49}... | collective-permute-start | bytes 196616 | tf_op jit(solution)/shard_map/ppermute | solution.py:239
  77.6 12.6 %collective-permute-start.14 = (bf16[32,1024]{1,0:T(8,128)(2,1)S(1)}, bf16[32,1024]{1,0:T(8,128)(2,1)S(1)}, u32[]{:S(2)}, u32[]{:S(2)}) collective-permute-start(bf16[32,1024]{1,0:T(8,128)(2,1)S(1)} %get-tuple-element.33), channel_id=1, source_target_pairs={{0,16},{8,24},{16,32},{24,40},{32,48},{40,56},{48,0},{56,8},{1,17}... | collective-permute-start | bytes 196616 | tf_op jit(solution)/shard_map/ppermute | solution.py:239
  81.5 9.5 %collective-permute-start.13 = (bf16[32,1024]{1,0:T(8,128)(2,1)S(1)}, bf16[32,1024]{1,0:T(8,128)(2,1)S(1)}, u32[]{:S(2)}, u32[]{:S(2)}) collective-permute-start(bf16[32,1024]{1,0:T(8,128)(2,1)S(1)} %get-tuple-element.34), channel_id=1, source_target_pairs={{0,40},{8,48},{16,56},{24,0},{32,8},{40,16},{48,24},{56,32},{1,41}... | collective-permute-start | bytes 196616 | tf_op jit(solution)/shard_map/ppermute | solution.py:239
  81.5 9.5 %collective-permute-start.12 = (bf16[32,1024]{1,0:T(8,128)(2,1)S(1)}, bf16[32,1024]{1,0:T(8,128)(2,1)S(1)}, u32[]{:S(2)}, u32[]{:S(2)}) collective-permute-start(bf16[32,1024]{1,0:T(8,128)(2,1)S(1)} %get-tuple-element.35), channel_id=1, source_target_pairs={{0,24},{8,32},{16,40},{24,48},{32,56},{40,0},{48,8},{56,16},{1,25}... | collective-permute-start | bytes 196616 | tf_op jit(solution)/shard_map/ppermute | solution.py:239
  86.6 8.7 %collective-permute-start.3 = (bf16[2,64,896]{2,1,0:T(8,128)(2,1)S(1)}, bf16[2,64,896]{2,1,0:T(8,128)(2,1)S(1)}, u32[]{:S(2)}, u32[]{:S(2)}) collective-permute-start(bf16[2,64,896]{2,1,0:T(8,128)(2,1)S(1)} %get-tuple-element.26), channel_id=1, source_target_pairs={{0,3},{1,0},{2,1},{3,2},{4,7},{5,4},{6,5},{7,6},{8,11},{9,8},{10,9... | collective-permute-start | bytes 688136 | tf_op jit(solution)/shard_map/ppermute | solution.py:227
  89.3 7.6 %collective-permute-start.5 = (bf16[2,64,896]{2,1,0:T(8,128)(2,1)S(1)}, bf16[2,64,896]{2,1,0:T(8,128)(2,1)S(1)}, u32[]{:S(2)}, u32[]{:S(2)}) collective-permute-start(bf16[2,64,896]{2,1,0:T(8,128)(2,1)S(1)} %get-tuple-element.27), channel_id=1, source_target_pairs={{0,2},{1,3},{2,0},{3,1},{4,6},{5,7},{6,4},{7,5},{8,10},{9,11},{10,... | collective-permute-start | bytes 688136 | tf_op jit(solution)/shard_map/ppermute | solution.py:227
  90.2 9.0 %collective-permute-start.4 = (bf16[2,64,896]{2,1,0:T(8,128)(2,1)S(1)}, bf16[2,64,896]{2,1,0:T(8,128)(2,1)S(1)}, u32[]{:S(2)}, u32[]{:S(2)}) collective-permute-start(bf16[2,64,896]{2,1,0:T(8,128)(2,1)S(1)} %get-tuple-element.28), channel_id=1, source_target_pairs={{0,1},{1,2},{2,3},{3,0},{4,5},{5,6},{6,7},{7,4},{8,9},{9,10},{10,1... | collective-permute-start | bytes 688136 | tf_op jit(solution)/shard_map/ppermute | solution.py:227
  91.1 9.1 %collective-permute-start.18 = (f32[14,1024]{1,0:T(8,128)S(1)}, f32[14,1024]{1,0:T(8,128)S(1)}, u32[]{:S(2)}, u32[]{:S(2)}) collective-permute-start(f32[14,1024]{1,0:T(8,128)S(1)} %slice_select_fusion), channel_id=1, source_target_pairs={{0,4},{4,0},{1,5},{5,1},{2,6},{6,2},{3,7},{7,3},{8,12},{12,8},{9,1... | collective-permute-start | bytes 172040 | tf_op jit(solution)/shard_map/ppermute | solution.py:243

commit v2 on v0

v2 whole, which is shorter than its diff:
```python
import jax
import jax.numpy as jnp
from jax import lax
from jax.experimental import pallas as pl
from jax.experimental.pallas import tpu as pltpu
from jax.sharding import Mesh, PartitionSpec as P

HEAD = 128
PAD = 32
BLOCK = 256
BF = jnp.bfloat16
F32 = jnp.float32
NN = (((1,), (0,)), ((), ()))
NT = (((1,), (1,)), ((), ()))
TN = (((0,), (0,)), ((), ()))
SMEM = pl.BlockSpec(memory_space=pltpu.SMEM)
VMEM = pl.BlockSpec(memory_space=pltpu.VMEM)
HBM = pl.BlockSpec(memory_space=pltpu.HBM)


def params(**more):
    return pltpu.CompilerParams(vmem_limit_bytes=32 * 1024 * 1024, **more)


def shape(dims, dtype):
    return pltpu.VMEM(dims, dtype)


def near_by(*arrays):
    return [pltpu.with_memory_space_constraint(a, pltpu.VMEM) for a in arrays]


def dot(a, b, dims=NN):
    return lax.dot_general(a, b, dims, preferred_element_type=F32)


def cost(flops, moved):
    return pl.CostEstimate(flops=flops, bytes_accessed=moved, transcendentals=0)


def hop(value, axis, size, step):
    inner = axis == "x"
    number = lambda i, core: core * size + i if inner else i * 2 + core
    pairs = []
    for core in range(2):
        for i in range(size):
            target = (i + (step if core == 0 else -step)) % size
            pairs.append((number(i, core), number(target, core)))
    return lax.ppermute(value, ("c", axis) if inner else (axis, "c"), pairs)


def swap(value):
    return lax.ppermute(value, "c", [(0, 1), (1, 0)])


def attention(q, g, k, v, live, empty):
    scale = HEAD ** (-0.5)
    tokens = q.shape[0]
    raw = jnp.exp(dot(q, k, NT) * scale) * live
    prob_grad = dot(g, v, NT)
    total = jnp.sum(raw, axis=-1, keepdims=True) + empty
    probs = raw * (1.0 / total)
    delta = jnp.sum(probs * prob_grad, axis=-1, keepdims=True)
    low = probs.astype(BF)
    score_grad = (probs * (prob_grad - delta) * scale).astype(BF)
    across = dot(jnp.concatenate([low, score_grad], axis=0), jnp.concatenate([v, k], axis=1))
    none = jnp.zeros_like(q)
    tall = jnp.concatenate(
        [jnp.concatenate([q, none], axis=1), jnp.concatenate([none, g], axis=1)], axis=0
    )
    down = dot(jnp.concatenate([score_grad, low], axis=0), tall, TN)
    return (
        across[:tokens, :HEAD].astype(BF),
        across[tokens:, HEAD:].astype(BF),
        down[:, :HEAD].astype(BF),
        down[:, HEAD:].astype(BF),
    )


def gathered(slabs, rows, offset):
    stretches, neigh, group, _ = slabs[0].shape
    first = offset
    for c in range(stretches):
        for s in slabs:
            for n in range(neigh):
                rows[first : first + group] = s[c, n]
                first += group


def load_body(*refs):
    count = (len(refs) - 1) // 2
    copies = [
        pltpu.make_async_copy(refs[i], refs[count + i], refs[-1].at[i]) for i in range(count)
    ]
    for copy in copies:
        copy.start()
    for copy in copies:
        copy.wait()


def load(*arrays):
    return pl.pallas_call(
        load_body,
        in_specs=[HBM] * len(arrays),
        out_specs=[VMEM] * len(arrays),
        out_shape=[shape(a.shape, a.dtype) for a in arrays],
        scratch_shapes=[pltpu.SemaphoreType.DMA((len(arrays),))],
        compiler_params=params(),
    )(*[pltpu.with_memory_space_constraint(a, pltpu.HBM) for a in arrays])


def attend_body(flags, s0, s1, s2, s3, key_w, value_w, queries, cotangent,
                attended, query_grad, keep, send, rows):
    stretches, neigh_count, group, _ = s0.shape
    span = 4 * neigh_count * group
    tokens = queries.shape[0] // stretches
    gathered((s0, s1, s2, s3), rows, 0)
    first = flags[0] == 0
    neigh = (lax.broadcasted_iota(jnp.int32, (1, span), 1) // group) % 2
    for start in range(0, queries.shape[1], BLOCK):
        here = slice(start, start + BLOCK)
        keys = dot(rows[...], key_w[:, here]).astype(BF)
        values = dot(rows[...], value_w[:, here]).astype(BF)
        for c in range(stretches):
            one, two = flags[1 + 2 * c], flags[2 + 2 * c]
            live = jnp.where(neigh == 0, one, two).astype(F32)
            empty = jnp.where(one + two == 0, 1.0, 0.0).astype(F32)
            r = slice(c * span, (c + 1) * span)
            t = slice(c * tokens, (c + 1) * tokens)
            for h in range(0, BLOCK, HEAD):
                w = slice(start + h, start + h + HEAD)
                out, q_grad, k_grad, v_grad = attention(
                    queries[t, w], cotangent[t, w],
                    keys[r, h : h + HEAD], values[r, h : h + HEAD], live, empty,
                )
                attended[t, w] = out
                query_grad[t, w] = q_grad
                keep[r, w] = jnp.where(first, k_grad, v_grad)
                send[r, w] = jnp.where(first, v_grad, k_grad)


def attend(flags, slabs, key_w, value_w, queries, cotangent):
    enc = slabs[0].shape[-1]
    row_count = 4 * slabs[0].size // enc
    tokens, width = queries.shape
    return pl.pallas_call(
        attend_body,
        in_specs=[SMEM] + [VMEM] * 8,
        out_specs=[VMEM] * 4,
        out_shape=[jax.ShapeDtypeStruct((tokens, width), BF)] * 2
        + [shape((row_count, width), BF)] * 2,
        scratch_shapes=[pltpu.VMEM((row_count, enc), BF)],
        compiler_params=params(),
        cost_estimate=cost(4 * 10**9, 5 * 10**6),
    )(flags, *near_by(*slabs, key_w, value_w, queries, cotangent))


def passage_body(flags, keep, send, key_hbm, value_hbm, o0, o1, o2, o3, key_w, value_w, sems):
    first = flags[0] == 0
    width = keep.shape[1]
    loads = []
    for i, start in enumerate(range(0, width, BLOCK)):
        here = pl.ds(start, BLOCK)
        for k, (source, target) in enumerate(((key_hbm, key_w), (value_hbm, value_w))):
            copy = pltpu.make_async_copy(source.at[:, here], target.at[i], sems.at[2 * i + k])
            copy.start()
            loads.append(copy)
    total = 0.0
    for i, start in enumerate(range(0, width, BLOCK)):
        a, b = keep[:, start : start + BLOCK], send[:, start : start + BLOCK]
        loads[2 * i].wait()
        loads[2 * i + 1].wait()
        total = total + dot(jnp.where(first, a, b), key_w[i], NT)
        total = total + dot(jnp.where(first, b, a), value_w[i], NT)
    stretches, neigh, group, _ = o0.shape
    start = 0
    for c in range(stretches):
        for o in (o0, o1, o2, o3):
            for n in range(neigh):
                o[c, n] = total[start : start + group].astype(o.dtype)
                start += group


def passage_grad(flags, keep, send, key_w, value_w, slab):
    enc, width = key_w.shape
    parts = width // BLOCK
    far = [pltpu.with_memory_space_constraint(a, pltpu.HBM) for a in (key_w, value_w)]
    return pl.pallas_call(
        passage_body,
        in_specs=[SMEM] + [VMEM] * 2 + [HBM] * 2,
        out_specs=[VMEM] * 4,
        out_shape=[shape(slab, d) for d in (F32, BF, F32, BF)],
        scratch_shapes=[
            pltpu.VMEM((parts, enc, BLOCK), BF),
            pltpu.VMEM((parts, enc, BLOCK), BF),
            pltpu.SemaphoreType.DMA((2 * parts,)),
        ],
        compiler_params=params(),
        cost_estimate=cost(4 * 10**9, 10**7),
    )(flags, *near_by(keep, send), *far)


def weight_body(a0, a1, a2, a3, grads, out, rows):
    gathered((a0, a1, a2, a3), rows, 0)
    out[...] = dot(rows[...], grads[...], TN)


def weight_grad(slabs, grads):
    enc = slabs[0].shape[-1]
    row_count, width = grads.shape
    return pl.pallas_call(
        weight_body,
        in_specs=[VMEM] * 5,
        out_specs=VMEM,
        out_shape=shape((enc, width), F32),
        scratch_shapes=[pltpu.VMEM((row_count, enc), BF)],
        compiler_params=params(),
        cost_estimate=cost(2 * 10**9, 5 * 10**6),
    )(*near_by(*slabs, grads))


def split_body(place, a0, a1, a2, a3, grads, partial, mine, far, back, front, rows, total):
    height = mine.shape[0]
    gathered((a0, a1, a2, a3), rows, 0)
    total[...] = partial[...] + dot(rows[...], grads[...], TN)
    for i, out in enumerate((mine, far, back, front)):
        first = pl.multiple_of(place[i] * height, 8)
        out[...] = total[pl.ds(first, height), :].astype(out.dtype)


def weight_split(place, slabs, grads, partial, parts):
    enc, width = partial.shape
    row_count = grads.shape[0]
    height = enc // parts
    return pl.pallas_call(
        split_body,
        in_specs=[SMEM] + [VMEM] * 6,
        out_specs=[VMEM] * 4,
        out_shape=[
            shape((height, width), F32),
            shape((height, width), BF),
            shape((height, width), BF),
            shape((height, width), F32),
        ],
        scratch_shapes=[pltpu.VMEM((row_count, enc), BF), pltpu.VMEM((enc, width), F32)],
        compiler_params=params(),
        cost_estimate=cost(2 * 10**9, 5 * 10**6),
    )(place, *near_by(*slabs, grads, partial))


def add_body(*refs):
    count = len(refs) // 3
    for i in range(count):
        total = refs[2 * i][...] + refs[2 * i + 1][...].astype(F32)
        refs[2 * count + i][...] = total.astype(BF)


def add(*pairs):
    return pl.pallas_call(
        add_body,
        in_specs=[VMEM] * (2 * len(pairs)),
        out_specs=[VMEM] * len(pairs),
        out_shape=[shape(a.shape, BF) for a, _ in pairs],
        compiler_params=params(),
    )(*near_by(*(a for pair in pairs for a in pair)))


def fold_body(place, mine, back, front, own, one, two, three, cross):
    height = own.shape[0]
    z, core = place[4], place[5]
    total = mine[...] + back[...].astype(F32) + front[...].astype(F32)
    pad = jnp.zeros((PAD - height, total.shape[1]), F32)
    for j in range(8):
        piece = total[j * height : (j + 1) * height]
        full = jnp.concatenate([piece, pad], axis=0)
        slot = lax.rem(jnp.where(core == 0, j - z, z - j) + 8, 8)

        @pl.when(slot == 0)
        def _():
            own[...] = piece

        @pl.when(slot == 1)
        def _():
            one[...] = full

        @pl.when(slot == 2)
        def _():
            two[...] = full

        @pl.when(slot == 3)
        def _():
            three[0] = full.astype(BF)

        @pl.when(slot == 4)
        def _():
            three[1] = full.astype(BF)

        for at, name in enumerate((7, 6, 5)):
            @pl.when(slot == name)
            def _():
                cross[at] = full.astype(BF)


def fold(place, mine, back, front):
    height, width = mine.shape[0] // 8, mine.shape[1]
    return pl.pallas_call(
        fold_body,
        in_specs=[SMEM] + [VMEM] * 3,
        out_specs=[VMEM] * 5,
        out_shape=[
            shape((height, width), F32),
            shape((PAD, width), F32),
            shape((PAD, width), F32),
            shape((2, PAD, width), BF),
            shape((3, PAD, width), BF),
        ],
        compiler_params=params(),
    )(place, *near_by(mine, back, front))


def pack_body(three, cross, out):
    out[:2] = three[...]
    out[2] = cross[2]


def pack(three, cross):
    return pl.pallas_call(
        pack_body,
        in_specs=[VMEM] * 2,
        out_specs=VMEM,
        out_shape=shape((3,) + three.shape[1:], BF),
        compiler_params=params(),
    )(*near_by(three, cross))


def relay_body(one, two, cross, arrived, to_one, to_two):
    to_one[0] = (one[...] + arrived[0].astype(F32)).astype(BF)
    to_one[1] = (cross[0].astype(F32) + arrived[2].astype(F32)).astype(BF)
    to_two[0] = (two[...] + arrived[1].astype(F32)).astype(BF)
    to_two[1] = cross[1]


def relay(one, two, cross, arrived):
    return pl.pallas_call(
        relay_body,
        in_specs=[VMEM] * 4,
        out_specs=[VMEM] * 2,
        out_shape=[shape((2,) + one.shape, BF)] * 2,
        compiler_params=params(),
    )(*near_by(one, two, cross, arrived))


def finish_body(place, own, one, two, stay, give):
    first = place[5] == 0
    height = own.shape[0]
    half = height // 2
    for k in range(2):
        value = (one[k].astype(F32) + two[k].astype(F32))[:height]
        if k == 0:
            value = value + own[...]
        low, high = value[:half], value[half:]
        stay[k] = jnp.where(first, low, high)
        give[k] = jnp.where(first, high, low)


def finish(place, own, one, two):
    height, width = own.shape
    dims = (2, height // 2, width)
    return pl.pallas_call(
        finish_body,
        in_specs=[SMEM] + [VMEM] * 3,
        out_specs=[VMEM] * 2,
        out_shape=[shape(dims, F32)] * 2,
        compiler_params=params(),
    )(place, *near_by(own, one, two))


def shards(queries, cotangent, neighbours, present, key_weight, value_weight):
    ny, nz, nx = 4, 8, 4
    y, z, core = lax.axis_index("y"), lax.axis_index("z"), lax.axis_index("c")
    first = core == 0
    sign = 1 - 2 * core
    place = jnp.stack([y, (y + 2) % ny, (y - sign) % ny, (y + sign) % ny, z, core])
    flags = jnp.concatenate([core[None], present.reshape(-1)]).astype(jnp.int32)
    tie = lax.optimization_barrier

    own = neighbours
    opposite = hop(own, "x", nx, 2)
    slabs = [own, hop(own, "x", nx, 1), hop(own, "x", nx, -1), opposite]
    others = [swap(s) for s in slabs]
    flags, place, start = tie((flags, place, own))
    loaded = load(key_weight, value_weight, queries, cotangent, start)
    slabs, loaded, others[0], others[3] = tie((slabs, loaded, others[0], others[3]))
    *loaded, slabs[0] = loaded

    attended, query_grad, keep, send = attend(flags, slabs, *loaded)
    received = swap(send)
    partial = weight_grad(slabs, keep)
    received, partial = tie((received, partial))
    mine, far, back, front = weight_split(place, others, received, partial, ny)
    far_in = hop(far, "y", ny, 1)
    keep, send, front = tie((keep, send, front))
    p0, p1, p2, p3 = passage_grad(flags, keep, send, key_weight, value_weight, own.shape)
    back_in = hop(back, "y", ny, -1)
    far_in, back_in, p1, p2, p3 = tie((far_in, back_in, p1, p2, p3))
    (front,) = add((front, far_in))
    front_in = hop(front, "y", ny, 1)
    front_in, beyond = tie((front_in, hop(p3, "x", nx, 1)))

    here, one, two, three, cross = fold(place, mine, back_in, front_in)
    cross = swap(cross)
    (share,) = add((p2, beyond))
    arrived = hop(pack(three, cross), "z", nz, 2)
    returned = [hop(p1, "x", nx, -1), hop(share, "x", nx, 1)]
    arrived, returned = tie((arrived, returned))
    one, two = relay(one, two, cross, arrived)
    stay, give = finish(place, here, hop(one, "z", nz, 1), hop(two, "z", nz, 2))
    other = swap(give)
    neighbour_grad = p0
    for r in returned:
        neighbour_grad = neighbour_grad + r.astype(F32)
    main, rest = stay[0] + other[1], stay[1] + other[0]
    return (
        attended,
        query_grad,
        neighbour_grad,
        jnp.where(first, main, rest),
        jnp.where(first, rest, main),
    )


def solution(mesh):
    mesh = Mesh(mesh.devices.reshape(4, 8, 2, 4), ("y", "z", "c", "x"))
    dp = ("y", "z", "c")
    placed = (
        P(dp, "x"),
        P(dp, "x"),
        P(dp, None, "x", None),
        P(dp, None),
        P(None, "x"),
        P(None, "x"),
    )
    return jax.shard_map(
        shards,
        mesh=mesh,
        in_specs=placed,
        out_specs=(
            P(dp, "x"),
            P(dp, "x"),
            P(dp, None, "x", None),
            P(dp, "x"),
            P(dp, "x"),
        ),
        check_vma=False,
    )
```

time: 276 us -> 81.7 us (0.30)
  waiting for transfers between devices: 192 us -> 24.8 us
  matrix products: 36.3 us -> 0 us
  starting transfers between devices: 0.26 us -> 32.8 us
  Pallas kernels: 0 us -> 20.9 us
  between operations: 16.4 us -> 0.74 us
  blocking collectives: 13.8 us -> 0 us
  local copies, waits for them, and re-layouts: 13.7 us -> 0.84 us
    unnamed x3 -> x0, waiting for transfers between devices: 183 us -> none
    dot_general x11 -> x0, matrix products: 36.3 us -> none  [the longest x1 9.38 us: shards(): jnp.einsum('chtr,cthd->crhd', score_grad, query_heads, preferred_element_...]
    ppermute x0 -> x19, starting transfers between devices: none -> 32.8 us  [the longest x12 23.9 us: hop(): return lax.ppermute(value, ('c', axis) if inner else (axis, 'c'), pairs)]
    ppermute x0 -> x19, waiting for transfers between devices: none -> 24.8 us  [the longest x12 23 us: hop(): return lax.ppermute(value, ('c', axis) if inner else (axis, 'c'), pairs)]
    pallas_call x0 -> x11, Pallas kernels: none -> 20.9 us  [the longest x1 9.02 us: attend(): pl.pallas_call(attend_body, in_specs=[SMEM] + [VMEM] * 8, out_specs=[VMEM...]
    all_gather x1 -> x0, blocking collectives: 13.8 us -> none  [shards(): gathered = lax.all_gather(neighbours, 'mp', axis=2, tiled=True)]
    reduce_scatter x1 -> x0, waiting for transfers between devices: 9.27 us -> none  [shards(): lax.psum_scatter(passage_grad.astype(jnp.bfloat16), 'mp', scatter_dimensi...]
    unnamed x39 -> x0, local copies, waits for them, and re-layouts: 8.01 us -> none
  transfers between devices with their start and end apart: 2 -> 19, of which waited for: 2 -> 11; matrix products, arithmetic and copies ran while one was open for 7% -> 2% of each run, Pallas kernels for 0% -> 10%
where the time goes in v2:
time: 81.7 us; the launch traced here: 81.6 us
  starting transfers between devices  32.8 us (40%)
  waiting for transfers between devices  24.8 us (30%)
  Pallas kernels  20.9 us (26%)
  other arithmetic  1.6 us (2%)
  local copies, waits for them, and re-layouts  0.84 us (1%)
    ppermute x12, starting transfers between devices, hop(): return lax.ppermute(value, ('c', axis) if inner else (axis, 'c'), pairs)  23.9 us
    ppermute x12, waiting for transfers between devices, hop(): return lax.ppermute(value, ('c', axis) if inner else (axis, 'c'), pairs)  23 us
    pallas_call x1, Pallas kernels, attend(): pl.pallas_call(attend_body, in_specs=[SMEM] + [VMEM] * 8, out_specs=[VMEM...  9.02 us
    ppermute x7, starting transfers between devices, swap(): return lax.ppermute(value, 'c', [(0, 1), (1, 0)])  8.93 us
    pallas_call x1, Pallas kernels, passage_grad(): pl.pallas_call(passage_body, in_specs=[SMEM] + [VMEM] * 2 + [HBM] * 2, ou...  4.62 us
    pallas_call x1, Pallas kernels, load(): pl.pallas_call(load_body, in_specs=[HBM] * len(arrays), out_specs=[VMEM]...  2.24 us
    pallas_call x1, Pallas kernels, weight_split(): pl.pallas_call(split_body, in_specs=[SMEM] + [VMEM] * 6, out_specs=[VMEM]...  1.91 us
    ppermute x7, waiting for transfers between devices, swap(): return lax.ppermute(value, 'c', [(0, 1), (1, 0)])  1.79 us
  transfers between devices with their start and end apart: 19, of which 11 were waited for; matrix products, arithmetic and copies ran while one was open for 2% of the time, Pallas kernels for 10%

profile of v2, /device:TPU:1, one launch (start us, length us, event | category | flops | bytes accessed | tf_op | source)
XLA Modules:
  0.0 81.6 jit_solution(10557639805100991288)
XLA Ops:
  0.6 3.7 %collective-permute-start.2 = (bf16[2,2,32,896]{3,2,1,0:T(8,128)(2,1)}, bf16[2,2,32,896]{3,2,1,0:T(8,128)(2,1)S(1)}, u32[]{:S(2)}, u32[]{:S(2)}) collective-permute-start(bf16[2,2,32,896]{3,2,1,0:T(8,128)(2,1)} %refs_4_), channel_id=1, source_target_pairs={{0,2},{1,3},{2,0},{3,1},{4,6},{5,7},{6,4},{7,5},{8,10},{9,11},{10,... | collective-permute-start | bytes 688136 | tf_op jit(solution)/shard_map/ppermute | solution.py:49
  4.6 2.4 %collective-permute-start = (bf16[2,2,32,896]{3,2,1,0:T(8,128)(2,1)}, bf16[2,2,32,896]{3,2,1,0:T(8,128)(2,1)S(1)}, u32[]{:S(2)}, u32[]{:S(2)}) collective-permute-start(bf16[2,2,32,896]{3,2,1,0:T(8,128)(2,1)} %refs_4_), channel_id=1, source_target_pairs={{0,1},{1,2},{2,3},{3,0},{4,7},{5,4},{6,5},{7,6},{8,9},{9,10},{10,1... | collective-permute-start | bytes 688136 | tf_op jit(solution)/shard_map/ppermute | solution.py:49
  7.3 1.7 %collective-permute-done.2.s3.a3 = bf16[2,2,32,896]{3,2,1,0:T(8,128)(2,1)S(1)} collective-permute-done((bf16[2,2,32,896]{3,2,1,0:T(8,128)(2,1)}, bf16[2,2,32,896]{3,2,1,0:T(8,128)(2,1)S(1)}, u32[]{:S(2)}, u32[]{:S(2)}) %collective-permute-start.2) | collective-permute-done | bytes 229408 | tf_op jit(solution)/shard_map/ppermute | solution.py:49
  9.0 4.7 %collective-permute-start.4 = (bf16[2,2,32,896]{3,2,1,0:T(8,128)(2,1)S(1)}, bf16[2,2,32,896]{3,2,1,0:T(8,128)(2,1)S(1)}, u32[]{:S(2)}, u32[]{:S(2)}) collective-permute-start(bf16[2,2,32,896]{3,2,1,0:T(8,128)(2,1)S(1)} %collective-permute-done.2.s3.a3), channel_id=1, source_target_pairs={{0,4},{4,0},{1,5},{5,1},{2,6},{6,2},{3,7},{7,3},{8,12},{12,8},{9,1... | collective-permute-start | bytes 688136 | tf_op jit(solution)/shard_map/ppermute | solution.py:53
  13.6 0.8 reshape.19
  14.5 2.2 %shard_map.101 = (bf16[896,1024]{1,0:T(8,128)(2,1)S(1)}, bf16[896,1024]{1,0:T(8,128)(2,1)S(1)}, bf16[128,1024]{1,0:T(8,128)(2,1)S(1)}, bf16[128,1024]{1,0:T(8,128)(2,1)S(1)}, bf16[2,2,32,896]{3,2,1,0:T(8,128)(2,1)S(1)}) custom-call(bf16[896,1024]{1,0:T(8,128)(2,1)} %key_hbm.1, bf16[896,1024]{1,0:T(8,128)(2,1)} %value_hbm.1, bf16[128,1024]{1,0:T(8,128)(2,1)} %refs_2_.1, ...), custom_call_target="tpu_custom_call" | custom-call | tf_op jit(solution)/shard_map/pallas_call | solution.py:102
  16.8 9.0 %shard_map.102 = (bf16[128,1024]{1,0:T(8,128)(2,1)}, bf16[128,1024]{1,0:T(8,128)(2,1)}, bf16[512,1024]{1,0:T(8,128)(2,1)S(1)}, bf16[512,1024]{1,0:T(8,128)(2,1)S(1)}) custom-call(s32[5]{0:T(128)S(1)} %pad_add_fusion.flags, bf16[2,2,32,896]{3,2,1,0:T(8,128)(2,1)S(1)} %get-tuple-element.66.s0.a0, bf16[2,2,32,896]{3,2,1,0:T(8,128)(2,1)S(1)} %collective-permute-done.s1.a1, ...), custom_call_target="tpu_custom_call" | custom-call | flops 4000000000 | bytes 5000000 | tf_op jit(solution)/shard_map/pallas_call | solution.py:146
  25.9 0.5 collective-permute-start.6
  26.4 1.2 %shard_map.103.partial = f32[896,1024]{1,0:T(8,128)S(1)} custom-call(bf16[2,2,32,896]{3,2,1,0:T(8,128)(2,1)S(1)} %get-tuple-element.66.s0.a0, bf16[2,2,32,896]{3,2,1,0:T(8,128)(2,1)S(1)} %collective-permute-done.s1.a1, bf16[2,2,32,896]{3,2,1,0:T(8,128)(2,1)S(1)} %collective-permute-done.1.s2.a2, bf16[2,2,32,896]{3,2,1,0:T(8,128)(2,1)S(1)} %collective-permute-done.2.s3.a3, ...), custom_call_target="tpu_custom_call" | custom-call | flops 2000000000 | bytes 5000000 | tf_op jit(solution)/shard_map/pallas_call | solution.py:211
  27.5 1.0 %collective-permute-done.7.grads = bf16[512,1024]{1,0:T(8,128)(2,1)S(1)} collective-permute-done((bf16[512,1024]{1,0:T(8,128)(2,1)S(1)}, bf16[512,1024]{1,0:T(8,128)(2,1)S(1)}, u32[]{:S(2)}, u32[]{:S(2)}) %collective-permute-start.7) | collective-permute-done | bytes 1048608 | tf_op jit(solution)/shard_map/ppermute | solution.py:53
  29.2 1.9 %shard_map.104 = (f32[224,1024]{1,0:T(8,128)S(1)}, bf16[224,1024]{1,0:T(8,128)(2,1)S(1)}, bf16[224,1024]{1,0:T(8,128)(2,1)S(1)}, f32[224,1024]{1,0:T(8,128)S(1)}) custom-call(s32[6]{0:T(128)S(1)} %stack.24.place, bf16[2,2,32,896]{3,2,1,0:T(8,128)(2,1)S(1)} %collective-permute-done.3.a0, bf16[2,2,32,896]{3,2,1,0:T(8,128)(2,1)S(1)} %collective-permute-done.5.a1, ...), custom_call_target="tpu_custom_call" | custom-call | flops 2000000000 | bytes 5000000 | tf_op jit(solution)/shard_map/pallas_call | solution.py:235
  31.1 2.1 %collective-permute-start.8 = (bf16[224,1024]{1,0:T(8,128)(2,1)S(1)}, bf16[224,1024]{1,0:T(8,128)(2,1)S(1)}, u32[]{:S(2)}, u32[]{:S(2)}) collective-permute-start(bf16[224,1024]{1,0:T(8,128)(2,1)S(1)} %get-tuple-element.88), channel_id=1, source_target_pairs={{0,64},{64,128},{128,192},{192,0},{4,196},{68,4},{132,68},{196,132... | collective-permute-start | bytes 1376264 | tf_op jit(solution)/shard_map/ppermute | solution.py:49
  33.2 4.6 %shard_map.105 = (f32[2,2,32,896]{3,2,1,0:T(8,128)S(1)}, bf16[2,2,32,896]{3,2,1,0:T(8,128)(2,1)S(1)}, f32[2,2,32,896]{3,2,1,0:T(8,128)S(1)}, bf16[2,2,32,896]{3,2,1,0:T(8,128)(2,1)S(1)}) custom-call(s32[5]{0:T(128)S(1)} %pad_add_fusion.flags, bf16[512,1024]{1,0:T(8,128)(2,1)S(1)} %get-tuple-element.84.grads.keep, ...), custom_call_target="tpu_custom_call" | custom-call | flops 4000000000 | bytes 10000000 | tf_op jit(solution)/shard_map/pallas_call | solution.py:188
  37.8 4.5 %collective-permute-done.8.refs_1_ = bf16[224,1024]{1,0:T(8,128)(2,1)S(1)} collective-permute-done((bf16[224,1024]{1,0:T(8,128)(2,1)S(1)}, bf16[224,1024]{1,0:T(8,128)(2,1)S(1)}, u32[]{:S(2)}, u32[]{:S(2)}) %collective-permute-start.8) | collective-permute-done | bytes 458784 | tf_op jit(solution)/shard_map/ppermute | solution.py:49
  42.3 3.1 %collective-permute-done.9.back = bf16[224,1024]{1,0:T(8,128)(2,1)S(1)} collective-permute-done((bf16[224,1024]{1,0:T(8,128)(2,1)S(1)}, bf16[224,1024]{1,0:T(8,128)(2,1)S(1)}, u32[]{:S(2)}, u32[]{:S(2)}) %collective-permute-start.9) | collective-permute-done | bytes 458784 | tf_op jit(solution)/shard_map/ppermute | solution.py:49
  45.5 0.6 collective-permute-start.10
  46.1 2.3 %collective-permute-start.11 = (bf16[2,2,32,896]{3,2,1,0:T(8,128)(2,1)S(1)}, bf16[2,2,32,896]{3,2,1,0:T(8,128)(2,1)S(1)}, u32[]{:S(2)}, u32[]{:S(2)}) collective-permute-start(bf16[2,2,32,896]{3,2,1,0:T(8,128)(2,1)S(1)} %get-tuple-element.96), channel_id=1, source_target_pairs={{0,1},{1,2},{2,3},{3,0},{4,7},{5,4},{6,5},{7,6},{8,9},{9,10},{10,1... | collective-permute-start | bytes 688136 | tf_op jit(solution)/shard_map/ppermute | solution.py:49
  48.4 3.0 %collective-permute-done.11.refs_1_ = bf16[2,2,32,896]{3,2,1,0:T(8,128)(2,1)S(1)} collective-permute-done((bf16[2,2,32,896]{3,2,1,0:T(8,128)(2,1)S(1)}, bf16[2,2,32,896]{3,2,1,0:T(8,128)(2,1)S(1)}, u32[]{:S(2)}, u32[]{:S(2)}) %collective-permute-start.11) | collective-permute-done | bytes 229408 | tf_op jit(solution)/shard_map/ppermute | solution.py:49
  51.4 1.8 %collective-permute-done.10.front = bf16[224,1024]{1,0:T(8,128)(2,1)S(1)} collective-permute-done((bf16[224,1024]{1,0:T(8,128)(2,1)S(1)}, bf16[224,1024]{1,0:T(8,128)(2,1)S(1)}, u32[]{:S(2)}, u32[]{:S(2)}) %collective-permute-start.10) | collective-permute-done | bytes 458784 | tf_op jit(solution)/shard_map/ppermute | solution.py:49
  53.2 1.1 %shard_map.107 = (f32[28,1024]{1,0:T(8,128)S(1)}, f32[32,1024]{1,0:T(8,128)S(1)}, f32[32,1024]{1,0:T(8,128)S(1)}, bf16[2,32,1024]{2,1,0:T(8,128)(2,1)S(1)}, bf16[3,32,1024]{2,1,0:T(8,128)(2,1)S(1)}) custom-call(s32[6]{0:T(128)S(1)} %stack.24.place, f32[224,1024]{1,0:T(8,128)S(1)} %get-tuple-element.87.mine, ...), custom_call_target="tpu_custom_call" | custom-call | tf_op jit(solution)/shard_map/pallas_call | solution.py:306
  54.3 1.6 %collective-permute-start.12 = (bf16[3,32,1024]{2,1,0:T(8,128)(2,1)S(1)}, bf16[3,32,1024]{2,1,0:T(8,128)(2,1)S(1)}, u32[]{:S(2)}, u32[]{:S(2)}) collective-permute-start(bf16[3,32,1024]{2,1,0:T(8,128)(2,1)S(1)} %get-tuple-element.99), channel_id=1, source_target_pairs={{0,4},{4,0},{1,5},{5,1},{2,6},{6,2},{3,7},{7,3},{8,12},{12,8},{9,1... | collective-permute-start | bytes 589832 | tf_op jit(solution)/shard_map/ppermute | solution.py:53
  55.9 0.7 collective-permute-start.14
  56.7 2.0 %collective-permute-start.15 = (bf16[2,2,32,896]{3,2,1,0:T(8,128)(2,1)S(1)}, bf16[2,2,32,896]{3,2,1,0:T(8,128)(2,1)S(1)}, u32[]{:S(2)}, u32[]{:S(2)}) collective-permute-start(bf16[2,2,32,896]{3,2,1,0:T(8,128)(2,1)S(1)} %shard_map.109), channel_id=1, source_target_pairs={{0,1},{1,2},{2,3},{3,0},{4,7},{5,4},{6,5},{7,6},{8,9},{9,10},{10,1... | collective-permute-start | bytes 688136 | tf_op jit(solution)/shard_map/ppermute | solution.py:49
  58.7 5.6 %collective-permute-start.13 = (bf16[3,32,1024]{2,1,0:T(8,128)(2,1)S(1)}, bf16[3,32,1024]{2,1,0:T(8,128)(2,1)S(1)}, u32[]{:S(2)}, u32[]{:S(2)}) collective-permute-start(bf16[3,32,1024]{2,1,0:T(8,128)(2,1)S(1)} %shard_map.108), channel_id=1, source_target_pairs={{0,16},{8,24},{16,32},{24,40},{32,48},{40,56},{48,0},{56,8},{4,52}... | collective-permute-start | bytes 589832 | tf_op jit(solution)/shard_map/ppermute | solution.py:49
  64.4 4.7 %collective-permute-done.13.arrived = bf16[3,32,1024]{2,1,0:T(8,128)(2,1)S(1)} collective-permute-done((bf16[3,32,1024]{2,1,0:T(8,128)(2,1)S(1)}, bf16[3,32,1024]{2,1,0:T(8,128)(2,1)S(1)}, u32[]{:S(2)}, u32[]{:S(2)}) %collective-permute-start.13) | collective-permute-done | bytes 196640 | tf_op jit(solution)/shard_map/ppermute | solution.py:49
  69.1 2.1 %collective-permute-start.16 = (bf16[2,32,1024]{2,1,0:T(8,128)(2,1)S(1)}, bf16[2,32,1024]{2,1,0:T(8,128)(2,1)S(1)}, u32[]{:S(2)}, u32[]{:S(2)}) collective-permute-start(bf16[2,32,1024]{2,1,0:T(8,128)(2,1)S(1)} %get-tuple-element.109), channel_id=1, source_target_pairs={{0,8},{8,16},{16,24},{24,32},{32,40},{40,48},{48,56},{56,0},{4,60}... | collective-permute-start | bytes 393224 | tf_op jit(solution)/shard_map/ppermute | solution.py:49
  71.2 2.1 %collective-permute-start.17 = (bf16[2,32,1024]{2,1,0:T(8,128)(2,1)S(1)}, bf16[2,32,1024]{2,1,0:T(8,128)(2,1)S(1)}, u32[]{:S(2)}, u32[]{:S(2)}) collective-permute-start(bf16[2,32,1024]{2,1,0:T(8,128)(2,1)S(1)} %get-tuple-element.110), channel_id=1, source_target_pairs={{0,16},{8,24},{16,32},{24,40},{32,48},{40,56},{48,0},{56,8},{4,52}... | collective-permute-start | bytes 393224 | tf_op jit(solution)/shard_map/ppermute | solution.py:49
  73.3 4.2 %collective-permute-done.17.two = bf16[2,32,1024]{2,1,0:T(8,128)(2,1)S(1)} collective-permute-done((bf16[2,32,1024]{2,1,0:T(8,128)(2,1)S(1)}, bf16[2,32,1024]{2,1,0:T(8,128)(2,1)S(1)}, u32[]{:S(2)}, u32[]{:S(2)}) %collective-permute-start.17) | collective-permute-done | bytes 131104 | tf_op jit(solution)/shard_map/ppermute | solution.py:49
  77.5 0.6 shard_map.111
  78.1 1.9 %collective-permute-start.18 = (f32[2,14,1024]{2,1,0:T(8,128)S(1)}, f32[2,14,1024]{2,1,0:T(8,128)S(1)}, u32[]{:S(2)}, u32[]{:S(2)}) collective-permute-start(f32[2,14,1024]{2,1,0:T(8,128)S(1)} %get-tuple-element.112), channel_id=1, source_target_pairs={{0,4},{4,0},{1,5},{5,1},{2,6},{6,2},{3,7},{7,3},{8,12},{12,8},{9,1... | collective-permute-start | bytes 344072 | tf_op jit(solution)/shard_map/ppermute | solution.py:53
  80.0 0.8 %convert_add_fusion = f32[2,2,32,896]{3,2,1,0:T(8,128)} fusion(bf16[2,2,32,896]{3,2,1,0:T(8,128)(2,1)S(1)} %collective-permute-done.15, f32[2,2,32,896]{3,2,1,0:T(8,128)S(1)} %get-tuple-element.86, bf16[2,2,32,896]{3,2,1,0:T(8,128)(2,1)S(1)} %collective-permute-done.14), kind=kLoop, calls=%fused_computation | loop fusion | flops 458752 | bytes 1376256 | tf_op jit(solution)/shard_map/add | solution.py:421
  81.0 0.7 select_bitcast_fusion
  (22 shorter events, 1.8 us)
Async XLA Ops:
  0.6 8.3 %collective-permute-start.2 = (bf16[2,2,32,896]{3,2,1,0:T(8,128)(2,1)}, bf16[2,2,32,896]{3,2,1,0:T(8,128)(2,1)S(1)}, u32[]{:S(2)}, u32[]{:S(2)}) collective-permute-start(bf16[2,2,32,896]{3,2,1,0:T(8,128)(2,1)} %refs_4_), channel_id=1, source_target_pairs={{0,2},{1,3},{2,0},{3,1},{4,6},{5,7},{6,4},{7,5},{8,10},{9,11},{10,... | collective-permute-start | bytes 688136 | tf_op jit(solution)/shard_map/ppermute | solution.py:49
  4.3 12.5 %collective-permute-start.1 = (bf16[2,2,32,896]{3,2,1,0:T(8,128)(2,1)}, bf16[2,2,32,896]{3,2,1,0:T(8,128)(2,1)S(1)}, u32[]{:S(2)}, u32[]{:S(2)}) collective-permute-start(bf16[2,2,32,896]{3,2,1,0:T(8,128)(2,1)} %refs_4_), channel_id=1, source_target_pairs={{0,3},{1,0},{2,1},{3,2},{4,5},{5,6},{6,7},{7,4},{8,11},{9,8},{10,9... | collective-permute-start | bytes 688136 | tf_op jit(solution)/shard_map/ppermute | solution.py:49
  4.6 12.2 %collective-permute-start = (bf16[2,2,32,896]{3,2,1,0:T(8,128)(2,1)}, bf16[2,2,32,896]{3,2,1,0:T(8,128)(2,1)S(1)}, u32[]{:S(2)}, u32[]{:S(2)}) collective-permute-start(bf16[2,2,32,896]{3,2,1,0:T(8,128)(2,1)} %refs_4_), channel_id=1, source_target_pairs={{0,1},{1,2},{2,3},{3,0},{4,7},{5,4},{6,5},{7,6},{8,9},{9,10},{10,1... | collective-permute-start | bytes 688136 | tf_op jit(solution)/shard_map/ppermute | solution.py:49
  7.0 9.9 %collective-permute-start.3 = (bf16[2,2,32,896]{3,2,1,0:T(8,128)(2,1)}, bf16[2,2,32,896]{3,2,1,0:T(8,128)(2,1)S(1)}, u32[]{:S(2)}, u32[]{:S(2)}) collective-permute-start(bf16[2,2,32,896]{3,2,1,0:T(8,128)(2,1)} %refs_4_), channel_id=1, source_target_pairs={{0,4},{4,0},{1,5},{5,1},{2,6},{6,2},{3,7},{7,3},{8,12},{12,8},{9,1... | collective-permute-start | bytes 688136 | tf_op jit(solution)/shard_map/ppermute | solution.py:53
  9.0 7.9 %collective-permute-start.4 = (bf16[2,2,32,896]{3,2,1,0:T(8,128)(2,1)S(1)}, bf16[2,2,32,896]{3,2,1,0:T(8,128)(2,1)S(1)}, u32[]{:S(2)}, u32[]{:S(2)}) collective-permute-start(bf16[2,2,32,896]{3,2,1,0:T(8,128)(2,1)S(1)} %collective-permute-done.2.s3.a3), channel_id=1, source_target_pairs={{0,4},{4,0},{1,5},{5,1},{2,6},{6,2},{3,7},{7,3},{8,12},{12,8},{9,1... | collective-permute-start | bytes 688136 | tf_op jit(solution)/shard_map/ppermute | solution.py:53
  25.9 2.7 %collective-permute-start.7 = (bf16[512,1024]{1,0:T(8,128)(2,1)S(1)}, bf16[512,1024]{1,0:T(8,128)(2,1)S(1)}, u32[]{:S(2)}, u32[]{:S(2)}) collective-permute-start(bf16[512,1024]{1,0:T(8,128)(2,1)S(1)} %get-tuple-element.85.send), channel_id=1, source_target_pairs={{0,4},{4,0},{1,5},{5,1},{2,6},{6,2},{3,7},{7,3},{8,12},{12,8},{9,1... | collective-permute-start | bytes 3145736 | tf_op jit(solution)/shard_map/ppermute | solution.py:53
  25.9 3.0 %collective-permute-start.6 = (bf16[2,2,32,896]{3,2,1,0:T(8,128)(2,1)S(1)}, bf16[2,2,32,896]{3,2,1,0:T(8,128)(2,1)S(1)}, u32[]{:S(2)}, u32[]{:S(2)}) collective-permute-start(bf16[2,2,32,896]{3,2,1,0:T(8,128)(2,1)S(1)} %collective-permute-done.1.s2.a2), channel_id=1, source_target_pairs={{0,4},{4,0},{1,5},{5,1},{2,6},{6,2},{3,7},{7,3},{8,12},{12,8},{9,1... | collective-permute-start | bytes 688136 | tf_op jit(solution)/shard_map/ppermute | solution.py:53
  26.4 2.8 %collective-permute-start.5 = (bf16[2,2,32,896]{3,2,1,0:T(8,128)(2,1)S(1)}, bf16[2,2,32,896]{3,2,1,0:T(8,128)(2,1)S(1)}, u32[]{:S(2)}, u32[]{:S(2)}) collective-permute-start(bf16[2,2,32,896]{3,2,1,0:T(8,128)(2,1)S(1)} %collective-permute-done.s1.a1), channel_id=1, source_target_pairs={{0,4},{4,0},{1,5},{5,1},{2,6},{6,2},{3,7},{7,3},{8,12},{12,8},{9,1... | collective-permute-start | bytes 688136 | tf_op jit(solution)/shard_map/ppermute | solution.py:53
  31.1 11.2 %collective-permute-start.8 = (bf16[224,1024]{1,0:T(8,128)(2,1)S(1)}, bf16[224,1024]{1,0:T(8,128)(2,1)S(1)}, u32[]{:S(2)}, u32[]{:S(2)}) collective-permute-start(bf16[224,1024]{1,0:T(8,128)(2,1)S(1)} %get-tuple-element.88), channel_id=1, source_target_pairs={{0,64},{64,128},{128,192},{192,0},{4,196},{68,4},{132,68},{196,132... | collective-permute-start | bytes 1376264 | tf_op jit(solution)/shard_map/ppermute | solution.py:49
  33.2 12.2 %collective-permute-start.9 = (bf16[224,1024]{1,0:T(8,128)(2,1)S(1)}, bf16[224,1024]{1,0:T(8,128)(2,1)S(1)}, u32[]{:S(2)}, u32[]{:S(2)}) collective-permute-start(bf16[224,1024]{1,0:T(8,128)(2,1)S(1)} %get-tuple-element.89), channel_id=1, source_target_pairs={{0,192},{64,0},{128,64},{192,128},{4,68},{68,132},{132,196},{196,4... | collective-permute-start | bytes 1376264 | tf_op jit(solution)/shard_map/ppermute | solution.py:49
  45.5 7.7 %collective-permute-start.10 = (bf16[224,1024]{1,0:T(8,128)(2,1)S(1)}, bf16[224,1024]{1,0:T(8,128)(2,1)S(1)}, u32[]{:S(2)}, u32[]{:S(2)}) collective-permute-start(bf16[224,1024]{1,0:T(8,128)(2,1)S(1)} %shard_map.106), channel_id=1, source_target_pairs={{0,64},{64,128},{128,192},{192,0},{4,196},{68,4},{132,68},{196,132... | collective-permute-start | bytes 1376264 | tf_op jit(solution)/shard_map/ppermute | solution.py:49
  46.1 5.3 %collective-permute-start.11 = (bf16[2,2,32,896]{3,2,1,0:T(8,128)(2,1)S(1)}, bf16[2,2,32,896]{3,2,1,0:T(8,128)(2,1)S(1)}, u32[]{:S(2)}, u32[]{:S(2)}) collective-permute-start(bf16[2,2,32,896]{3,2,1,0:T(8,128)(2,1)S(1)} %get-tuple-element.96), channel_id=1, source_target_pairs={{0,1},{1,2},{2,3},{3,0},{4,7},{5,4},{6,5},{7,6},{8,9},{9,10},{10,1... | collective-permute-start | bytes 688136 | tf_op jit(solution)/shard_map/ppermute | solution.py:49
  54.3 4.4 %collective-permute-start.12 = (bf16[3,32,1024]{2,1,0:T(8,128)(2,1)S(1)}, bf16[3,32,1024]{2,1,0:T(8,128)(2,1)S(1)}, u32[]{:S(2)}, u32[]{:S(2)}) collective-permute-start(bf16[3,32,1024]{2,1,0:T(8,128)(2,1)S(1)} %get-tuple-element.99), channel_id=1, source_target_pairs={{0,4},{4,0},{1,5},{5,1},{2,6},{6,2},{3,7},{7,3},{8,12},{12,8},{9,1... | collective-permute-start | bytes 589832 | tf_op jit(solution)/shard_map/ppermute | solution.py:53
  55.9 8.4 %collective-permute-start.14 = (bf16[2,2,32,896]{3,2,1,0:T(8,128)(2,1)S(1)}, bf16[2,2,32,896]{3,2,1,0:T(8,128)(2,1)S(1)}, u32[]{:S(2)}, u32[]{:S(2)}) collective-permute-start(bf16[2,2,32,896]{3,2,1,0:T(8,128)(2,1)S(1)} %get-tuple-element.100), channel_id=1, source_target_pairs={{0,3},{1,0},{2,1},{3,2},{4,5},{5,6},{6,7},{7,4},{8,11},{9,8},{10,9... | collective-permute-start | bytes 688136 | tf_op jit(solution)/shard_map/ppermute | solution.py:49
  56.7 7.7 %collective-permute-start.15 = (bf16[2,2,32,896]{3,2,1,0:T(8,128)(2,1)S(1)}, bf16[2,2,32,896]{3,2,1,0:T(8,128)(2,1)S(1)}, u32[]{:S(2)}, u32[]{:S(2)}) collective-permute-start(bf16[2,2,32,896]{3,2,1,0:T(8,128)(2,1)S(1)} %shard_map.109), channel_id=1, source_target_pairs={{0,1},{1,2},{2,3},{3,0},{4,7},{5,4},{6,5},{7,6},{8,9},{9,10},{10,1... | collective-permute-start | bytes 688136 | tf_op jit(solution)/shard_map/ppermute | solution.py:49
  58.7 10.3 %collective-permute-start.13 = (bf16[3,32,1024]{2,1,0:T(8,128)(2,1)S(1)}, bf16[3,32,1024]{2,1,0:T(8,128)(2,1)S(1)}, u32[]{:S(2)}, u32[]{:S(2)}) collective-permute-start(bf16[3,32,1024]{2,1,0:T(8,128)(2,1)S(1)} %shard_map.108), channel_id=1, source_target_pairs={{0,16},{8,24},{16,32},{24,40},{32,48},{40,56},{48,0},{56,8},{4,52}... | collective-permute-start | bytes 589832 | tf_op jit(solution)/shard_map/ppermute | solution.py:49
  69.1 4.2 %collective-permute-start.16 = (bf16[2,32,1024]{2,1,0:T(8,128)(2,1)S(1)}, bf16[2,32,1024]{2,1,0:T(8,128)(2,1)S(1)}, u32[]{:S(2)}, u32[]{:S(2)}) collective-permute-start(bf16[2,32,1024]{2,1,0:T(8,128)(2,1)S(1)} %get-tuple-element.109), channel_id=1, source_target_pairs={{0,8},{8,16},{16,24},{24,32},{32,40},{40,48},{48,56},{56,0},{4,60}... | collective-permute-start | bytes 393224 | tf_op jit(solution)/shard_map/ppermute | solution.py:49
  71.2 6.3 %collective-permute-start.17 = (bf16[2,32,1024]{2,1,0:T(8,128)(2,1)S(1)}, bf16[2,32,1024]{2,1,0:T(8,128)(2,1)S(1)}, u32[]{:S(2)}, u32[]{:S(2)}) collective-permute-start(bf16[2,32,1024]{2,1,0:T(8,128)(2,1)S(1)} %get-tuple-element.110), channel_id=1, source_target_pairs={{0,16},{8,24},{16,32},{24,40},{32,48},{40,56},{48,0},{56,8},{4,52}... | collective-permute-start | bytes 393224 | tf_op jit(solution)/shard_map/ppermute | solution.py:49
  78.1 2.9 %collective-permute-start.18 = (f32[2,14,1024]{2,1,0:T(8,128)S(1)}, f32[2,14,1024]{2,1,0:T(8,128)S(1)}, u32[]{:S(2)}, u32[]{:S(2)}) collective-permute-start(f32[2,14,1024]{2,1,0:T(8,128)S(1)} %get-tuple-element.112), channel_id=1, source_target_pairs={{0,4},{4,0},{1,5},{5,1},{2,6},{6,2},{3,7},{7,3},{8,12},{12,8},{9,1... | collective-permute-start | bytes 344072 | tf_op jit(solution)/shard_map/ppermute | solution.py:53

commit v3 on v2

v3 whole, which is shorter than its diff:
```python
import jax
import jax.numpy as jnp
from jax import lax
from jax.experimental import pallas as pl
from jax.experimental.pallas import tpu as pltpu
from jax.sharding import Mesh, PartitionSpec as P

HEAD = 128
PAD = 32
BLOCK = 512
BF = jnp.bfloat16
F32 = jnp.float32
NN = (((1,), (0,)), ((), ()))
NT = (((1,), (1,)), ((), ()))
TN = (((0,), (0,)), ((), ()))
SMEM = pl.BlockSpec(memory_space=pltpu.SMEM)
VMEM = pl.BlockSpec(memory_space=pltpu.VMEM)
HBM = pl.BlockSpec(memory_space=pltpu.HBM)


def params(**more):
    return pltpu.CompilerParams(vmem_limit_bytes=32 * 1024 * 1024, **more)


def shape(dims, dtype):
    return pltpu.VMEM(dims, dtype)


def near_by(*arrays):
    return [pltpu.with_memory_space_constraint(a, pltpu.VMEM) for a in arrays]


def dot(a, b, dims=NN):
    return lax.dot_general(a, b, dims, preferred_element_type=F32)


def cost(flops, moved):
    return pl.CostEstimate(flops=flops, bytes_accessed=moved, transcendentals=0)


def hop(value, axis, size, step, cross=False):
    inner = axis == "x"
    number = lambda i, core: core * size + i if inner else i * 2 + core
    pairs = []
    for core in range(2):
        for i in range(size):
            target = (i + (step if core == 0 else -step)) % size
            pairs.append((number(i, core), number(target, 1 - core if cross else core)))
    return lax.ppermute(value, ("c", axis) if inner else (axis, "c"), pairs)


def swap(value):
    return lax.ppermute(value, "c", [(0, 1), (1, 0)])


def scored(q, g, k, v, live, empty):
    scale = HEAD ** (-0.5)
    raw = jnp.exp(dot(q, k, NT) * scale) * live
    prob_grad = dot(g, v, NT)
    total = jnp.sum(raw, axis=-1, keepdims=True) + empty
    probs = raw * (1.0 / total)
    delta = jnp.sum(probs * prob_grad, axis=-1, keepdims=True)
    return probs.astype(BF), (probs * (prob_grad - delta) * scale).astype(BF)


def applied(q, g, k, v, low, score_grad):
    tokens = q.shape[0]
    across = dot(jnp.concatenate([low, score_grad], axis=0), jnp.concatenate([v, k], axis=1))
    none = jnp.zeros_like(q)
    tall = jnp.concatenate(
        [jnp.concatenate([q, none], axis=1), jnp.concatenate([none, g], axis=1)], axis=0
    )
    down = dot(jnp.concatenate([score_grad, low], axis=0), tall, TN)
    return (
        across[:tokens, :HEAD].astype(BF),
        across[tokens:, HEAD:].astype(BF),
        down[:, :HEAD].astype(BF),
        down[:, HEAD:].astype(BF),
    )


def gathered(slabs, rows, offset):
    stretches, neigh, group, _ = slabs[0].shape
    first = offset
    for c in range(stretches):
        for s in slabs:
            for n in range(neigh):
                rows[first : first + group] = s[c, n]
                first += group


def load_body(*refs):
    count = (len(refs) - 1) // 2
    copies = [
        pltpu.make_async_copy(refs[i], refs[count + i], refs[-1].at[i]) for i in range(count)
    ]
    for copy in copies:
        copy.start()
    for copy in copies:
        copy.wait()


def load(*arrays):
    return pl.pallas_call(
        load_body,
        in_specs=[HBM] * len(arrays),
        out_specs=[VMEM] * len(arrays),
        out_shape=[shape(a.shape, a.dtype) for a in arrays],
        scratch_shapes=[pltpu.SemaphoreType.DMA((len(arrays),))],
        compiler_params=params(),
    )(*[pltpu.with_memory_space_constraint(a, pltpu.HBM) for a in arrays])


def project_body(a, b, key_w, value_w, keys, values, rows):
    stretches, neigh_count, group, _ = a.shape
    gathered((a, b), rows, 0)
    span = 2 * neigh_count * group
    for weight, out in ((key_w, keys), (value_w, values)):
        done = dot(rows[...], weight[...]).astype(BF)
        for c in range(stretches):
            out[c] = done[c * span : (c + 1) * span]


def project(slabs, key_w, value_w):
    stretches, neigh_count, group, enc = slabs[0].shape
    dims = (stretches, 2 * neigh_count * group, key_w.shape[1])
    return pl.pallas_call(
        project_body,
        in_specs=[VMEM] * 4,
        out_specs=[VMEM] * 2,
        out_shape=[shape(dims, BF)] * 2,
        scratch_shapes=[pltpu.VMEM((stretches * dims[1], enc), BF)],
        compiler_params=params(),
    )(*near_by(*slabs, key_w, value_w))


def attend_body(group, flags, k1, v1, k2, v2, queries, cotangent,
                attended, query_grad, keep, send):
    stretches, half, width = k1.shape
    span = 2 * half
    tokens = queries.shape[0] // stretches
    first = flags[0] == 0
    neigh = (lax.broadcasted_iota(jnp.int32, (1, span), 1) // group) % 2
    masks = []
    for c in range(stretches):
        one, two = flags[1 + 2 * c], flags[2 + 2 * c]
        live = jnp.where(neigh == 0, one, two).astype(F32)
        masks.append((live, jnp.where(one + two == 0, 1.0, 0.0).astype(F32)))
    for start in range(0, width, BLOCK):
        waiting = []
        for c in range(stretches):
            r = slice(c * span, (c + 1) * span)
            t = slice(c * tokens, (c + 1) * tokens)
            for h in range(start, start + BLOCK, HEAD):
                w = slice(h, h + HEAD)
                heads = (
                    queries[t, w], cotangent[t, w],
                    jnp.concatenate([k1[c, :, w], k2[c, :, w]], axis=0),
                    jnp.concatenate([v1[c, :, w], v2[c, :, w]], axis=0),
                )
                waiting.append((r, t, w, heads, scored(*heads, *masks[c])))
        for r, t, w, heads, scores in waiting:
            out, q_grad, k_grad, v_grad = applied(*heads, *scores)
            attended[t, w] = out
            query_grad[t, w] = q_grad
            keep[r, w] = jnp.where(first, k_grad, v_grad)
            send[r, w] = jnp.where(first, v_grad, k_grad)


def attend(flags, k1, v1, k2, v2, queries, cotangent, group):
    stretches, half, width = k1.shape
    tokens = queries.shape[0]
    row_count = 2 * stretches * half
    return pl.pallas_call(
        lambda *refs: attend_body(group, *refs),
        in_specs=[SMEM] + [VMEM] * 6,
        out_specs=[VMEM] * 4,
        out_shape=[jax.ShapeDtypeStruct((tokens, width), BF)] * 2
        + [shape((row_count, width), BF)] * 2,
        compiler_params=params(),
    )(flags, *near_by(k1, v1, k2, v2, queries, cotangent))


def passage_body(flags, keep, send, key_hbm, value_hbm, o0, o1, o2, o3, key_w, value_w, sems):
    first = flags[0] == 0
    width = keep.shape[1]
    loads = []
    for i, start in enumerate(range(0, width, BLOCK)):
        here = pl.ds(start, BLOCK)
        for k, (source, target) in enumerate(((key_hbm, key_w), (value_hbm, value_w))):
            copy = pltpu.make_async_copy(source.at[:, here], target.at[i], sems.at[2 * i + k])
            copy.start()
            loads.append(copy)
    total = 0.0
    for i, start in enumerate(range(0, width, BLOCK)):
        a, b = keep[:, start : start + BLOCK], send[:, start : start + BLOCK]
        loads[2 * i].wait()
        loads[2 * i + 1].wait()
        total = total + dot(jnp.where(first, a, b), key_w[i], NT)
        total = total + dot(jnp.where(first, b, a), value_w[i], NT)
    stretches, neigh, group, _ = o0.shape
    start = 0
    for c in range(stretches):
        for o in (o0, o1, o2, o3):
            for n in range(neigh):
                o[c, n] = total[start : start + group].astype(o.dtype)
                start += group


def passage_grad(flags, keep, send, key_w, value_w, slab):
    enc, width = key_w.shape
    parts = width // BLOCK
    far = [pltpu.with_memory_space_constraint(a, pltpu.HBM) for a in (key_w, value_w)]
    return pl.pallas_call(
        passage_body,
        in_specs=[SMEM] + [VMEM] * 2 + [HBM] * 2,
        out_specs=[VMEM] * 4,
        out_shape=[shape(slab, d) for d in (F32, BF, BF, F32)],
        scratch_shapes=[
            pltpu.VMEM((parts, enc, BLOCK), BF),
            pltpu.VMEM((parts, enc, BLOCK), BF),
            pltpu.SemaphoreType.DMA((2 * parts,)),
        ],
        compiler_params=params(),
        cost_estimate=cost(4 * 10**9, 10**7),
    )(flags, *near_by(keep, send), *far)


def weight_body(a0, a1, a2, a3, grads, out, rows):
    gathered((a0, a1, a2, a3), rows, 0)
    out[...] = dot(rows[...], grads[...], TN)


def weight_grad(slabs, grads):
    enc = slabs[0].shape[-1]
    row_count, width = grads.shape
    return pl.pallas_call(
        weight_body,
        in_specs=[VMEM] * 5,
        out_specs=VMEM,
        out_shape=shape((enc, width), F32),
        scratch_shapes=[pltpu.VMEM((row_count, enc), BF)],
        compiler_params=params(),
        cost_estimate=cost(2 * 10**9, 5 * 10**6),
    )(*near_by(*slabs, grads))


def split_body(place, a0, a1, a2, a3, grads, partial, mine, far, back, front, rows, total):
    height = mine.shape[0]
    gathered((a0, a1, a2, a3), rows, 0)
    total[...] = partial[...] + dot(rows[...], grads[...], TN)
    for i, out in enumerate((mine, far, back, front)):
        first = pl.multiple_of(place[i] * height, 8)
        out[...] = total[pl.ds(first, height), :].astype(out.dtype)


def weight_split(place, slabs, grads, partial, parts):
    enc, width = partial.shape
    row_count = grads.shape[0]
    height = enc // parts
    return pl.pallas_call(
        split_body,
        in_specs=[SMEM] + [VMEM] * 6,
        out_specs=[VMEM] * 4,
        out_shape=[
            shape((height, width), F32),
            shape((height, width), BF),
            shape((height, width), BF),
            shape((height, width), F32),
        ],
        scratch_shapes=[pltpu.VMEM((row_count, enc), BF), pltpu.VMEM((enc, width), F32)],
        compiler_params=params(),
        cost_estimate=cost(2 * 10**9, 5 * 10**6),
    )(place, *near_by(*slabs, grads, partial))


def add_body(a, b, out):
    out[...] = (a[...] + b[...].astype(F32)).astype(BF)


def add(a, b):
    return pl.pallas_call(
        add_body,
        in_specs=[VMEM] * 2,
        out_specs=VMEM,
        out_shape=shape(a.shape, BF),
        compiler_params=params(),
    )(*near_by(a, b))


def deal_body(place, a, b, c, d, front, front_cross, base, base_cross):
    z, core = place[4], place[5]
    height = a.shape[0] // 8
    pad = jnp.zeros((PAD - height, a.shape[1]), F32)
    total = a[...] + b[...].astype(F32)
    rest = c[...] + d[...].astype(F32)
    for j in range(8):
        rows = slice(j * height, (j + 1) * height)
        one = jnp.concatenate([total[rows], pad], axis=0).astype(BF)
        two = jnp.concatenate([rest[rows], pad], axis=0)
        slot = lax.rem(jnp.where(core == 0, j - z, z - j) + 8, 8)

        @pl.when(slot < 5)
        def _():
            front[slot] = one
            base[slot] = two

        @pl.when(slot > 4)
        def _():
            front_cross[7 - slot] = one
            base_cross[7 - slot] = two


def deal(place, front, far_in, mine, back_in):
    width = mine.shape[1]
    return pl.pallas_call(
        deal_body,
        in_specs=[SMEM] + [VMEM] * 4,
        out_specs=[VMEM] * 4,
        out_shape=[shape((n, PAD, width), dtype) for dtype in (BF, F32) for n in (5, 3)],
        compiler_params=params(),
    )(place, *near_by(front, far_in, mine, back_in))


def fold_body(base, front, cross, front_cross, own, one, two, three):
    height = own.shape[0]
    add_up = lambda a, b, i: a[i] + b[i].astype(F32)
    own[...] = add_up(base, front, 0)[:height]
    one[0] = add_up(base, front, 1).astype(BF)
    one[1] = add_up(base, front, 4).astype(BF)
    one[2] = add_up(cross, front_cross, 0).astype(BF)
    two[0] = add_up(base, front, 2).astype(BF)
    two[1] = add_up(cross, front_cross, 1).astype(BF)
    three[0] = add_up(base, front, 3)
    three[1] = add_up(cross, front_cross, 2)


def fold(base, front, cross, front_cross, height):
    _, pad, width = base.shape
    return pl.pallas_call(
        fold_body,
        in_specs=[VMEM] * 4,
        out_specs=[VMEM] * 4,
        out_shape=[
            shape((height, width), F32),
            shape((3, pad, width), BF),
            shape((2, pad, width), BF),
            shape((2, pad, width), F32),
        ],
        compiler_params=params(),
    )(*near_by(base, front, cross, front_cross))


def relay_body(three, arrived, out):
    out[0] = (three[0] + arrived[1].astype(F32)).astype(BF)
    out[1] = three[1].astype(BF)


def relay(three, arrived):
    return pl.pallas_call(
        relay_body,
        in_specs=[VMEM] * 2,
        out_specs=VMEM,
        out_shape=shape(three.shape, BF),
        compiler_params=params(),
    )(*near_by(three, arrived))


def finish_body(place, own, one, two, three, stay, give):
    first = place[5] == 0
    height = own.shape[0]
    half = height // 2
    for k in range(2):
        value = one[2 * k].astype(F32) + two[k].astype(F32) + three[k].astype(F32)
        value = value[:height]
        if k == 0:
            value = value + own[...]
        low, high = value[:half], value[half:]
        stay[k] = jnp.where(first, low, high)
        give[k] = jnp.where(first, high, low)


def finish(place, own, one, two, three):
    height, width = own.shape
    dims = (2, height // 2, width)
    return pl.pallas_call(
        finish_body,
        in_specs=[SMEM] + [VMEM] * 4,
        out_specs=[VMEM] * 2,
        out_shape=[shape(dims, F32)] * 2,
        compiler_params=params(),
    )(place, *near_by(own, one, two, three))


def shards(queries, cotangent, neighbours, present, key_weight, value_weight):
    ny, nz, nx = 4, 8, 4
    y, z, core = lax.axis_index("y"), lax.axis_index("z"), lax.axis_index("c")
    first = core == 0
    sign = 1 - 2 * core
    place = jnp.stack([y, (y + 2) % ny, (y - sign) % ny, (y + sign) % ny, z, core])
    flags = jnp.concatenate([core[None], present.reshape(-1)]).astype(jnp.int32)
    tie = lax.optimization_barrier

    own = neighbours
    opposite, behind, ahead = (hop(own, "x", nx, step) for step in (2, 1, -1))
    flags, place, start = tie((flags, place, own))
    key_w, value_w, q, g, own = load(key_weight, value_weight, queries, cotangent, start)
    opposite, own = tie((opposite, own))
    k1, v1 = project((own, opposite), key_w, value_w)
    others = [swap(neighbours), swap(opposite)]
    behind, ahead, k1, v1, *others = tie((behind, ahead, k1, v1, *others))
    k2, v2 = project((behind, ahead), key_w, value_w)
    others += [swap(behind), swap(ahead)]
    k2, *others = tie((k2, *others))
    slabs = (own, opposite, behind, ahead)

    attended, query_grad, keep, send = attend(flags, k1, v1, k2, v2, q, g, own.shape[2])
    received = swap(send)
    partial = weight_grad(slabs, keep)
    received, partial = tie((received, partial))
    mine, far, back, front = weight_split(place, others, received, partial, ny)
    far_in = hop(far, "y", ny, 1)
    keep, send, front = tie((keep, send, front))
    p0, p3, p1, p2 = passage_grad(flags, keep, send, key_weight, value_weight, own.shape)
    back_in = hop(back, "y", ny, -1)
    far_in, back_in, p1, p2, p3 = tie((far_in, back_in, p1, p2, p3))
    front, front_cross, base, cross = deal(place, front, far_in, mine, back_in)
    front_in = hop(front, "y", ny, 1)
    cross_in = hop(front_cross, "y", ny, 1, cross=True)
    cross = swap(cross)
    front_in, cross_in, beyond = tie((front_in, cross_in, hop(p3, "x", nx, 1)))
    p1_in = hop(p1, "x", nx, -1)

    here, one, two, three = fold(base, front_in, cross, cross_in, mine.shape[0] // nz)
    one_in = hop(one, "z", nz, 1)
    two_in = hop(two, "z", nz, 2)
    three_in = hop(relay(three, one_in), "z", nz, 3)
    share = add(p2, beyond)
    returned = [p1_in, hop(share, "x", nx, 1)]
    three_in, returned = tie((three_in, returned))
    stay, give = finish(place, here, one_in, two_in, three_in)
    other = swap(give)
    neighbour_grad = p0
    for r in returned:
        neighbour_grad = neighbour_grad + r.astype(F32)
    main, rest = stay[0] + other[1], stay[1] + other[0]
    return (
        attended,
        query_grad,
        neighbour_grad,
        jnp.where(first, main, rest),
        jnp.where(first, rest, main),
    )


def solution(mesh):
    mesh = Mesh(mesh.devices.reshape(4, 8, 2, 4), ("y", "z", "c", "x"))
    dp = ("y", "z", "c")
    placed = (
        P(dp, "x"),
        P(dp, "x"),
        P(dp, None, "x", None),
        P(dp, None),
        P(None, "x"),
        P(None, "x"),
    )
    return jax.shard_map(
        shards,
        mesh=mesh,
        in_specs=placed,
        out_specs=(
            P(dp, "x"),
            P(dp, "x"),
            P(dp, None, "x", None),
            P(dp, "x"),
            P(dp, "x"),
        ),
        check_vma=False,
    )
```

time: 81.7 us -> 76.7 us (0.939)
  Pallas kernels: 20.9 us -> 17.6 us
  waiting for transfers between devices: 24.8 us -> 23.5 us
    ppermute x7, starting transfers between devices: 8.93 us -> 5.46 us  [swap(): return lax.ppermute(value, 'c', [(0, 1), (1, 0)])]
    pallas_call x7 -> x8, Pallas kernels: 10.9 us -> 7.72 us  [the longest x1 3.42 us: attend(): pl.pallas_call(lambda *refs: attend_body(group, *refs), in_specs=[SMEM] +...]
    ppermute x12 -> x13, starting transfers between devices: 23.9 us -> 26.9 us  [hop(): return lax.ppermute(value, ('c', axis) if inner else (axis, 'c'), pairs)]
    ppermute x12 -> x13, waiting for transfers between devices: 23 us -> 21.7 us  [hop(): return lax.ppermute(value, ('c', axis) if inner else (axis, 'c'), pairs)]
  transfers between devices with their start and end apart: 19 -> 20, of which waited for: 11 -> 9; matrix products, arithmetic and copies ran while one was open for 2% -> 2% of each run, Pallas kernels for 10% -> 14%
where the time goes in v3:
time: 76.7 us; the launch traced here: 76.6 us
  starting transfers between devices  32.3 us (42%)
  waiting for transfers between devices  23.5 us (31%)
  Pallas kernels  17.6 us (23%)
  other arithmetic  1.6 us (2%)
  local copies, waits for them, and re-layouts  0.84 us (1%)
    ppermute x13, starting transfers between devices, hop(): return lax.ppermute(value, ('c', axis) if inner else (axis, 'c'), pairs)  26.9 us
    ppermute x13, waiting for transfers between devices, hop(): return lax.ppermute(value, ('c', axis) if inner else (axis, 'c'), pairs)  21.7 us
    ppermute x7, starting transfers between devices, swap(): return lax.ppermute(value, 'c', [(0, 1), (1, 0)])  5.46 us
    pallas_call x1, Pallas kernels, passage_grad(): pl.pallas_call(passage_body, in_specs=[SMEM] + [VMEM] * 2 + [HBM] * 2, ou...  4.55 us
    pallas_call x1, Pallas kernels, attend(): pl.pallas_call(lambda *refs: attend_body(group, *refs), in_specs=[SMEM] +...  3.42 us
    pallas_call x2, Pallas kernels, project(): pl.pallas_call(project_body, in_specs=[VMEM] * 4, out_specs=[VMEM] * 2, o...  2.49 us
    pallas_call x1, Pallas kernels, load(): pl.pallas_call(load_body, in_specs=[HBM] * len(arrays), out_specs=[VMEM]...  2.24 us
    pallas_call x1, Pallas kernels, weight_split(): pl.pallas_call(split_body, in_specs=[SMEM] + [VMEM] * 6, out_specs=[VMEM]...  1.9 us
  transfers between devices with their start and end apart: 20, of which 9 were waited for; matrix products, arithmetic and copies ran while one was open for 2% of the time, Pallas kernels for 14%

profile of v3, /device:TPU:1, one launch (start us, length us, event | category | flops | bytes accessed | tf_op | source)
XLA Modules:
  0.0 76.6 jit_solution(3814250018010790291)
XLA Ops:
  0.6 3.7 %collective-permute-start.2 = (bf16[2,2,32,896]{3,2,1,0:T(8,128)(2,1)}, bf16[2,2,32,896]{3,2,1,0:T(8,128)(2,1)S(1)}, u32[]{:S(2)}, u32[]{:S(2)}) collective-permute-start(bf16[2,2,32,896]{3,2,1,0:T(8,128)(2,1)} %refs_4_), channel_id=1, source_target_pairs={{0,2},{1,3},{2,0},{3,1},{4,6},{5,7},{6,4},{7,5},{8,10},{9,11},{10,... | collective-permute-start | bytes 688136 | tf_op jit(solution)/shard_map/ppermute | solution.py:49
  4.3 0.3 collective-permute-start.1
  4.6 2.4 %collective-permute-start = (bf16[2,2,32,896]{3,2,1,0:T(8,128)(2,1)}, bf16[2,2,32,896]{3,2,1,0:T(8,128)(2,1)S(1)}, u32[]{:S(2)}, u32[]{:S(2)}) collective-permute-start(bf16[2,2,32,896]{3,2,1,0:T(8,128)(2,1)} %refs_4_), channel_id=1, source_target_pairs={{0,1},{1,2},{2,3},{3,0},{4,7},{5,4},{6,5},{7,6},{8,9},{9,10},{10,1... | collective-permute-start | bytes 688136 | tf_op jit(solution)/shard_map/ppermute | solution.py:49
  7.3 0.8 reshape.19
  8.2 2.2 %shard_map.101 = (bf16[896,1024]{1,0:T(8,128)(2,1)S(1)}, bf16[896,1024]{1,0:T(8,128)(2,1)S(1)}, bf16[128,1024]{1,0:T(8,128)(2,1)S(1)}, bf16[128,1024]{1,0:T(8,128)(2,1)S(1)}, bf16[2,2,32,896]{3,2,1,0:T(8,128)(2,1)S(1)}) custom-call(bf16[896,1024]{1,0:T(8,128)(2,1)} %key_hbm.1, bf16[896,1024]{1,0:T(8,128)(2,1)} %value_hbm.1, bf16[128,1024]{1,0:T(8,128)(2,1)} %refs_2_.1, ...), custom_call_target="tpu_custom_call" | custom-call | tf_op jit(solution)/shard_map/pallas_call | solution.py:104
  10.5 3.2 %collective-permute-start.4 = (bf16[2,2,32,896]{3,2,1,0:T(8,128)(2,1)S(1)}, bf16[2,2,32,896]{3,2,1,0:T(8,128)(2,1)S(1)}, u32[]{:S(2)}, u32[]{:S(2)}) collective-permute-start(bf16[2,2,32,896]{3,2,1,0:T(8,128)(2,1)S(1)} %collective-permute-done.2.b.a1), channel_id=1, source_target_pairs={{0,4},{4,0},{1,5},{5,1},{2,6},{6,2},{3,7},{7,3},{8,12},{12,8},{9,1... | collective-permute-start | bytes 688136 | tf_op jit(solution)/shard_map/ppermute | solution.py:53
  13.6 1.2 %shard_map.102 = (bf16[2,128,1024]{2,1,0:T(8,128)(2,1)S(1)}, bf16[2,128,1024]{2,1,0:T(8,128)(2,1)S(1)}) custom-call(bf16[2,2,32,896]{3,2,1,0:T(8,128)(2,1)S(1)} %get-tuple-element.71.a.a0, bf16[2,2,32,896]{3,2,1,0:T(8,128)(2,1)S(1)} %collective-permute-done.2.b.a1, bf16[896,1024]{1,0:T(8,128)(2,1)S(1)} %get-tuple-element.73.key_w, ...), custom_call_target="tpu_custom_call" | custom-call | tf_op jit(solution)/shard_map/pallas_call | solution.py:127
  15.0 1.4 %collective-permute-start.5 = (bf16[2,2,32,896]{3,2,1,0:T(8,128)(2,1)S(1)}, bf16[2,2,32,896]{3,2,1,0:T(8,128)(2,1)S(1)}, u32[]{:S(2)}, u32[]{:S(2)}) collective-permute-start(bf16[2,2,32,896]{3,2,1,0:T(8,128)(2,1)S(1)} %collective-permute-done.a.a2), channel_id=1, source_target_pairs={{0,4},{4,0},{1,5},{5,1},{2,6},{6,2},{3,7},{7,3},{8,12},{12,8},{9,1... | collective-permute-start | bytes 688136 | tf_op jit(solution)/shard_map/ppermute | solution.py:53
  16.5 1.2 %shard_map.103 = (bf16[2,128,1024]{2,1,0:T(8,128)(2,1)S(1)}, bf16[2,128,1024]{2,1,0:T(8,128)(2,1)S(1)}) custom-call(bf16[2,2,32,896]{3,2,1,0:T(8,128)(2,1)S(1)} %collective-permute-done.a.a2, bf16[2,2,32,896]{3,2,1,0:T(8,128)(2,1)S(1)} %collective-permute-done.1.b.a3, bf16[896,1024]{1,0:T(8,128)(2,1)S(1)} %get-tuple-element.73.key_w, ...), custom_call_target="tpu_custom_call" | custom-call | tf_op jit(solution)/shard_map/pallas_call | solution.py:127
  17.9 3.4 %shard_map.104 = (bf16[128,1024]{1,0:T(8,128)(2,1)}, bf16[128,1024]{1,0:T(8,128)(2,1)}, bf16[512,1024]{1,0:T(8,128)(2,1)S(1)}, bf16[512,1024]{1,0:T(8,128)(2,1)S(1)}) custom-call(s32[5]{0:T(128)S(1)} %pad_add_fusion.refs_0_.flags, bf16[2,128,1024]{2,1,0:T(8,128)(2,1)S(1)} %get-tuple-element.77.refs_1_, bf16[2,128,1024]{2,1,0:T(8,128)(2,1)S(1)} %get-tuple-element.78.refs_2_, ...), custom_call_target="tpu_custom_call" | custom-call | tf_op jit(solution)/shard_map/pallas_call | solution.py:174
  21.3 0.3 collective-permute-start.7
  21.6 1.1 %shard_map.105.partial = f32[896,1024]{1,0:T(8,128)S(1)} custom-call(bf16[2,2,32,896]{3,2,1,0:T(8,128)(2,1)S(1)} %get-tuple-element.71.a.a0, bf16[2,2,32,896]{3,2,1,0:T(8,128)(2,1)S(1)} %collective-permute-done.2.b.a1, bf16[2,2,32,896]{3,2,1,0:T(8,128)(2,1)S(1)} %collective-permute-done.a.a2, bf16[2,2,32,896]{3,2,1,0:T(8,128)(2,1)S(1)} %collective-permute-done.1.b.a3, ...), custom_call_target="tpu_custom_call" | custom-call | flops 2000000000 | bytes 5000000 | tf_op jit(solution)/shard_map/pallas_call | solution.py:237
  22.8 1.2 %collective-permute-done.7.grads = bf16[512,1024]{1,0:T(8,128)(2,1)S(1)} collective-permute-done((bf16[512,1024]{1,0:T(8,128)(2,1)S(1)}, bf16[512,1024]{1,0:T(8,128)(2,1)S(1)}, u32[]{:S(2)}, u32[]{:S(2)}) %collective-permute-start.7) | collective-permute-done | bytes 1048608 | tf_op jit(solution)/shard_map/ppermute | solution.py:53
  24.0 1.9 %shard_map.106 = (f32[224,1024]{1,0:T(8,128)S(1)}, bf16[224,1024]{1,0:T(8,128)(2,1)S(1)}, bf16[224,1024]{1,0:T(8,128)(2,1)S(1)}, f32[224,1024]{1,0:T(8,128)S(1)}) custom-call(s32[6]{0:T(128)S(1)} %stack.24.place, bf16[2,2,32,896]{3,2,1,0:T(8,128)(2,1)S(1)} %collective-permute-done.3.a0, bf16[2,2,32,896]{3,2,1,0:T(8,128)(2,1)S(1)} %collective-permute-done.4.a1, ...), custom_call_target="tpu_custom_call" | custom-call | flops 2000000000 | bytes 5000000 | tf_op jit(solution)/shard_map/pallas_call | solution.py:261
  25.9 2.8 %collective-permute-start.8 = (bf16[224,1024]{1,0:T(8,128)(2,1)S(1)}, bf16[224,1024]{1,0:T(8,128)(2,1)S(1)}, u32[]{:S(2)}, u32[]{:S(2)}) collective-permute-start(bf16[224,1024]{1,0:T(8,128)(2,1)S(1)} %get-tuple-element.104), channel_id=1, source_target_pairs={{0,64},{64,128},{128,192},{192,0},{4,196},{68,4},{132,68},{196,132... | collective-permute-start | bytes 1376264 | tf_op jit(solution)/shard_map/ppermute | solution.py:49
  28.7 4.5 %shard_map.107 = (f32[2,2,32,896]{3,2,1,0:T(8,128)S(1)}, bf16[2,2,32,896]{3,2,1,0:T(8,128)(2,1)S(1)}, bf16[2,2,32,896]{3,2,1,0:T(8,128)(2,1)S(1)}, f32[2,2,32,896]{3,2,1,0:T(8,128)S(1)}) custom-call(s32[5]{0:T(128)S(1)} %pad_add_fusion.refs_0_.flags, bf16[512,1024]{1,0:T(8,128)(2,1)S(1)} %get-tuple-element.100.grads.keep, ...), custom_call_target="tpu_custom_call" | custom-call | flops 4000000000 | bytes 10000000 | tf_op jit(solution)/shard_map/pallas_call | solution.py:214
  33.2 4.7 %collective-permute-done.8.b = bf16[224,1024]{1,0:T(8,128)(2,1)S(1)} collective-permute-done((bf16[224,1024]{1,0:T(8,128)(2,1)S(1)}, bf16[224,1024]{1,0:T(8,128)(2,1)S(1)}, u32[]{:S(2)}, u32[]{:S(2)}) %collective-permute-start.8) | collective-permute-done | bytes 458784 | tf_op jit(solution)/shard_map/ppermute | solution.py:49
  38.0 2.2 %collective-permute-done.9.d = bf16[224,1024]{1,0:T(8,128)(2,1)S(1)} collective-permute-done((bf16[224,1024]{1,0:T(8,128)(2,1)S(1)}, bf16[224,1024]{1,0:T(8,128)(2,1)S(1)}, u32[]{:S(2)}, u32[]{:S(2)}) %collective-permute-start.9) | collective-permute-done | bytes 458784 | tf_op jit(solution)/shard_map/ppermute | solution.py:49
  40.2 1.0 %shard_map.108 = (bf16[5,32,1024]{2,1,0:T(8,128)(2,1)S(1)}, bf16[3,32,1024]{2,1,0:T(8,128)(2,1)S(1)}, f32[5,32,1024]{2,1,0:T(8,128)S(1)}, f32[3,32,1024]{2,1,0:T(8,128)S(1)}) custom-call(s32[6]{0:T(128)S(1)} %stack.24.place, f32[224,1024]{1,0:T(8,128)S(1)} %get-tuple-element.103.a, bf16[224,1024]{1,0:T(8,128)(2,1)S(1)} %collective-permute-done.8.b, ...), custom_call_target="tpu_custom_call" | custom-call | tf_op jit(solution)/shard_map/pallas_call | solution.py:316
  41.3 2.6 %collective-permute-start.10 = (bf16[5,32,1024]{2,1,0:T(8,128)(2,1)S(1)}, bf16[5,32,1024]{2,1,0:T(8,128)(2,1)S(1)}, u32[]{:S(2)}, u32[]{:S(2)}) collective-permute-start(bf16[5,32,1024]{2,1,0:T(8,128)(2,1)S(1)} %get-tuple-element.113), channel_id=1, source_target_pairs={{0,64},{64,128},{128,192},{192,0},{4,196},{68,4},{132,68},{196,132... | collective-permute-start | bytes 983048 | tf_op jit(solution)/shard_map/ppermute | solution.py:49
  43.9 2.4 %collective-permute-start.12 = (bf16[2,2,32,896]{3,2,1,0:T(8,128)(2,1)S(1)}, bf16[2,2,32,896]{3,2,1,0:T(8,128)(2,1)S(1)}, u32[]{:S(2)}, u32[]{:S(2)}) collective-permute-start(bf16[2,2,32,896]{3,2,1,0:T(8,128)(2,1)S(1)} %get-tuple-element.115), channel_id=1, source_target_pairs={{0,1},{1,2},{2,3},{3,0},{4,7},{5,4},{6,5},{7,6},{8,9},{9,10},{10,1... | collective-permute-start | bytes 688136 | tf_op jit(solution)/shard_map/ppermute | solution.py:49
  46.3 6.3 %collective-permute-done.11.front_cross = bf16[3,32,1024]{2,1,0:T(8,128)(2,1)S(1)} collective-permute-done((bf16[3,32,1024]{2,1,0:T(8,128)(2,1)S(1)}, bf16[3,32,1024]{2,1,0:T(8,128)(2,1)S(1)}, u32[]{:S(2)}, u32[]{:S(2)}) %collective-permute-start.11) | collective-permute-done | bytes 196640 | tf_op jit(solution)/shard_map/ppermute | solution.py:49
  52.7 5.6 %collective-permute-start.14 = (bf16[3,32,1024]{2,1,0:T(8,128)(2,1)S(1)}, bf16[3,32,1024]{2,1,0:T(8,128)(2,1)S(1)}, u32[]{:S(2)}, u32[]{:S(2)}) collective-permute-start(bf16[3,32,1024]{2,1,0:T(8,128)(2,1)S(1)} %get-tuple-element.120), channel_id=1, source_target_pairs={{0,8},{8,16},{16,24},{24,32},{32,40},{40,48},{48,56},{56,0},{4,60}... | collective-permute-start | bytes 589832 | tf_op jit(solution)/shard_map/ppermute | solution.py:49
  58.5 2.7 %collective-permute-start.17 = (bf16[2,2,32,896]{3,2,1,0:T(8,128)(2,1)S(1)}, bf16[2,2,32,896]{3,2,1,0:T(8,128)(2,1)S(1)}, u32[]{:S(2)}, u32[]{:S(2)}) collective-permute-start(bf16[2,2,32,896]{3,2,1,0:T(8,128)(2,1)S(1)} %shard_map.111), channel_id=1, source_target_pairs={{0,1},{1,2},{2,3},{3,0},{4,7},{5,4},{6,5},{7,6},{8,9},{9,10},{10,1... | collective-permute-start | bytes 688136 | tf_op jit(solution)/shard_map/ppermute | solution.py:49
  61.2 2.8 %collective-permute-start.15 = (bf16[2,32,1024]{2,1,0:T(8,128)(2,1)S(1)}, bf16[2,32,1024]{2,1,0:T(8,128)(2,1)S(1)}, u32[]{:S(2)}, u32[]{:S(2)}) collective-permute-start(bf16[2,32,1024]{2,1,0:T(8,128)(2,1)S(1)} %shard_map.110), channel_id=1, source_target_pairs={{0,24},{8,32},{16,40},{24,48},{32,56},{40,0},{48,8},{56,16},{4,44}... | collective-permute-start | bytes 393224 | tf_op jit(solution)/shard_map/ppermute | solution.py:49
  64.0 1.6 %collective-permute-start.18 = (bf16[2,32,1024]{2,1,0:T(8,128)(2,1)S(1)}, bf16[2,32,1024]{2,1,0:T(8,128)(2,1)S(1)}, u32[]{:S(2)}, u32[]{:S(2)}) collective-permute-start(bf16[2,32,1024]{2,1,0:T(8,128)(2,1)S(1)} %get-tuple-element.127), channel_id=1, source_target_pairs={{0,16},{8,24},{16,32},{24,40},{32,48},{40,56},{48,0},{56,8},{4,52}... | collective-permute-start | bytes 393224 | tf_op jit(solution)/shard_map/ppermute | solution.py:49
  65.5 4.5 %collective-permute-done.15.three = bf16[2,32,1024]{2,1,0:T(8,128)(2,1)S(1)} collective-permute-done((bf16[2,32,1024]{2,1,0:T(8,128)(2,1)S(1)}, bf16[2,32,1024]{2,1,0:T(8,128)(2,1)S(1)}, u32[]{:S(2)}, u32[]{:S(2)}) %collective-permute-start.15) | collective-permute-done | bytes 131104 | tf_op jit(solution)/shard_map/ppermute | solution.py:49
  70.0 3.8 %collective-permute-done.18.two = bf16[2,32,1024]{2,1,0:T(8,128)(2,1)S(1)} collective-permute-done((bf16[2,32,1024]{2,1,0:T(8,128)(2,1)S(1)}, bf16[2,32,1024]{2,1,0:T(8,128)(2,1)S(1)}, u32[]{:S(2)}, u32[]{:S(2)}) %collective-permute-start.18) | collective-permute-done | bytes 131104 | tf_op jit(solution)/shard_map/ppermute | solution.py:49
  73.8 0.6 shard_map.112
  74.5 0.8 %convert_add_fusion = f32[2,2,32,896]{3,2,1,0:T(8,128)} fusion(bf16[2,2,32,896]{3,2,1,0:T(8,128)(2,1)S(1)} %collective-permute-done.17, f32[2,2,32,896]{3,2,1,0:T(8,128)S(1)} %get-tuple-element.102, bf16[2,2,32,896]{3,2,1,0:T(8,128)(2,1)S(1)} %collective-permute-done.16), kind=kLoop, calls=%fused_computation | loop fusion | flops 458752 | bytes 1376256 | tf_op jit(solution)/shard_map/add | solution.py:445
  75.4 0.5 collective-permute-done.19
  75.9 0.7 select_bitcast_fusion
  (25 shorter events, 1.3 us)
Async XLA Ops:
  0.6 9.8 %collective-permute-start.2 = (bf16[2,2,32,896]{3,2,1,0:T(8,128)(2,1)}, bf16[2,2,32,896]{3,2,1,0:T(8,128)(2,1)S(1)}, u32[]{:S(2)}, u32[]{:S(2)}) collective-permute-start(bf16[2,2,32,896]{3,2,1,0:T(8,128)(2,1)} %refs_4_), channel_id=1, source_target_pairs={{0,2},{1,3},{2,0},{3,1},{4,6},{5,7},{6,4},{7,5},{8,10},{9,11},{10,... | collective-permute-start | bytes 688136 | tf_op jit(solution)/shard_map/ppermute | solution.py:49
  4.3 10.6 %collective-permute-start.1 = (bf16[2,2,32,896]{3,2,1,0:T(8,128)(2,1)}, bf16[2,2,32,896]{3,2,1,0:T(8,128)(2,1)S(1)}, u32[]{:S(2)}, u32[]{:S(2)}) collective-permute-start(bf16[2,2,32,896]{3,2,1,0:T(8,128)(2,1)} %refs_4_), channel_id=1, source_target_pairs={{0,3},{1,0},{2,1},{3,2},{4,5},{5,6},{6,7},{7,4},{8,11},{9,8},{10,9... | collective-permute-start | bytes 688136 | tf_op jit(solution)/shard_map/ppermute | solution.py:49
  4.6 10.4 %collective-permute-start = (bf16[2,2,32,896]{3,2,1,0:T(8,128)(2,1)}, bf16[2,2,32,896]{3,2,1,0:T(8,128)(2,1)S(1)}, u32[]{:S(2)}, u32[]{:S(2)}) collective-permute-start(bf16[2,2,32,896]{3,2,1,0:T(8,128)(2,1)} %refs_4_), channel_id=1, source_target_pairs={{0,1},{1,2},{2,3},{3,0},{4,7},{5,4},{6,5},{7,6},{8,9},{9,10},{10,1... | collective-permute-start | bytes 688136 | tf_op jit(solution)/shard_map/ppermute | solution.py:49
  7.0 8.0 %collective-permute-start.3 = (bf16[2,2,32,896]{3,2,1,0:T(8,128)(2,1)}, bf16[2,2,32,896]{3,2,1,0:T(8,128)(2,1)S(1)}, u32[]{:S(2)}, u32[]{:S(2)}) collective-permute-start(bf16[2,2,32,896]{3,2,1,0:T(8,128)(2,1)} %refs_4_), channel_id=1, source_target_pairs={{0,4},{4,0},{1,5},{5,1},{2,6},{6,2},{3,7},{7,3},{8,12},{12,8},{9,1... | collective-permute-start | bytes 688136 | tf_op jit(solution)/shard_map/ppermute | solution.py:53
  10.5 4.6 %collective-permute-start.4 = (bf16[2,2,32,896]{3,2,1,0:T(8,128)(2,1)S(1)}, bf16[2,2,32,896]{3,2,1,0:T(8,128)(2,1)S(1)}, u32[]{:S(2)}, u32[]{:S(2)}) collective-permute-start(bf16[2,2,32,896]{3,2,1,0:T(8,128)(2,1)S(1)} %collective-permute-done.2.b.a1), channel_id=1, source_target_pairs={{0,4},{4,0},{1,5},{5,1},{2,6},{6,2},{3,7},{7,3},{8,12},{12,8},{9,1... | collective-permute-start | bytes 688136 | tf_op jit(solution)/shard_map/ppermute | solution.py:53
  15.0 2.7 %collective-permute-start.5 = (bf16[2,2,32,896]{3,2,1,0:T(8,128)(2,1)S(1)}, bf16[2,2,32,896]{3,2,1,0:T(8,128)(2,1)S(1)}, u32[]{:S(2)}, u32[]{:S(2)}) collective-permute-start(bf16[2,2,32,896]{3,2,1,0:T(8,128)(2,1)S(1)} %collective-permute-done.a.a2), channel_id=1, source_target_pairs={{0,4},{4,0},{1,5},{5,1},{2,6},{6,2},{3,7},{7,3},{8,12},{12,8},{9,1... | collective-permute-start | bytes 688136 | tf_op jit(solution)/shard_map/ppermute | solution.py:53
  16.4 1.5 %collective-permute-start.6 = (bf16[2,2,32,896]{3,2,1,0:T(8,128)(2,1)S(1)}, bf16[2,2,32,896]{3,2,1,0:T(8,128)(2,1)S(1)}, u32[]{:S(2)}, u32[]{:S(2)}) collective-permute-start(bf16[2,2,32,896]{3,2,1,0:T(8,128)(2,1)S(1)} %collective-permute-done.1.b.a3), channel_id=1, source_target_pairs={{0,4},{4,0},{1,5},{5,1},{2,6},{6,2},{3,7},{7,3},{8,12},{12,8},{9,1... | collective-permute-start | bytes 688136 | tf_op jit(solution)/shard_map/ppermute | solution.py:53
  21.3 2.7 %collective-permute-start.7 = (bf16[512,1024]{1,0:T(8,128)(2,1)S(1)}, bf16[512,1024]{1,0:T(8,128)(2,1)S(1)}, u32[]{:S(2)}, u32[]{:S(2)}) collective-permute-start(bf16[512,1024]{1,0:T(8,128)(2,1)S(1)} %get-tuple-element.101.send), channel_id=1, source_target_pairs={{0,4},{4,0},{1,5},{5,1},{2,6},{6,2},{3,7},{7,3},{8,12},{12,8},{9,1... | collective-permute-start | bytes 3145736 | tf_op jit(solution)/shard_map/ppermute | solution.py:53
  25.9 12.1 %collective-permute-start.8 = (bf16[224,1024]{1,0:T(8,128)(2,1)S(1)}, bf16[224,1024]{1,0:T(8,128)(2,1)S(1)}, u32[]{:S(2)}, u32[]{:S(2)}) collective-permute-start(bf16[224,1024]{1,0:T(8,128)(2,1)S(1)} %get-tuple-element.104), channel_id=1, source_target_pairs={{0,64},{64,128},{128,192},{192,0},{4,196},{68,4},{132,68},{196,132... | collective-permute-start | bytes 1376264 | tf_op jit(solution)/shard_map/ppermute | solution.py:49
  28.7 11.5 %collective-permute-start.9 = (bf16[224,1024]{1,0:T(8,128)(2,1)S(1)}, bf16[224,1024]{1,0:T(8,128)(2,1)S(1)}, u32[]{:S(2)}, u32[]{:S(2)}) collective-permute-start(bf16[224,1024]{1,0:T(8,128)(2,1)S(1)} %get-tuple-element.105), channel_id=1, source_target_pairs={{0,192},{64,0},{128,64},{192,128},{4,68},{68,132},{132,196},{196,4... | collective-permute-start | bytes 1376264 | tf_op jit(solution)/shard_map/ppermute | solution.py:49
  41.2 11.4 %collective-permute-start.13 = (f32[3,32,1024]{2,1,0:T(8,128)S(1)}, f32[3,32,1024]{2,1,0:T(8,128)S(1)}, u32[]{:S(2)}, u32[]{:S(2)}) collective-permute-start(f32[3,32,1024]{2,1,0:T(8,128)S(1)} %get-tuple-element.117), channel_id=1, source_target_pairs={{0,4},{4,0},{1,5},{5,1},{2,6},{6,2},{3,7},{7,3},{8,12},{12,8},{9,1... | collective-permute-start | bytes 1179656 | tf_op jit(solution)/shard_map/ppermute | solution.py:53
  41.3 11.3 %collective-permute-start.10 = (bf16[5,32,1024]{2,1,0:T(8,128)(2,1)S(1)}, bf16[5,32,1024]{2,1,0:T(8,128)(2,1)S(1)}, u32[]{:S(2)}, u32[]{:S(2)}) collective-permute-start(bf16[5,32,1024]{2,1,0:T(8,128)(2,1)S(1)} %get-tuple-element.113), channel_id=1, source_target_pairs={{0,64},{64,128},{128,192},{192,0},{4,196},{68,4},{132,68},{196,132... | collective-permute-start | bytes 983048 | tf_op jit(solution)/shard_map/ppermute | solution.py:49
  43.9 8.7 %collective-permute-start.12 = (bf16[2,2,32,896]{3,2,1,0:T(8,128)(2,1)S(1)}, bf16[2,2,32,896]{3,2,1,0:T(8,128)(2,1)S(1)}, u32[]{:S(2)}, u32[]{:S(2)}) collective-permute-start(bf16[2,2,32,896]{3,2,1,0:T(8,128)(2,1)S(1)} %get-tuple-element.115), channel_id=1, source_target_pairs={{0,1},{1,2},{2,3},{3,0},{4,7},{5,4},{6,5},{7,6},{8,9},{9,10},{10,1... | collective-permute-start | bytes 688136 | tf_op jit(solution)/shard_map/ppermute | solution.py:49
  46.3 6.3 %collective-permute-start.11 = (bf16[3,32,1024]{2,1,0:T(8,128)(2,1)S(1)}, bf16[3,32,1024]{2,1,0:T(8,128)(2,1)S(1)}, u32[]{:S(2)}, u32[]{:S(2)}) collective-permute-start(bf16[3,32,1024]{2,1,0:T(8,128)(2,1)S(1)} %get-tuple-element.114), channel_id=1, source_target_pairs={{0,68},{64,132},{128,196},{192,4},{4,192},{68,0},{132,64},{196,128... | collective-permute-start | bytes 589832 | tf_op jit(solution)/shard_map/ppermute | solution.py:49
  52.7 8.5 %collective-permute-start.14 = (bf16[3,32,1024]{2,1,0:T(8,128)(2,1)S(1)}, bf16[3,32,1024]{2,1,0:T(8,128)(2,1)S(1)}, u32[]{:S(2)}, u32[]{:S(2)}) collective-permute-start(bf16[3,32,1024]{2,1,0:T(8,128)(2,1)S(1)} %get-tuple-element.120), channel_id=1, source_target_pairs={{0,8},{8,16},{16,24},{24,32},{32,40},{40,48},{48,56},{56,0},{4,60}... | collective-permute-start | bytes 589832 | tf_op jit(solution)/shard_map/ppermute | solution.py:49
  58.4 7.2 %collective-permute-start.16 = (bf16[2,2,32,896]{3,2,1,0:T(8,128)(2,1)S(1)}, bf16[2,2,32,896]{3,2,1,0:T(8,128)(2,1)S(1)}, u32[]{:S(2)}, u32[]{:S(2)}) collective-permute-start(bf16[2,2,32,896]{3,2,1,0:T(8,128)(2,1)S(1)} %get-tuple-element.121), channel_id=1, source_target_pairs={{0,3},{1,0},{2,1},{3,2},{4,5},{5,6},{6,7},{7,4},{8,11},{9,8},{10,9... | collective-permute-start | bytes 688136 | tf_op jit(solution)/shard_map/ppermute | solution.py:49
  58.5 7.1 %collective-permute-start.17 = (bf16[2,2,32,896]{3,2,1,0:T(8,128)(2,1)S(1)}, bf16[2,2,32,896]{3,2,1,0:T(8,128)(2,1)S(1)}, u32[]{:S(2)}, u32[]{:S(2)}) collective-permute-start(bf16[2,2,32,896]{3,2,1,0:T(8,128)(2,1)S(1)} %shard_map.111), channel_id=1, source_target_pairs={{0,1},{1,2},{2,3},{3,0},{4,7},{5,4},{6,5},{7,6},{8,9},{9,10},{10,1... | collective-permute-start | bytes 688136 | tf_op jit(solution)/shard_map/ppermute | solution.py:49
  61.2 8.8 %collective-permute-start.15 = (bf16[2,32,1024]{2,1,0:T(8,128)(2,1)S(1)}, bf16[2,32,1024]{2,1,0:T(8,128)(2,1)S(1)}, u32[]{:S(2)}, u32[]{:S(2)}) collective-permute-start(bf16[2,32,1024]{2,1,0:T(8,128)(2,1)S(1)} %shard_map.110), channel_id=1, source_target_pairs={{0,24},{8,32},{16,40},{24,48},{32,56},{40,0},{48,8},{56,16},{4,44}... | collective-permute-start | bytes 393224 | tf_op jit(solution)/shard_map/ppermute | solution.py:49
  64.0 9.8 %collective-permute-start.18 = (bf16[2,32,1024]{2,1,0:T(8,128)(2,1)S(1)}, bf16[2,32,1024]{2,1,0:T(8,128)(2,1)S(1)}, u32[]{:S(2)}, u32[]{:S(2)}) collective-permute-start(bf16[2,32,1024]{2,1,0:T(8,128)(2,1)S(1)} %get-tuple-element.127), channel_id=1, source_target_pairs={{0,16},{8,24},{16,32},{24,40},{32,48},{40,56},{48,0},{56,8},{4,52}... | collective-permute-start | bytes 393224 | tf_op jit(solution)/shard_map/ppermute | solution.py:49
  74.4 1.4 %collective-permute-start.19 = (f32[2,14,1024]{2,1,0:T(8,128)S(1)}, f32[2,14,1024]{2,1,0:T(8,128)S(1)}, u32[]{:S(2)}, u32[]{:S(2)}) collective-permute-start(f32[2,14,1024]{2,1,0:T(8,128)S(1)} %get-tuple-element.130), channel_id=1, source_target_pairs={{0,4},{4,0},{1,5},{5,1},{2,6},{6,2},{3,7},{7,3},{8,12},{12,8},{9,1... | collective-permute-start | bytes 344072 | tf_op jit(solution)/shard_map/ppermute | solution.py:53

commit v4 on v3

--- a/solution.py
+++ b/solution.py
@@ -288,43 +288,39 @@
     )(*near_by(a, b))
 
 
-def deal_body(place, a, b, c, d, front, front_cross, base, base_cross):
+def deal_body(place, a, b, ours, theirs):
     z, core = place[4], place[5]
-    height = a.shape[0] // 8
-    pad = jnp.zeros((PAD - height, a.shape[1]), F32)
     total = a[...] + b[...].astype(F32)
-    rest = c[...] + d[...].astype(F32)
+    height = total.shape[0] // 8
+    pad = jnp.zeros((PAD - height, total.shape[1]), F32)
     for j in range(8):
-        rows = slice(j * height, (j + 1) * height)
-        one = jnp.concatenate([total[rows], pad], axis=0).astype(BF)
-        two = jnp.concatenate([rest[rows], pad], axis=0)
+        piece = jnp.concatenate([total[j * height : (j + 1) * height], pad], axis=0)
         slot = lax.rem(jnp.where(core == 0, j - z, z - j) + 8, 8)
 
         @pl.when(slot < 5)
         def _():
-            front[slot] = one
-            base[slot] = two
+            ours[slot] = piece.astype(ours.dtype)
 
         @pl.when(slot > 4)
         def _():
-            front_cross[7 - slot] = one
-            base_cross[7 - slot] = two
-
-
-def deal(place, front, far_in, mine, back_in):
-    width = mine.shape[1]
+            theirs[7 - slot] = piece.astype(theirs.dtype)
+
+
+def deal(place, a, b, dtype):
+    width = a.shape[1]
     return pl.pallas_call(
         deal_body,
-        in_specs=[SMEM] + [VMEM] * 4,
-        out_specs=[VMEM] * 4,
-        out_shape=[shape((n, PAD, width), dtype) for dtype in (BF, F32) for n in (5, 3)],
-        compiler_params=params(),
-    )(place, *near_by(front, far_in, mine, back_in))
+        in_specs=[SMEM] + [VMEM] * 2,
+        out_specs=[VMEM] * 2,
+        out_shape=[shape((5, PAD, width), dtype), shape((3, PAD, width), BF)],
+        compiler_params=params(),
+        cost_estimate=cost(0, 0),
+    )(place, *near_by(a, b))
 
 
 def fold_body(base, front, cross, front_cross, own, one, two, three):
     height = own.shape[0]
-    add_up = lambda a, b, i: a[i] + b[i].astype(F32)
+    add_up = lambda a, b, i: a[i].astype(F32) + b[i].astype(F32)
     own[...] = add_up(base, front, 0)[:height]
     one[0] = add_up(base, front, 1).astype(BF)
     one[1] = add_up(base, front, 4).astype(BF)
@@ -389,6 +385,7 @@
         out_specs=[VMEM] * 2,
         out_shape=[shape(dims, F32)] * 2,
         compiler_params=params(),
+        cost_estimate=pl.CostEstimate(flops=2 * 10**10, bytes_accessed=4 * 10**7, transcendentals=0),
     )(place, *near_by(own, one, two, three))
 
 
@@ -422,22 +419,23 @@
     far_in = hop(far, "y", ny, 1)
     keep, send, front = tie((keep, send, front))
     p0, p3, p1, p2 = passage_grad(flags, keep, send, key_weight, value_weight, own.shape)
+    back, p1, p2, p3 = tie((back, p1, p2, p3))
     back_in = hop(back, "y", ny, -1)
-    far_in, back_in, p1, p2, p3 = tie((far_in, back_in, p1, p2, p3))
-    front, front_cross, base, cross = deal(place, front, far_in, mine, back_in)
+    front, front_cross = deal(place, front, far_in, BF)
+    front, front_cross, mine = tie((front, front_cross, mine))
     front_in = hop(front, "y", ny, 1)
     cross_in = hop(front_cross, "y", ny, 1, cross=True)
+    base, cross = deal(place, mine, back_in, F32)
     cross = swap(cross)
     front_in, cross_in, beyond = tie((front_in, cross_in, hop(p3, "x", nx, 1)))
-    p1_in = hop(p1, "x", nx, -1)
 
     here, one, two, three = fold(base, front_in, cross, cross_in, mine.shape[0] // nz)
     one_in = hop(one, "z", nz, 1)
     two_in = hop(two, "z", nz, 2)
-    three_in = hop(relay(three, one_in), "z", nz, 3)
     share = add(p2, beyond)
-    returned = [p1_in, hop(share, "x", nx, 1)]
-    three_in, returned = tie((three_in, returned))
+    three, share, p1 = tie((relay(three, one_in), share, p1))
+    three_in = hop(three, "z", nz, 3)
+    returned = [hop(p1, "x", nx, -1), hop(share, "x", nx, 1)]
     stay, give = finish(place, here, one_in, two_in, three_in)
     other = swap(give)
     neighbour_grad = p0

time: 76.7 us -> 70.3 us (0.917)
  the two profiles are of different devices: /device:TPU:1 before, /device:TPU:40 now
where the time goes in v4:
time: 70.3 us; the launch traced here: 70.2 us
  starting transfers between devices  28.6 us (41%)
  waiting for transfers between devices  20.3 us (29%)
  Pallas kernels  18.1 us (26%)
  other arithmetic  1.58 us (2%)
  local copies, waits for them, and re-layouts  0.84 us (1%)
  between operations  0.77 us (1%)
    ppermute x13, starting transfers between devices, hop(): return lax.ppermute(value, ('c', axis) if inner else (axis, 'c'), pairs)  27.4 us
    ppermute x13, waiting for transfers between devices, hop(): return lax.ppermute(value, ('c', axis) if inner else (axis, 'c'), pairs)  18.9 us
    pallas_call x1, Pallas kernels, passage_grad(): pl.pallas_call(passage_body, in_specs=[SMEM] + [VMEM] * 2 + [HBM] * 2, ou...  4.55 us
    pallas_call x1, Pallas kernels, attend(): pl.pallas_call(lambda *refs: attend_body(group, *refs), in_specs=[SMEM] +...  3.42 us
    pallas_call x2, Pallas kernels, project(): pl.pallas_call(project_body, in_specs=[VMEM] * 4, out_specs=[VMEM] * 2, o...  2.49 us
    pallas_call x1, Pallas kernels, load(): pl.pallas_call(load_body, in_specs=[HBM] * len(arrays), out_specs=[VMEM]...  2.24 us
    pallas_call x1, Pallas kernels, weight_split(): pl.pallas_call(split_body, in_specs=[SMEM] + [VMEM] * 6, out_specs=[VMEM]...  1.9 us
    pallas_call x2, Pallas kernels, deal(): pl.pallas_call(deal_body, in_specs=[SMEM] + [VMEM] * 2, out_specs=[VMEM]...  1.59 us
  transfers between devices with their start and end apart: 20, of which 10 were waited for; matrix products, arithmetic and copies ran while one was open for 2% of the time, Pallas kernels for 18%

profile of v4, /device:TPU:40, one launch (start us, length us, event | category | flops | bytes accessed | tf_op | source)
XLA Modules:
  0.0 70.2 jit_solution(928433486221249098)
XLA Ops:
  0.6 3.1 %collective-permute-start.2 = (bf16[2,2,32,896]{3,2,1,0:T(8,128)(2,1)}, bf16[2,2,32,896]{3,2,1,0:T(8,128)(2,1)S(1)}, u32[]{:S(2)}, u32[]{:S(2)}) collective-permute-start(bf16[2,2,32,896]{3,2,1,0:T(8,128)(2,1)} %refs_4_), channel_id=1, source_target_pairs={{0,2},{1,3},{2,0},{3,1},{4,6},{5,7},{6,4},{7,5},{8,10},{9,11},{10,... | collective-permute-start | bytes 688136 | tf_op jit(solution)/shard_map/ppermute | solution.py:49
  3.7 1.1 %collective-permute-start.1 = (bf16[2,2,32,896]{3,2,1,0:T(8,128)(2,1)}, bf16[2,2,32,896]{3,2,1,0:T(8,128)(2,1)S(1)}, u32[]{:S(2)}, u32[]{:S(2)}) collective-permute-start(bf16[2,2,32,896]{3,2,1,0:T(8,128)(2,1)} %refs_4_), channel_id=1, source_target_pairs={{0,3},{1,0},{2,1},{3,2},{4,5},{5,6},{6,7},{7,4},{8,11},{9,8},{10,9... | collective-permute-start | bytes 688136 | tf_op jit(solution)/shard_map/ppermute | solution.py:49
  4.9 0.9 %collective-permute-start = (bf16[2,2,32,896]{3,2,1,0:T(8,128)(2,1)}, bf16[2,2,32,896]{3,2,1,0:T(8,128)(2,1)S(1)}, u32[]{:S(2)}, u32[]{:S(2)}) collective-permute-start(bf16[2,2,32,896]{3,2,1,0:T(8,128)(2,1)} %refs_4_), channel_id=1, source_target_pairs={{0,1},{1,2},{2,3},{3,0},{4,7},{5,4},{6,5},{7,6},{8,9},{9,10},{10,1... | collective-permute-start | bytes 688136 | tf_op jit(solution)/shard_map/ppermute | solution.py:49
  6.0 0.8 %reshape.19 = s32[4]{0:T(128)S(1)} reshape(s32[2,2]{1,0:T(2,128)} %param.9) | data formatting | bytes 32 | tf_op jit(solution)/shard_map/reshape | solution.py:398
  6.9 2.2 %shard_map.101 = (bf16[896,1024]{1,0:T(8,128)(2,1)S(1)}, bf16[896,1024]{1,0:T(8,128)(2,1)S(1)}, bf16[128,1024]{1,0:T(8,128)(2,1)S(1)}, bf16[128,1024]{1,0:T(8,128)(2,1)S(1)}, bf16[2,2,32,896]{3,2,1,0:T(8,128)(2,1)S(1)}) custom-call(bf16[896,1024]{1,0:T(8,128)(2,1)} %key_hbm.1, bf16[896,1024]{1,0:T(8,128)(2,1)} %value_hbm.1, bf16[128,1024]{1,0:T(8,128)(2,1)} %refs_2_.1, ...), custom_call_target="tpu_custom_call" | custom-call | tf_op jit(solution)/shard_map/pallas_call | solution.py:104
  9.1 1.8 %collective-permute-done.2.b.a1 = bf16[2,2,32,896]{3,2,1,0:T(8,128)(2,1)S(1)} collective-permute-done((bf16[2,2,32,896]{3,2,1,0:T(8,128)(2,1)}, bf16[2,2,32,896]{3,2,1,0:T(8,128)(2,1)S(1)}, u32[]{:S(2)}, u32[]{:S(2)}) %collective-permute-start.2) | collective-permute-done | bytes 229408 | tf_op jit(solution)/shard_map/ppermute | solution.py:49
  10.9 1.2 %shard_map.102 = (bf16[2,128,1024]{2,1,0:T(8,128)(2,1)S(1)}, bf16[2,128,1024]{2,1,0:T(8,128)(2,1)S(1)}) custom-call(bf16[2,2,32,896]{3,2,1,0:T(8,128)(2,1)S(1)} %get-tuple-element.73.a.a0, bf16[2,2,32,896]{3,2,1,0:T(8,128)(2,1)S(1)} %collective-permute-done.2.b.a1, bf16[896,1024]{1,0:T(8,128)(2,1)S(1)} %get-tuple-element.75.key_w, ...), custom_call_target="tpu_custom_call" | custom-call | tf_op jit(solution)/shard_map/pallas_call | solution.py:127
  12.2 2.6 %collective-permute-done.1.b.a3 = bf16[2,2,32,896]{3,2,1,0:T(8,128)(2,1)S(1)} collective-permute-done((bf16[2,2,32,896]{3,2,1,0:T(8,128)(2,1)}, bf16[2,2,32,896]{3,2,1,0:T(8,128)(2,1)S(1)}, u32[]{:S(2)}, u32[]{:S(2)}) %collective-permute-start.1) | collective-permute-done | bytes 229408 | tf_op jit(solution)/shard_map/ppermute | solution.py:49
  15.4 1.2 %shard_map.103 = (bf16[2,128,1024]{2,1,0:T(8,128)(2,1)S(1)}, bf16[2,128,1024]{2,1,0:T(8,128)(2,1)S(1)}) custom-call(bf16[2,2,32,896]{3,2,1,0:T(8,128)(2,1)S(1)} %collective-permute-done.a.a2, bf16[2,2,32,896]{3,2,1,0:T(8,128)(2,1)S(1)} %collective-permute-done.1.b.a3, bf16[896,1024]{1,0:T(8,128)(2,1)S(1)} %get-tuple-element.75.key_w, ...), custom_call_target="tpu_custom_call" | custom-call | tf_op jit(solution)/shard_map/pallas_call | solution.py:127
  16.7 3.4 %shard_map.104 = (bf16[128,1024]{1,0:T(8,128)(2,1)}, bf16[128,1024]{1,0:T(8,128)(2,1)}, bf16[512,1024]{1,0:T(8,128)(2,1)S(1)}, bf16[512,1024]{1,0:T(8,128)(2,1)S(1)}) custom-call(s32[5]{0:T(128)S(1)} %pad_add_fusion.refs_0_.flags, bf16[2,128,1024]{2,1,0:T(8,128)(2,1)S(1)} %get-tuple-element.79.refs_1_, bf16[2,128,1024]{2,1,0:T(8,128)(2,1)S(1)} %get-tuple-element.80.refs_2_, ...), custom_call_target="tpu_custom_call" | custom-call | tf_op jit(solution)/shard_map/pallas_call | solution.py:174
  20.3 1.1 %shard_map.105.partial = f32[896,1024]{1,0:T(8,128)S(1)} custom-call(bf16[2,2,32,896]{3,2,1,0:T(8,128)(2,1)S(1)} %get-tuple-element.73.a.a0, bf16[2,2,32,896]{3,2,1,0:T(8,128)(2,1)S(1)} %collective-permute-done.2.b.a1, bf16[2,2,32,896]{3,2,1,0:T(8,128)(2,1)S(1)} %collective-permute-done.a.a2, bf16[2,2,32,896]{3,2,1,0:T(8,128)(2,1)S(1)} %collective-permute-done.1.b.a3, ...), custom_call_target="tpu_custom_call" | custom-call | flops 2000000000 | bytes 5000000 | tf_op jit(solution)/shard_map/pallas_call | solution.py:237
  21.5 1.3 %collective-permute-done.7.grads = bf16[512,1024]{1,0:T(8,128)(2,1)S(1)} collective-permute-done((bf16[512,1024]{1,0:T(8,128)(2,1)S(1)}, bf16[512,1024]{1,0:T(8,128)(2,1)S(1)}, u32[]{:S(2)}, u32[]{:S(2)}) %collective-permute-start.7) | collective-permute-done | bytes 1048608 | tf_op jit(solution)/shard_map/ppermute | solution.py:53
  22.8 1.9 %shard_map.106 = (f32[224,1024]{1,0:T(8,128)S(1)}, bf16[224,1024]{1,0:T(8,128)(2,1)S(1)}, bf16[224,1024]{1,0:T(8,128)(2,1)S(1)}, f32[224,1024]{1,0:T(8,128)S(1)}) custom-call(s32[6]{0:T(128)S(1)} %stack.24.place, bf16[2,2,32,896]{3,2,1,0:T(8,128)(2,1)S(1)} %collective-permute-done.3.a0, bf16[2,2,32,896]{3,2,1,0:T(8,128)(2,1)S(1)} %collective-permute-done.4.a1, ...), custom_call_target="tpu_custom_call" | custom-call | flops 2000000000 | bytes 5000000 | tf_op jit(solution)/shard_map/pallas_call | solution.py:261
  24.7 1.8 %collective-permute-start.8 = (bf16[224,1024]{1,0:T(8,128)(2,1)S(1)}, bf16[224,1024]{1,0:T(8,128)(2,1)S(1)}, u32[]{:S(2)}, u32[]{:S(2)}) collective-permute-start(bf16[224,1024]{1,0:T(8,128)(2,1)S(1)} %get-tuple-element.106), channel_id=1, source_target_pairs={{0,64},{64,128},{128,192},{192,0},{4,196},{68,4},{132,68},{196,132... | collective-permute-start | bytes 1376264 | tf_op jit(solution)/shard_map/ppermute | solution.py:49
  26.5 4.5 %shard_map.107 = (f32[2,2,32,896]{3,2,1,0:T(8,128)S(1)}, bf16[2,2,32,896]{3,2,1,0:T(8,128)(2,1)S(1)}, bf16[2,2,32,896]{3,2,1,0:T(8,128)(2,1)S(1)}, f32[2,2,32,896]{3,2,1,0:T(8,128)S(1)}) custom-call(s32[5]{0:T(128)S(1)} %pad_add_fusion.refs_0_.flags, bf16[512,1024]{1,0:T(8,128)(2,1)S(1)} %get-tuple-element.102.grads.keep, ...), custom_call_target="tpu_custom_call" | custom-call | flops 4000000000 | bytes 10000000 | tf_op jit(solution)/shard_map/pallas_call | solution.py:214
  31.6 1.8 %collective-permute-done.8.b = bf16[224,1024]{1,0:T(8,128)(2,1)S(1)} collective-permute-done((bf16[224,1024]{1,0:T(8,128)(2,1)S(1)}, bf16[224,1024]{1,0:T(8,128)(2,1)S(1)}, u32[]{:S(2)}, u32[]{:S(2)}) %collective-permute-start.8) | collective-permute-done | bytes 458784 | tf_op jit(solution)/shard_map/ppermute | solution.py:49
  33.4 0.8 %shard_map.108 = (bf16[5,32,1024]{2,1,0:T(8,128)(2,1)S(1)}, bf16[3,32,1024]{2,1,0:T(8,128)(2,1)S(1)}) custom-call(s32[6]{0:T(128)S(1)} %stack.24.place, f32[224,1024]{1,0:T(8,128)S(1)} %get-tuple-element.105.a, bf16[224,1024]{1,0:T(8,128)(2,1)S(1)} %collective-permute-done.8.b), custom_call_target="tpu_custom_call" | custom-call | tf_op jit(solution)/shard_map/pallas_call | solution.py:311
  34.2 2.5 %collective-permute-start.10 = (bf16[5,32,1024]{2,1,0:T(8,128)(2,1)S(1)}, bf16[5,32,1024]{2,1,0:T(8,128)(2,1)S(1)}, u32[]{:S(2)}, u32[]{:S(2)}) collective-permute-start(bf16[5,32,1024]{2,1,0:T(8,128)(2,1)S(1)} %get-tuple-element.117), channel_id=1, source_target_pairs={{0,64},{64,128},{128,192},{192,0},{4,196},{68,4},{132,68},{196,132... | collective-permute-start | bytes 983048 | tf_op jit(solution)/shard_map/ppermute | solution.py:49
  36.7 1.4 %collective-permute-start.12 = (bf16[2,2,32,896]{3,2,1,0:T(8,128)(2,1)S(1)}, bf16[2,2,32,896]{3,2,1,0:T(8,128)(2,1)S(1)}, u32[]{:S(2)}, u32[]{:S(2)}) collective-permute-start(bf16[2,2,32,896]{3,2,1,0:T(8,128)(2,1)S(1)} %get-tuple-element.119), channel_id=1, source_target_pairs={{0,1},{1,2},{2,3},{3,0},{4,7},{5,4},{6,5},{7,6},{8,9},{9,10},{10,1... | collective-permute-start | bytes 688136 | tf_op jit(solution)/shard_map/ppermute | solution.py:49
  38.1 4.8 %collective-permute-done.9.b = bf16[224,1024]{1,0:T(8,128)(2,1)S(1)} collective-permute-done((bf16[224,1024]{1,0:T(8,128)(2,1)S(1)}, bf16[224,1024]{1,0:T(8,128)(2,1)S(1)}, u32[]{:S(2)}, u32[]{:S(2)}) %collective-permute-start.9) | collective-permute-done | bytes 458784 | tf_op jit(solution)/shard_map/ppermute | solution.py:49
  43.0 0.8 %shard_map.109 = (f32[5,32,1024]{2,1,0:T(8,128)S(1)}, bf16[3,32,1024]{2,1,0:T(8,128)(2,1)S(1)}) custom-call(s32[6]{0:T(128)S(1)} %stack.24.place, f32[224,1024]{1,0:T(8,128)S(1)} %get-tuple-element.110.a, bf16[224,1024]{1,0:T(8,128)(2,1)S(1)} %collective-permute-done.9.b), custom_call_target="tpu_custom_call" | custom-call | tf_op jit(solution)/shard_map/pallas_call | solution.py:311
  43.9 1.3 %collective-permute-done.11.front_cross = bf16[3,32,1024]{2,1,0:T(8,128)(2,1)S(1)} collective-permute-done((bf16[3,32,1024]{2,1,0:T(8,128)(2,1)S(1)}, bf16[3,32,1024]{2,1,0:T(8,128)(2,1)S(1)}, u32[]{:S(2)}, u32[]{:S(2)}) %collective-permute-start.11) | collective-permute-done | bytes 196640 | tf_op jit(solution)/shard_map/ppermute | solution.py:49
  45.4 2.0 %collective-permute-start.14 = (bf16[3,32,1024]{2,1,0:T(8,128)(2,1)S(1)}, bf16[3,32,1024]{2,1,0:T(8,128)(2,1)S(1)}, u32[]{:S(2)}, u32[]{:S(2)}) collective-permute-start(bf16[3,32,1024]{2,1,0:T(8,128)(2,1)S(1)} %get-tuple-element.124), channel_id=1, source_target_pairs={{0,8},{8,16},{16,24},{24,32},{32,40},{40,48},{48,56},{56,0},{4,60}... | collective-permute-start | bytes 589832 | tf_op jit(solution)/shard_map/ppermute | solution.py:49
  47.4 4.5 %collective-permute-start.17 = (bf16[2,32,1024]{2,1,0:T(8,128)(2,1)S(1)}, bf16[2,32,1024]{2,1,0:T(8,128)(2,1)S(1)}, u32[]{:S(2)}, u32[]{:S(2)}) collective-permute-start(bf16[2,32,1024]{2,1,0:T(8,128)(2,1)S(1)} %get-tuple-element.131), channel_id=1, source_target_pairs={{0,16},{8,24},{16,32},{24,40},{32,48},{40,56},{48,0},{56,8},{4,52}... | collective-permute-start | bytes 393224 | tf_op jit(solution)/shard_map/ppermute | solution.py:49
  52.0 6.9 %collective-permute-start.18 = (bf16[2,32,1024]{2,1,0:T(8,128)(2,1)S(1)}, bf16[2,32,1024]{2,1,0:T(8,128)(2,1)S(1)}, u32[]{:S(2)}, u32[]{:S(2)}) collective-permute-start(bf16[2,32,1024]{2,1,0:T(8,128)(2,1)S(1)} %shard_map.111), channel_id=1, source_target_pairs={{0,24},{8,32},{16,40},{24,48},{32,56},{40,0},{48,8},{56,16},{4,44}... | collective-permute-start | bytes 393224 | tf_op jit(solution)/shard_map/ppermute | solution.py:49
  58.9 2.6 %collective-permute-start.15 = (bf16[2,2,32,896]{3,2,1,0:T(8,128)(2,1)S(1)}, bf16[2,2,32,896]{3,2,1,0:T(8,128)(2,1)S(1)}, u32[]{:S(2)}, u32[]{:S(2)}) collective-permute-start(bf16[2,2,32,896]{3,2,1,0:T(8,128)(2,1)S(1)} %get-tuple-element.128), channel_id=1, source_target_pairs={{0,3},{1,0},{2,1},{3,2},{4,5},{5,6},{6,7},{7,4},{8,11},{9,8},{10,9... | collective-permute-start | bytes 688136 | tf_op jit(solution)/shard_map/ppermute | solution.py:49
  61.5 1.3 %collective-permute-done.18.three = bf16[2,32,1024]{2,1,0:T(8,128)(2,1)S(1)} collective-permute-done((bf16[2,32,1024]{2,1,0:T(8,128)(2,1)S(1)}, bf16[2,32,1024]{2,1,0:T(8,128)(2,1)S(1)}, u32[]{:S(2)}, u32[]{:S(2)}) %collective-permute-start.18) | collective-permute-done | bytes 131104 | tf_op jit(solution)/shard_map/ppermute | solution.py:49
  62.8 0.6 shard_map.113
  63.6 1.5 %collective-permute-done.15 = bf16[2,2,32,896]{3,2,1,0:T(8,128)(2,1)S(1)} collective-permute-done((bf16[2,2,32,896]{3,2,1,0:T(8,128)(2,1)S(1)}, bf16[2,2,32,896]{3,2,1,0:T(8,128)(2,1)S(1)}, u32[]{:S(2)}, u32[]{:S(2)}) %collective-permute-start.15) | collective-permute-done | bytes 229408 | tf_op jit(solution)/shard_map/ppermute | solution.py:49
  65.0 3.7 %collective-permute-done.16 = bf16[2,2,32,896]{3,2,1,0:T(8,128)(2,1)S(1)} collective-permute-done((bf16[2,2,32,896]{3,2,1,0:T(8,128)(2,1)S(1)}, bf16[2,2,32,896]{3,2,1,0:T(8,128)(2,1)S(1)}, u32[]{:S(2)}, u32[]{:S(2)}) %collective-permute-start.16) | collective-permute-done | bytes 229408 | tf_op jit(solution)/shard_map/ppermute | solution.py:49
  68.7 0.8 %convert_add_fusion = f32[2,2,32,896]{3,2,1,0:T(8,128)} fusion(bf16[2,2,32,896]{3,2,1,0:T(8,128)(2,1)S(1)} %collective-permute-done.16, f32[2,2,32,896]{3,2,1,0:T(8,128)S(1)} %get-tuple-element.104, bf16[2,2,32,896]{3,2,1,0:T(8,128)(2,1)S(1)} %collective-permute-done.15), kind=kLoop, calls=%fused_computation | loop fusion | flops 458752 | bytes 1376256 | tf_op jit(solution)/shard_map/add | solution.py:443
  69.6 0.7 select_bitcast_fusion
  (26 shorter events, 2.2 us)
Async XLA Ops:
  0.6 10.3 %collective-permute-start.2 = (bf16[2,2,32,896]{3,2,1,0:T(8,128)(2,1)}, bf16[2,2,32,896]{3,2,1,0:T(8,128)(2,1)S(1)}, u32[]{:S(2)}, u32[]{:S(2)}) collective-permute-start(bf16[2,2,32,896]{3,2,1,0:T(8,128)(2,1)} %refs_4_), channel_id=1, source_target_pairs={{0,2},{1,3},{2,0},{3,1},{4,6},{5,7},{6,4},{7,5},{8,10},{9,11},{10,... | collective-permute-start | bytes 688136 | tf_op jit(solution)/shard_map/ppermute | solution.py:49
  3.7 11.0 %collective-permute-start.1 = (bf16[2,2,32,896]{3,2,1,0:T(8,128)(2,1)}, bf16[2,2,32,896]{3,2,1,0:T(8,128)(2,1)S(1)}, u32[]{:S(2)}, u32[]{:S(2)}) collective-permute-start(bf16[2,2,32,896]{3,2,1,0:T(8,128)(2,1)} %refs_4_), channel_id=1, source_target_pairs={{0,3},{1,0},{2,1},{3,2},{4,5},{5,6},{6,7},{7,4},{8,11},{9,8},{10,9... | collective-permute-start | bytes 688136 | tf_op jit(solution)/shard_map/ppermute | solution.py:49
  4.9 9.9 %collective-permute-start = (bf16[2,2,32,896]{3,2,1,0:T(8,128)(2,1)}, bf16[2,2,32,896]{3,2,1,0:T(8,128)(2,1)S(1)}, u32[]{:S(2)}, u32[]{:S(2)}) collective-permute-start(bf16[2,2,32,896]{3,2,1,0:T(8,128)(2,1)} %refs_4_), channel_id=1, source_target_pairs={{0,1},{1,2},{2,3},{3,0},{4,7},{5,4},{6,5},{7,6},{8,9},{9,10},{10,1... | collective-permute-start | bytes 688136 | tf_op jit(solution)/shard_map/ppermute | solution.py:49
  5.8 9.0 %collective-permute-start.3 = (bf16[2,2,32,896]{3,2,1,0:T(8,128)(2,1)}, bf16[2,2,32,896]{3,2,1,0:T(8,128)(2,1)S(1)}, u32[]{:S(2)}, u32[]{:S(2)}) collective-permute-start(bf16[2,2,32,896]{3,2,1,0:T(8,128)(2,1)} %refs_4_), channel_id=1, source_target_pairs={{0,4},{4,0},{1,5},{5,1},{2,6},{6,2},{3,7},{7,3},{8,12},{12,8},{9,1... | collective-permute-start | bytes 688136 | tf_op jit(solution)/shard_map/ppermute | solution.py:53
  10.9 3.9 %collective-permute-start.4 = (bf16[2,2,32,896]{3,2,1,0:T(8,128)(2,1)S(1)}, bf16[2,2,32,896]{3,2,1,0:T(8,128)(2,1)S(1)}, u32[]{:S(2)}, u32[]{:S(2)}) collective-permute-start(bf16[2,2,32,896]{3,2,1,0:T(8,128)(2,1)S(1)} %collective-permute-done.2.b.a1), channel_id=1, source_target_pairs={{0,4},{4,0},{1,5},{5,1},{2,6},{6,2},{3,7},{7,3},{8,12},{12,8},{9,1... | collective-permute-start | bytes 688136 | tf_op jit(solution)/shard_map/ppermute | solution.py:53
  14.8 1.9 %collective-permute-start.5 = (bf16[2,2,32,896]{3,2,1,0:T(8,128)(2,1)S(1)}, bf16[2,2,32,896]{3,2,1,0:T(8,128)(2,1)S(1)}, u32[]{:S(2)}, u32[]{:S(2)}) collective-permute-start(bf16[2,2,32,896]{3,2,1,0:T(8,128)(2,1)S(1)} %collective-permute-done.a.a2), channel_id=1, source_target_pairs={{0,4},{4,0},{1,5},{5,1},{2,6},{6,2},{3,7},{7,3},{8,12},{12,8},{9,1... | collective-permute-start | bytes 688136 | tf_op jit(solution)/shard_map/ppermute | solution.py:53
  14.9 1.8 %collective-permute-start.6 = (bf16[2,2,32,896]{3,2,1,0:T(8,128)(2,1)S(1)}, bf16[2,2,32,896]{3,2,1,0:T(8,128)(2,1)S(1)}, u32[]{:S(2)}, u32[]{:S(2)}) collective-permute-start(bf16[2,2,32,896]{3,2,1,0:T(8,128)(2,1)S(1)} %collective-permute-done.1.b.a3), channel_id=1, source_target_pairs={{0,4},{4,0},{1,5},{5,1},{2,6},{6,2},{3,7},{7,3},{8,12},{12,8},{9,1... | collective-permute-start | bytes 688136 | tf_op jit(solution)/shard_map/ppermute | solution.py:53
  20.1 2.7 %collective-permute-start.7 = (bf16[512,1024]{1,0:T(8,128)(2,1)S(1)}, bf16[512,1024]{1,0:T(8,128)(2,1)S(1)}, u32[]{:S(2)}, u32[]{:S(2)}) collective-permute-start(bf16[512,1024]{1,0:T(8,128)(2,1)S(1)} %get-tuple-element.103.send), channel_id=1, source_target_pairs={{0,4},{4,0},{1,5},{5,1},{2,6},{6,2},{3,7},{7,3},{8,12},{12,8},{9,1... | collective-permute-start | bytes 3145736 | tf_op jit(solution)/shard_map/ppermute | solution.py:53
  24.7 8.7 %collective-permute-start.8 = (bf16[224,1024]{1,0:T(8,128)(2,1)S(1)}, bf16[224,1024]{1,0:T(8,128)(2,1)S(1)}, u32[]{:S(2)}, u32[]{:S(2)}) collective-permute-start(bf16[224,1024]{1,0:T(8,128)(2,1)S(1)} %get-tuple-element.106), channel_id=1, source_target_pairs={{0,64},{64,128},{128,192},{192,0},{4,196},{68,4},{132,68},{196,132... | collective-permute-start | bytes 1376264 | tf_op jit(solution)/shard_map/ppermute | solution.py:49
  31.1 11.9 %collective-permute-start.9 = (bf16[224,1024]{1,0:T(8,128)(2,1)S(1)}, bf16[224,1024]{1,0:T(8,128)(2,1)S(1)}, u32[]{:S(2)}, u32[]{:S(2)}) collective-permute-start(bf16[224,1024]{1,0:T(8,128)(2,1)S(1)} %get-tuple-element.115), channel_id=1, source_target_pairs={{0,192},{64,0},{128,64},{192,128},{4,68},{68,132},{132,196},{196,4... | collective-permute-start | bytes 1376264 | tf_op jit(solution)/shard_map/ppermute | solution.py:49
  34.2 11.0 %collective-permute-start.10 = (bf16[5,32,1024]{2,1,0:T(8,128)(2,1)S(1)}, bf16[5,32,1024]{2,1,0:T(8,128)(2,1)S(1)}, u32[]{:S(2)}, u32[]{:S(2)}) collective-permute-start(bf16[5,32,1024]{2,1,0:T(8,128)(2,1)S(1)} %get-tuple-element.117), channel_id=1, source_target_pairs={{0,64},{64,128},{128,192},{192,0},{4,196},{68,4},{132,68},{196,132... | collective-permute-start | bytes 983048 | tf_op jit(solution)/shard_map/ppermute | solution.py:49
  36.7 7.2 %collective-permute-start.12 = (bf16[2,2,32,896]{3,2,1,0:T(8,128)(2,1)S(1)}, bf16[2,2,32,896]{3,2,1,0:T(8,128)(2,1)S(1)}, u32[]{:S(2)}, u32[]{:S(2)}) collective-permute-start(bf16[2,2,32,896]{3,2,1,0:T(8,128)(2,1)S(1)} %get-tuple-element.119), channel_id=1, source_target_pairs={{0,1},{1,2},{2,3},{3,0},{4,7},{5,4},{6,5},{7,6},{8,9},{9,10},{10,1... | collective-permute-start | bytes 688136 | tf_op jit(solution)/shard_map/ppermute | solution.py:49
  38.1 7.1 %collective-permute-start.11 = (bf16[3,32,1024]{2,1,0:T(8,128)(2,1)S(1)}, bf16[3,32,1024]{2,1,0:T(8,128)(2,1)S(1)}, u32[]{:S(2)}, u32[]{:S(2)}) collective-permute-start(bf16[3,32,1024]{2,1,0:T(8,128)(2,1)S(1)} %get-tuple-element.118), channel_id=1, source_target_pairs={{0,68},{64,132},{128,196},{192,4},{4,192},{68,0},{132,64},{196,128... | collective-permute-start | bytes 589832 | tf_op jit(solution)/shard_map/ppermute | solution.py:49
  43.8 1.5 %collective-permute-start.13 = (bf16[3,32,1024]{2,1,0:T(8,128)(2,1)S(1)}, bf16[3,32,1024]{2,1,0:T(8,128)(2,1)S(1)}, u32[]{:S(2)}, u32[]{:S(2)}) collective-permute-start(bf16[3,32,1024]{2,1,0:T(8,128)(2,1)S(1)} %get-tuple-element.121), channel_id=1, source_target_pairs={{0,4},{4,0},{1,5},{5,1},{2,6},{6,2},{3,7},{7,3},{8,12},{12,8},{9,1... | collective-permute-start | bytes 589832 | tf_op jit(solution)/shard_map/ppermute | solution.py:53
  45.4 6.5 %collective-permute-start.14 = (bf16[3,32,1024]{2,1,0:T(8,128)(2,1)S(1)}, bf16[3,32,1024]{2,1,0:T(8,128)(2,1)S(1)}, u32[]{:S(2)}, u32[]{:S(2)}) collective-permute-start(bf16[3,32,1024]{2,1,0:T(8,128)(2,1)S(1)} %get-tuple-element.124), channel_id=1, source_target_pairs={{0,8},{8,16},{16,24},{24,32},{32,40},{40,48},{48,56},{56,0},{4,60}... | collective-permute-start | bytes 589832 | tf_op jit(solution)/shard_map/ppermute | solution.py:49
  47.4 14.1 %collective-permute-start.17 = (bf16[2,32,1024]{2,1,0:T(8,128)(2,1)S(1)}, bf16[2,32,1024]{2,1,0:T(8,128)(2,1)S(1)}, u32[]{:S(2)}, u32[]{:S(2)}) collective-permute-start(bf16[2,32,1024]{2,1,0:T(8,128)(2,1)S(1)} %get-tuple-element.131), channel_id=1, source_target_pairs={{0,16},{8,24},{16,32},{24,40},{32,48},{40,56},{48,0},{56,8},{4,52}... | collective-permute-start | bytes 393224 | tf_op jit(solution)/shard_map/ppermute | solution.py:49
  52.0 10.8 %collective-permute-start.18 = (bf16[2,32,1024]{2,1,0:T(8,128)(2,1)S(1)}, bf16[2,32,1024]{2,1,0:T(8,128)(2,1)S(1)}, u32[]{:S(2)}, u32[]{:S(2)}) collective-permute-start(bf16[2,32,1024]{2,1,0:T(8,128)(2,1)S(1)} %shard_map.111), channel_id=1, source_target_pairs={{0,24},{8,32},{16,40},{24,48},{32,56},{40,0},{48,8},{56,16},{4,44}... | collective-permute-start | bytes 393224 | tf_op jit(solution)/shard_map/ppermute | solution.py:49
  58.9 6.2 %collective-permute-start.15 = (bf16[2,2,32,896]{3,2,1,0:T(8,128)(2,1)S(1)}, bf16[2,2,32,896]{3,2,1,0:T(8,128)(2,1)S(1)}, u32[]{:S(2)}, u32[]{:S(2)}) collective-permute-start(bf16[2,2,32,896]{3,2,1,0:T(8,128)(2,1)S(1)} %get-tuple-element.128), channel_id=1, source_target_pairs={{0,3},{1,0},{2,1},{3,2},{4,5},{5,6},{6,7},{7,4},{8,11},{9,8},{10,9... | collective-permute-start | bytes 688136 | tf_op jit(solution)/shard_map/ppermute | solution.py:49
  61.5 7.2 %collective-permute-start.16 = (bf16[2,2,32,896]{3,2,1,0:T(8,128)(2,1)S(1)}, bf16[2,2,32,896]{3,2,1,0:T(8,128)(2,1)S(1)}, u32[]{:S(2)}, u32[]{:S(2)}) collective-permute-start(bf16[2,2,32,896]{3,2,1,0:T(8,128)(2,1)S(1)} %shard_map.112), channel_id=1, source_target_pairs={{0,1},{1,2},{2,3},{3,0},{4,7},{5,4},{6,5},{7,6},{8,9},{9,10},{10,1... | collective-permute-start | bytes 688136 | tf_op jit(solution)/shard_map/ppermute | solution.py:49
  63.5 6.1 %collective-permute-start.19 = (f32[2,14,1024]{2,1,0:T(8,128)S(1)}, f32[2,14,1024]{2,1,0:T(8,128)S(1)}, u32[]{:S(2)}, u32[]{:S(2)}) collective-permute-start(f32[2,14,1024]{2,1,0:T(8,128)S(1)} %get-tuple-element.134), channel_id=1, source_target_pairs={{0,4},{4,0},{1,5},{5,1},{2,6},{6,2},{3,7},{7,3},{8,12},{12,8},{9,1... | collective-permute-start | bytes 344072 | tf_op jit(solution)/shard_map/ppermute | solution.py:53

commit v5 on v4

--- a/solution.py
+++ b/solution.py
@@ -8,6 +8,7 @@
 HEAD = 128
 PAD = 32
 BLOCK = 512
+PART = 256
 BF = jnp.bfloat16
 F32 = jnp.float32
 NN = (((1,), (0,)), ((), ()))
@@ -181,97 +182,117 @@
     )(flags, *near_by(k1, v1, k2, v2, queries, cotangent))
 
 
-def passage_body(flags, keep, send, key_hbm, value_hbm, o0, o1, o2, o3, key_w, value_w, sems):
+def passage_add(flags, keep, send, total, columns, weights):
     first = flags[0] == 0
-    width = keep.shape[1]
-    loads = []
-    for i, start in enumerate(range(0, width, BLOCK)):
-        here = pl.ds(start, BLOCK)
-        for k, (source, target) in enumerate(((key_hbm, key_w), (value_hbm, value_w))):
-            copy = pltpu.make_async_copy(source.at[:, here], target.at[i], sems.at[2 * i + k])
-            copy.start()
-            loads.append(copy)
-    total = 0.0
-    for i, start in enumerate(range(0, width, BLOCK)):
-        a, b = keep[:, start : start + BLOCK], send[:, start : start + BLOCK]
-        loads[2 * i].wait()
-        loads[2 * i + 1].wait()
-        total = total + dot(jnp.where(first, a, b), key_w[i], NT)
-        total = total + dot(jnp.where(first, b, a), value_w[i], NT)
-    stretches, neigh, group, _ = o0.shape
+    for (key_w, value_w), start in zip(weights, columns):
+        a, b = keep[:, start : start + PART], send[:, start : start + PART]
+        total = total + dot(jnp.where(first, a, b), key_w[...], NT)
+        total = total + dot(jnp.where(first, b, a), value_w[...], NT)
+    return total
+
+
+def passage_open_body(flags, keep, send, key_hbm, value_hbm, partial, *refs):
+    parts = keep.shape[1] // PART
+    rest, (key_w, value_w, sems) = refs[: 2 * parts - 2], refs[2 * parts - 2 :]
+    targets = (key_w, value_w) + rest
+    loads = [
+        pltpu.make_async_copy(
+            (key_hbm, value_hbm)[i % 2].at[:, pl.ds(i // 2 * PART, PART)], target, sems.at[i]
+        )
+        for i, target in enumerate(targets)
+    ]
+    for load in loads:
+        load.start()
+    for load in loads[:2]:
+        load.wait()
+    partial[...] = passage_add(flags, keep, send, 0.0, (0,), ((key_w, value_w),))
+    for load in loads[2:]:
+        load.wait()
+
+
+def passage_open(flags, keep, send, key_w, value_w):
+    enc, width = key_w.shape
+    rest = 2 * (width // PART) - 2
+    far = [pltpu.with_memory_space_constraint(a, pltpu.HBM) for a in (key_w, value_w)]
+    return pl.pallas_call(
+        passage_open_body,
+        in_specs=[SMEM] + [VMEM] * 2 + [HBM] * 2,
+        out_specs=[VMEM] * (1 + rest),
+        out_shape=[shape((keep.shape[0], enc), F32)] + [shape((enc, PART), BF)] * rest,
+        scratch_shapes=[
+            pltpu.VMEM((enc, PART), BF),
+            pltpu.VMEM((enc, PART), BF),
+            pltpu.SemaphoreType.DMA((rest + 2,)),
+        ],
+        compiler_params=params(),
+        cost_estimate=cost(2 * 10**9, 5 * 10**6),
+    )(flags, *near_by(keep, send), *far)
+
+
+def passage_close_body(flags, keep, send, partial, *refs):
+    rest, outs = refs[:-4], refs[-4:]
+    pairs = list(zip(rest[::2], rest[1::2]))
+    columns = range(PART, keep.shape[1], PART)
+    total = passage_add(flags, keep, send, partial[...], columns, pairs)
+    stretches, neigh, group, _ = outs[0].shape
     start = 0
     for c in range(stretches):
-        for o in (o0, o1, o2, o3):
+        for o in outs:
             for n in range(neigh):
                 o[c, n] = total[start : start + group].astype(o.dtype)
                 start += group
 
 
-def passage_grad(flags, keep, send, key_w, value_w, slab):
-    enc, width = key_w.shape
-    parts = width // BLOCK
-    far = [pltpu.with_memory_space_constraint(a, pltpu.HBM) for a in (key_w, value_w)]
-    return pl.pallas_call(
-        passage_body,
-        in_specs=[SMEM] + [VMEM] * 2 + [HBM] * 2,
+def passage_close(flags, keep, send, partial, rest, slab):
+    return pl.pallas_call(
+        passage_close_body,
+        in_specs=[SMEM] + [VMEM] * (3 + len(rest)),
         out_specs=[VMEM] * 4,
         out_shape=[shape(slab, d) for d in (F32, BF, BF, F32)],
-        scratch_shapes=[
-            pltpu.VMEM((parts, enc, BLOCK), BF),
-            pltpu.VMEM((parts, enc, BLOCK), BF),
-            pltpu.SemaphoreType.DMA((2 * parts,)),
-        ],
-        compiler_params=params(),
-        cost_estimate=cost(4 * 10**9, 10**7),
-    )(flags, *near_by(keep, send), *far)
-
-
-def weight_body(a0, a1, a2, a3, grads, out, rows):
+        compiler_params=params(),
+        cost_estimate=cost(2 * 10**9, 5 * 10**6),
+    )(flags, *near_by(keep, send, partial, *rest))
+
+
+def weight_body(a0, a1, a2, a3, b0, b1, b2, b3, grads, out, turned, rows):
+    gathered((b0, b1, b2, b3), rows, 0)
+    turned[...] = rows[...].T
     gathered((a0, a1, a2, a3), rows, 0)
     out[...] = dot(rows[...], grads[...], TN)
 
 
-def weight_grad(slabs, grads):
+def weight_grad(slabs, slabs_other, grads):
     enc = slabs[0].shape[-1]
     row_count, width = grads.shape
     return pl.pallas_call(
         weight_body,
-        in_specs=[VMEM] * 5,
-        out_specs=VMEM,
-        out_shape=shape((enc, width), F32),
+        in_specs=[VMEM] * 9,
+        out_specs=[VMEM] * 2,
+        out_shape=[shape((enc, width), F32), shape((enc, row_count), BF)],
         scratch_shapes=[pltpu.VMEM((row_count, enc), BF)],
         compiler_params=params(),
         cost_estimate=cost(2 * 10**9, 5 * 10**6),
-    )(*near_by(*slabs, grads))
-
-
-def split_body(place, a0, a1, a2, a3, grads, partial, mine, far, back, front, rows, total):
-    height = mine.shape[0]
-    gathered((a0, a1, a2, a3), rows, 0)
-    total[...] = partial[...] + dot(rows[...], grads[...], TN)
-    for i, out in enumerate((mine, far, back, front)):
-        first = pl.multiple_of(place[i] * height, 8)
-        out[...] = total[pl.ds(first, height), :].astype(out.dtype)
-
-
-def weight_split(place, slabs, grads, partial, parts):
+    )(*near_by(*slabs, *slabs_other, grads))
+
+
+def split_body(which, place, turned, grads, partial, *outs):
+    for i, out in zip(which, outs):
+        height = out.shape[0]
+        here = pl.ds(pl.multiple_of(place[i] * height, 32), height)
+        total = partial[here, :] + dot(turned[here, :], grads[...])
+        out[...] = total.astype(out.dtype)
+
+
+def weight_split(place, turned, grads, partial, parts, which, dtypes):
     enc, width = partial.shape
-    row_count = grads.shape[0]
-    height = enc // parts
-    return pl.pallas_call(
-        split_body,
-        in_specs=[SMEM] + [VMEM] * 6,
-        out_specs=[VMEM] * 4,
-        out_shape=[
-            shape((height, width), F32),
-            shape((height, width), BF),
-            shape((height, width), BF),
-            shape((height, width), F32),
-        ],
-        scratch_shapes=[pltpu.VMEM((row_count, enc), BF), pltpu.VMEM((enc, width), F32)],
-        compiler_params=params(),
-        cost_estimate=cost(2 * 10**9, 5 * 10**6),
-    )(place, *near_by(*slabs, grads, partial))
+    return pl.pallas_call(
+        lambda *refs: split_body(which, *refs),
+        in_specs=[SMEM] + [VMEM] * 3,
+        out_specs=[VMEM] * len(which),
+        out_shape=[shape((enc // parts, width), d) for d in dtypes],
+        compiler_params=params(),
+        cost_estimate=cost(10**9, 5 * 10**6),
+    )(place, *near_by(turned, grads, partial))
 
 
 def add_body(a, b, out):
@@ -413,29 +434,36 @@
 
     attended, query_grad, keep, send = attend(flags, k1, v1, k2, v2, q, g, own.shape[2])
     received = swap(send)
-    partial = weight_grad(slabs, keep)
+    partial, turned = weight_grad(slabs, others, keep)
     received, partial = tie((received, partial))
-    mine, far, back, front = weight_split(place, others, received, partial, ny)
+    (far,) = weight_split(place, turned, received, partial, ny, (1,), (BF,))
     far_in = hop(far, "y", ny, 1)
+    far, partial = tie((far, partial))
+    mine, back, front = weight_split(
+        place, turned, received, partial, ny, (0, 2, 3), (F32, BF, F32)
+    )
     keep, send, front = tie((keep, send, front))
-    p0, p3, p1, p2 = passage_grad(flags, keep, send, key_weight, value_weight, own.shape)
-    back, p1, p2, p3 = tie((back, p1, p2, p3))
+    part, *rest = passage_open(flags, keep, send, key_weight, value_weight)
+    back, part = tie((back, part))
     back_in = hop(back, "y", ny, -1)
+    p0, p3, p1, p2 = passage_close(flags, keep, send, part, rest, own.shape)
+    far_in, p1, p2, p3 = tie((far_in, p1, p2, p3))
     front, front_cross = deal(place, front, far_in, BF)
     front, front_cross, mine = tie((front, front_cross, mine))
     front_in = hop(front, "y", ny, 1)
     cross_in = hop(front_cross, "y", ny, 1, cross=True)
     base, cross = deal(place, mine, back_in, F32)
     cross = swap(cross)
-    front_in, cross_in, beyond = tie((front_in, cross_in, hop(p3, "x", nx, 1)))
+    p1_in = hop(p1, "x", nx, -1)
+    front_in, cross_in, beyond, p1_in = tie((front_in, cross_in, hop(p3, "x", nx, 1), p1_in))
 
     here, one, two, three = fold(base, front_in, cross, cross_in, mine.shape[0] // nz)
     one_in = hop(one, "z", nz, 1)
     two_in = hop(two, "z", nz, 2)
     share = add(p2, beyond)
-    three, share, p1 = tie((relay(three, one_in), share, p1))
+    three, share = tie((relay(three, one_in), share))
     three_in = hop(three, "z", nz, 3)
-    returned = [hop(p1, "x", nx, -1), hop(share, "x", nx, 1)]
+    returned = [p1_in, hop(share, "x", nx, 1)]
     stay, give = finish(place, here, one_in, two_in, three_in)
     other = swap(give)
     neighbour_grad = p0

time: 70.3 us -> 68.4 us (0.973)
  the two profiles are of different devices: /device:TPU:40 before, /device:TPU:1 now
where the time goes in v5:
time: 68.4 us; the launch traced here: 68.1 us
  starting transfers between devices  35.1 us (51%)
  Pallas kernels  19.1 us (28%)
  waiting for transfers between devices  10.7 us (16%)
  other arithmetic  1.59 us (2%)
  local copies, waits for them, and re-layouts  0.84 us (1%)
  between operations  0.8 us (1%)
    ppermute x13, starting transfers between devices, hop(): return lax.ppermute(value, ('c', axis) if inner else (axis, 'c'), pairs)  28.4 us
    ppermute x13, waiting for transfers between devices, hop(): return lax.ppermute(value, ('c', axis) if inner else (axis, 'c'), pairs)  9.22 us
    ppermute x7, starting transfers between devices, swap(): return lax.ppermute(value, 'c', [(0, 1), (1, 0)])  6.71 us
    pallas_call x1, Pallas kernels, attend(): pl.pallas_call(lambda *refs: attend_body(group, *refs), in_specs=[SMEM] +...  3.43 us
    pallas_call x1, Pallas kernels, passage_open(): pl.pallas_call(passage_open_body, in_specs=[SMEM] + [VMEM] * 2 + [HBM] *...  2.65 us
    pallas_call x2, Pallas kernels, project(): pl.pallas_call(project_body, in_specs=[VMEM] * 4, out_specs=[VMEM] * 2, o...  2.5 us
    pallas_call x2, Pallas kernels, weight_split(): pl.pallas_call(lambda *refs: split_body(which, *refs), in_specs=[SMEM] +...  2.37 us
    pallas_call x1, Pallas kernels, passage_close(): pl.pallas_call(passage_close_body, in_specs=[SMEM] + [VMEM] * (3 + len(re...  2.36 us
  transfers between devices with their start and end apart: 20, of which 7 were waited for; matrix products, arithmetic and copies ran while one was open for 3% of the time, Pallas kernels for 22%

profile of v5, /device:TPU:1, one launch (start us, length us, event | category | flops | bytes accessed | tf_op | source)
XLA Modules:
  0.0 68.1 jit_solution(7386462451664960027)
XLA Ops:
  0.6 3.7 %collective-permute-start.2 = (bf16[2,2,32,896]{3,2,1,0:T(8,128)(2,1)}, bf16[2,2,32,896]{3,2,1,0:T(8,128)(2,1)S(1)}, u32[]{:S(2)}, u32[]{:S(2)}) collective-permute-start(bf16[2,2,32,896]{3,2,1,0:T(8,128)(2,1)} %refs_4_), channel_id=1, source_target_pairs={{0,2},{1,3},{2,0},{3,1},{4,6},{5,7},{6,4},{7,5},{8,10},{9,11},{10,... | collective-permute-start | bytes 688136 | tf_op jit(solution)/shard_map/ppermute | solution.py:50
  4.6 2.4 %collective-permute-start = (bf16[2,2,32,896]{3,2,1,0:T(8,128)(2,1)}, bf16[2,2,32,896]{3,2,1,0:T(8,128)(2,1)S(1)}, u32[]{:S(2)}, u32[]{:S(2)}) collective-permute-start(bf16[2,2,32,896]{3,2,1,0:T(8,128)(2,1)} %refs_4_), channel_id=1, source_target_pairs={{0,1},{1,2},{2,3},{3,0},{4,7},{5,4},{6,5},{7,6},{8,9},{9,10},{10,1... | collective-permute-start | bytes 688136 | tf_op jit(solution)/shard_map/ppermute | solution.py:50
  7.3 0.8 %reshape.19 = s32[4]{0:T(128)S(1)} reshape(s32[2,2]{1,0:T(2,128)} %param.9) | data formatting | bytes 32 | tf_op jit(solution)/shard_map/reshape | solution.py:419
  8.2 2.2 %shard_map.101 = (bf16[896,1024]{1,0:T(8,128)(2,1)S(1)}, bf16[896,1024]{1,0:T(8,128)(2,1)S(1)}, bf16[128,1024]{1,0:T(8,128)(2,1)S(1)}, bf16[128,1024]{1,0:T(8,128)(2,1)S(1)}, bf16[2,2,32,896]{3,2,1,0:T(8,128)(2,1)S(1)}) custom-call(bf16[896,1024]{1,0:T(8,128)(2,1)} %key_hbm.1, bf16[896,1024]{1,0:T(8,128)(2,1)} %value_hbm.1, bf16[128,1024]{1,0:T(8,128)(2,1)} %refs_2_.1, ...), custom_call_target="tpu_custom_call" | custom-call | tf_op jit(solution)/shard_map/pallas_call | solution.py:105
  10.5 3.2 %collective-permute-start.4 = (bf16[2,2,32,896]{3,2,1,0:T(8,128)(2,1)S(1)}, bf16[2,2,32,896]{3,2,1,0:T(8,128)(2,1)S(1)}, u32[]{:S(2)}, u32[]{:S(2)}) collective-permute-start(bf16[2,2,32,896]{3,2,1,0:T(8,128)(2,1)S(1)} %collective-permute-done.2.b.a1), channel_id=1, source_target_pairs={{0,4},{4,0},{1,5},{5,1},{2,6},{6,2},{3,7},{7,3},{8,12},{12,8},{9,1... | collective-permute-start | bytes 688136 | tf_op jit(solution)/shard_map/ppermute | solution.py:54
  13.6 1.3 %shard_map.102 = (bf16[2,128,1024]{2,1,0:T(8,128)(2,1)S(1)}, bf16[2,128,1024]{2,1,0:T(8,128)(2,1)S(1)}) custom-call(bf16[2,2,32,896]{3,2,1,0:T(8,128)(2,1)S(1)} %get-tuple-element.84.a.a0, bf16[2,2,32,896]{3,2,1,0:T(8,128)(2,1)S(1)} %collective-permute-done.2.b.a1, bf16[896,1024]{1,0:T(8,128)(2,1)S(1)} %get-tuple-element.86.key_w, ...), custom_call_target="tpu_custom_call" | custom-call | tf_op jit(solution)/shard_map/pallas_call | solution.py:128
  15.0 1.4 %collective-permute-start.5 = (bf16[2,2,32,896]{3,2,1,0:T(8,128)(2,1)S(1)}, bf16[2,2,32,896]{3,2,1,0:T(8,128)(2,1)S(1)}, u32[]{:S(2)}, u32[]{:S(2)}) collective-permute-start(bf16[2,2,32,896]{3,2,1,0:T(8,128)(2,1)S(1)} %collective-permute-done.a.a2), channel_id=1, source_target_pairs={{0,4},{4,0},{1,5},{5,1},{2,6},{6,2},{3,7},{7,3},{8,12},{12,8},{9,1... | collective-permute-start | bytes 688136 | tf_op jit(solution)/shard_map/ppermute | solution.py:54
  16.5 1.2 %shard_map.103 = (bf16[2,128,1024]{2,1,0:T(8,128)(2,1)S(1)}, bf16[2,128,1024]{2,1,0:T(8,128)(2,1)S(1)}) custom-call(bf16[2,2,32,896]{3,2,1,0:T(8,128)(2,1)S(1)} %collective-permute-done.a.a2, bf16[2,2,32,896]{3,2,1,0:T(8,128)(2,1)S(1)} %collective-permute-done.1.b.a3, bf16[896,1024]{1,0:T(8,128)(2,1)S(1)} %get-tuple-element.86.key_w, ...), custom_call_target="tpu_custom_call" | custom-call | tf_op jit(solution)/shard_map/pallas_call | solution.py:128
  17.9 3.4 %shard_map.104 = (bf16[128,1024]{1,0:T(8,128)(2,1)}, bf16[128,1024]{1,0:T(8,128)(2,1)}, bf16[512,1024]{1,0:T(8,128)(2,1)S(1)}, bf16[512,1024]{1,0:T(8,128)(2,1)S(1)}) custom-call(s32[5]{0:T(128)S(1)} %pad_add_fusion.refs_0_.flags, bf16[2,128,1024]{2,1,0:T(8,128)(2,1)S(1)} %get-tuple-element.90.refs_1_, bf16[2,128,1024]{2,1,0:T(8,128)(2,1)S(1)} %get-tuple-element.91.refs_2_, ...), custom_call_target="tpu_custom_call" | custom-call | tf_op jit(solution)/shard_map/pallas_call | solution.py:175
  21.6 1.2 %shard_map.105 = (f32[896,1024]{1,0:T(8,128)S(1)}, bf16[896,512]{1,0:T(8,128)(2,1)S(1)}) custom-call(bf16[2,2,32,896]{3,2,1,0:T(8,128)(2,1)S(1)} %get-tuple-element.84.a.a0, bf16[2,2,32,896]{3,2,1,0:T(8,128)(2,1)S(1)} %collective-permute-done.2.b.a1, bf16[2,2,32,896]{3,2,1,0:T(8,128)(2,1)S(1)} %collective-permute-done.a.a2, ...), custom_call_target="tpu_custom_call" | custom-call | flops 2000000000 | bytes 5000000 | tf_op jit(solution)/shard_map/pallas_call | solution.py:267
  22.8 1.2 %collective-permute-done.7.refs_2_ = bf16[512,1024]{1,0:T(8,128)(2,1)S(1)} collective-permute-done((bf16[512,1024]{1,0:T(8,128)(2,1)S(1)}, bf16[512,1024]{1,0:T(8,128)(2,1)S(1)}, u32[]{:S(2)}, u32[]{:S(2)}) %collective-permute-start.7) | collective-permute-done | bytes 1048608 | tf_op jit(solution)/shard_map/ppermute | solution.py:54
  24.0 0.9 %shard_map.106 = bf16[224,1024]{1,0:T(8,128)(2,1)S(1)} custom-call(s32[6]{0:T(128)S(1)} %stack.24.refs_0_.place, bf16[896,512]{1,0:T(8,128)(2,1)S(1)} %get-tuple-element.110.refs_1_, bf16[512,1024]{1,0:T(8,128)(2,1)S(1)} %collective-permute-done.7.refs_2_, f32[896,1024]{1,0:T(8,128)S(1)} %get-tuple-element.114.refs_3_), custom_call_target="tpu_custom_call" | custom-call | flops 1000000000 | bytes 5000000 | tf_op jit(solution)/shard_map/pallas_call | solution.py:288
  24.9 2.8 %collective-permute-start.8 = (bf16[224,1024]{1,0:T(8,128)(2,1)S(1)}, bf16[224,1024]{1,0:T(8,128)(2,1)S(1)}, u32[]{:S(2)}, u32[]{:S(2)}) collective-permute-start(bf16[224,1024]{1,0:T(8,128)(2,1)S(1)} %shard_map.106), channel_id=1, source_target_pairs={{0,64},{64,128},{128,192},{192,0},{4,196},{68,4},{132,68},{196,132... | collective-permute-start | bytes 1376264 | tf_op jit(solution)/shard_map/ppermute | solution.py:50
  27.7 1.4 %shard_map.107 = (f32[224,1024]{1,0:T(8,128)S(1)}, bf16[224,1024]{1,0:T(8,128)(2,1)S(1)}, f32[224,1024]{1,0:T(8,128)S(1)}) custom-call(s32[6]{0:T(128)S(1)} %stack.24.refs_0_.place, bf16[896,512]{1,0:T(8,128)(2,1)S(1)} %get-tuple-element.110.refs_1_, bf16[512,1024]{1,0:T(8,128)(2,1)S(1)} %collective-permute-done.7.refs_2_, ...), custom_call_target="tpu_custom_call" | custom-call | flops 1000000000 | bytes 5000000 | tf_op jit(solution)/shard_map/pallas_call | solution.py:288
  29.2 2.7 %shard_map.108 = (f32[512,896]{1,0:T(8,128)S(1)}, bf16[896,256]{1,0:T(8,128)(2,1)S(1)}, bf16[896,256]{1,0:T(8,128)(2,1)S(1)}, bf16[896,256]{1,0:T(8,128)(2,1)S(1...) custom-call(s32[5]{0:T(128)S(1)} %pad_add_fusion.refs_0_.flags, ...), custom_call_target="tpu_custom_call" | custom-call | flops 2000000000 | bytes 5000000 | tf_op jit(solution)/shard_map/pallas_call | solution.py:217
  32.1 2.4 %shard_map.109 = (f32[2,2,32,896]{3,2,1,0:T(8,128)S(1)}, bf16[2,2,32,896]{3,2,1,0:T(8,128)(2,1)S(1)}, bf16[2,2,32,896]{3,2,1,0:T(8,128)(2,1)S(1)}, f32[2,2,32,896]{3,2,1,0:T(8,128)S(1)}) custom-call(s32[5]{0:T(128)S(1)} %pad_add_fusion.refs_0_.flags, bf16[512,1024]{1,0:T(8,128)(2,1)S(1)} %get-tuple-element.116.grads.keep, ...), custom_call_target="tpu_custom_call" | custom-call | flops 2000000000 | bytes 5000000 | tf_op jit(solution)/shard_map/pallas_call | solution.py:247
  34.5 0.8 %shard_map.110 = (bf16[5,32,1024]{2,1,0:T(8,128)(2,1)S(1)}, bf16[3,32,1024]{2,1,0:T(8,128)(2,1)S(1)}) custom-call(s32[6]{0:T(128)S(1)} %stack.24.refs_0_.place, f32[224,1024]{1,0:T(8,128)S(1)} %get-tuple-element.128.a, bf16[224,1024]{1,0:T(8,128)(2,1)S(1)} %collective-permute-done.8.b), custom_call_target="tpu_custom_call" | custom-call | tf_op jit(solution)/shard_map/pallas_call | solution.py:332
  35.3 2.7 %collective-permute-start.9 = (bf16[5,32,1024]{2,1,0:T(8,128)(2,1)S(1)}, bf16[5,32,1024]{2,1,0:T(8,128)(2,1)S(1)}, u32[]{:S(2)}, u32[]{:S(2)}) collective-permute-start(bf16[5,32,1024]{2,1,0:T(8,128)(2,1)S(1)} %get-tuple-element.136), channel_id=1, source_target_pairs={{0,64},{64,128},{128,192},{192,0},{4,196},{68,4},{132,68},{196,132... | collective-permute-start | bytes 983048 | tf_op jit(solution)/shard_map/ppermute | solution.py:50
  38.0 2.3 %collective-permute-start.11 = (bf16[2,2,32,896]{3,2,1,0:T(8,128)(2,1)S(1)}, bf16[2,2,32,896]{3,2,1,0:T(8,128)(2,1)S(1)}, u32[]{:S(2)}, u32[]{:S(2)}) collective-permute-start(bf16[2,2,32,896]{3,2,1,0:T(8,128)(2,1)S(1)} %get-tuple-element.138), channel_id=1, source_target_pairs={{0,1},{1,2},{2,3},{3,0},{4,7},{5,4},{6,5},{7,6},{8,9},{9,10},{10,1... | collective-permute-start | bytes 688136 | tf_op jit(solution)/shard_map/ppermute | solution.py:50
  40.4 1.9 %collective-permute-start.10 = (bf16[3,32,1024]{2,1,0:T(8,128)(2,1)S(1)}, bf16[3,32,1024]{2,1,0:T(8,128)(2,1)S(1)}, u32[]{:S(2)}, u32[]{:S(2)}) collective-permute-start(bf16[3,32,1024]{2,1,0:T(8,128)(2,1)S(1)} %get-tuple-element.137), channel_id=1, source_target_pairs={{0,68},{64,132},{128,196},{192,4},{4,192},{68,0},{132,64},{196,128... | collective-permute-start | bytes 589832 | tf_op jit(solution)/shard_map/ppermute | solution.py:50
  42.2 0.8 %shard_map.111 = (f32[5,32,1024]{2,1,0:T(8,128)S(1)}, bf16[3,32,1024]{2,1,0:T(8,128)(2,1)S(1)}) custom-call(s32[6]{0:T(128)S(1)} %stack.24.refs_0_.place, f32[224,1024]{1,0:T(8,128)S(1)} %get-tuple-element.141.a, bf16[224,1024]{1,0:T(8,128)(2,1)S(1)} %collective-permute-done.13.b), custom_call_target="tpu_custom_call" | custom-call | tf_op jit(solution)/shard_map/pallas_call | solution.py:332
  43.1 3.5 %collective-permute-done.10.front_cross = bf16[3,32,1024]{2,1,0:T(8,128)(2,1)S(1)} collective-permute-done((bf16[3,32,1024]{2,1,0:T(8,128)(2,1)S(1)}, bf16[3,32,1024]{2,1,0:T(8,128)(2,1)S(1)}, u32[]{:S(2)}, u32[]{:S(2)}) %collective-permute-start.10) | collective-permute-done | bytes 196640 | tf_op jit(solution)/shard_map/ppermute | solution.py:50
  46.8 5.7 %collective-permute-start.15 = (bf16[3,32,1024]{2,1,0:T(8,128)(2,1)S(1)}, bf16[3,32,1024]{2,1,0:T(8,128)(2,1)S(1)}, u32[]{:S(2)}, u32[]{:S(2)}) collective-permute-start(bf16[3,32,1024]{2,1,0:T(8,128)(2,1)S(1)} %get-tuple-element.148), channel_id=1, source_target_pairs={{0,8},{8,16},{16,24},{24,32},{32,40},{40,48},{48,56},{56,0},{4,60}... | collective-permute-start | bytes 589832 | tf_op jit(solution)/shard_map/ppermute | solution.py:50
  52.5 1.2 %collective-permute-start.17 = (bf16[2,32,1024]{2,1,0:T(8,128)(2,1)S(1)}, bf16[2,32,1024]{2,1,0:T(8,128)(2,1)S(1)}, u32[]{:S(2)}, u32[]{:S(2)}) collective-permute-start(bf16[2,32,1024]{2,1,0:T(8,128)(2,1)S(1)} %get-tuple-element.153), channel_id=1, source_target_pairs={{0,16},{8,24},{16,32},{24,40},{32,48},{40,56},{48,0},{56,8},{4,52}... | collective-permute-start | bytes 393224 | tf_op jit(solution)/shard_map/ppermute | solution.py:50
  53.7 2.0 %collective-permute-done.15.arrived.one = bf16[3,32,1024]{2,1,0:T(8,128)(2,1)S(1)} collective-permute-done((bf16[3,32,1024]{2,1,0:T(8,128)(2,1)S(1)}, bf16[3,32,1024]{2,1,0:T(8,128)(2,1)S(1)}, u32[]{:S(2)}, u32[]{:S(2)}) %collective-permute-start.15) | collective-permute-done | bytes 196640 | tf_op jit(solution)/shard_map/ppermute | solution.py:50
  55.7 2.4 %collective-permute-start.18 = (bf16[2,32,1024]{2,1,0:T(8,128)(2,1)S(1)}, bf16[2,32,1024]{2,1,0:T(8,128)(2,1)S(1)}, u32[]{:S(2)}, u32[]{:S(2)}) collective-permute-start(bf16[2,32,1024]{2,1,0:T(8,128)(2,1)S(1)} %shard_map.113), channel_id=1, source_target_pairs={{0,24},{8,32},{16,40},{24,48},{32,56},{40,0},{48,8},{56,16},{4,44}... | collective-permute-start | bytes 393224 | tf_op jit(solution)/shard_map/ppermute | solution.py:50
  58.1 2.8 %collective-permute-start.16 = (bf16[2,2,32,896]{3,2,1,0:T(8,128)(2,1)S(1)}, bf16[2,2,32,896]{3,2,1,0:T(8,128)(2,1)S(1)}, u32[]{:S(2)}, u32[]{:S(2)}) collective-permute-start(bf16[2,2,32,896]{3,2,1,0:T(8,128)(2,1)S(1)} %shard_map.114), channel_id=1, source_target_pairs={{0,1},{1,2},{2,3},{3,0},{4,7},{5,4},{6,5},{7,6},{8,9},{9,10},{10,1... | collective-permute-start | bytes 688136 | tf_op jit(solution)/shard_map/ppermute | solution.py:50
  60.9 3.6 %collective-permute-done.18.three = bf16[2,32,1024]{2,1,0:T(8,128)(2,1)S(1)} collective-permute-done((bf16[2,32,1024]{2,1,0:T(8,128)(2,1)S(1)}, bf16[2,32,1024]{2,1,0:T(8,128)(2,1)S(1)}, u32[]{:S(2)}, u32[]{:S(2)}) %collective-permute-start.18) | collective-permute-done | bytes 131104 | tf_op jit(solution)/shard_map/ppermute | solution.py:50
  64.5 0.6 shard_map.115
  65.1 1.3 %collective-permute-start.19 = (f32[2,14,1024]{2,1,0:T(8,128)S(1)}, f32[2,14,1024]{2,1,0:T(8,128)S(1)}, u32[]{:S(2)}, u32[]{:S(2)}) collective-permute-start(f32[2,14,1024]{2,1,0:T(8,128)S(1)} %get-tuple-element.156), channel_id=1, source_target_pairs={{0,4},{4,0},{1,5},{5,1},{2,6},{6,2},{3,7},{7,3},{8,12},{12,8},{9,1... | collective-permute-start | bytes 344072 | tf_op jit(solution)/shard_map/ppermute | solution.py:54
  66.5 0.8 %convert_add_fusion = f32[2,2,32,896]{3,2,1,0:T(8,128)} fusion(bf16[2,2,32,896]{3,2,1,0:T(8,128)(2,1)S(1)} %collective-permute-done.16, f32[2,2,32,896]{3,2,1,0:T(8,128)S(1)} %get-tuple-element.127, bf16[2,2,32,896]{3,2,1,0:T(8,128)(2,1)S(1)} %collective-permute-done.12), kind=kLoop, calls=%fused_computation | loop fusion | flops 458752 | bytes 1376256 | tf_op jit(solution)/shard_map/add | solution.py:471
  67.5 0.7 select_bitcast_fusion
  (28 shorter events, 2.1 us)
Async XLA Ops:
  0.6 9.8 %collective-permute-start.2 = (bf16[2,2,32,896]{3,2,1,0:T(8,128)(2,1)}, bf16[2,2,32,896]{3,2,1,0:T(8,128)(2,1)S(1)}, u32[]{:S(2)}, u32[]{:S(2)}) collective-permute-start(bf16[2,2,32,896]{3,2,1,0:T(8,128)(2,1)} %refs_4_), channel_id=1, source_target_pairs={{0,2},{1,3},{2,0},{3,1},{4,6},{5,7},{6,4},{7,5},{8,10},{9,11},{10,... | collective-permute-start | bytes 688136 | tf_op jit(solution)/shard_map/ppermute | solution.py:50
  4.3 10.6 %collective-permute-start.1 = (bf16[2,2,32,896]{3,2,1,0:T(8,128)(2,1)}, bf16[2,2,32,896]{3,2,1,0:T(8,128)(2,1)S(1)}, u32[]{:S(2)}, u32[]{:S(2)}) collective-permute-start(bf16[2,2,32,896]{3,2,1,0:T(8,128)(2,1)} %refs_4_), channel_id=1, source_target_pairs={{0,3},{1,0},{2,1},{3,2},{4,5},{5,6},{6,7},{7,4},{8,11},{9,8},{10,9... | collective-permute-start | bytes 688136 | tf_op jit(solution)/shard_map/ppermute | solution.py:50
  4.6 10.4 %collective-permute-start = (bf16[2,2,32,896]{3,2,1,0:T(8,128)(2,1)}, bf16[2,2,32,896]{3,2,1,0:T(8,128)(2,1)S(1)}, u32[]{:S(2)}, u32[]{:S(2)}) collective-permute-start(bf16[2,2,32,896]{3,2,1,0:T(8,128)(2,1)} %refs_4_), channel_id=1, source_target_pairs={{0,1},{1,2},{2,3},{3,0},{4,7},{5,4},{6,5},{7,6},{8,9},{9,10},{10,1... | collective-permute-start | bytes 688136 | tf_op jit(solution)/shard_map/ppermute | solution.py:50
  7.0 8.0 %collective-permute-start.3 = (bf16[2,2,32,896]{3,2,1,0:T(8,128)(2,1)}, bf16[2,2,32,896]{3,2,1,0:T(8,128)(2,1)S(1)}, u32[]{:S(2)}, u32[]{:S(2)}) collective-permute-start(bf16[2,2,32,896]{3,2,1,0:T(8,128)(2,1)} %refs_4_), channel_id=1, source_target_pairs={{0,4},{4,0},{1,5},{5,1},{2,6},{6,2},{3,7},{7,3},{8,12},{12,8},{9,1... | collective-permute-start | bytes 688136 | tf_op jit(solution)/shard_map/ppermute | solution.py:54
  10.5 4.6 %collective-permute-start.4 = (bf16[2,2,32,896]{3,2,1,0:T(8,128)(2,1)S(1)}, bf16[2,2,32,896]{3,2,1,0:T(8,128)(2,1)S(1)}, u32[]{:S(2)}, u32[]{:S(2)}) collective-permute-start(bf16[2,2,32,896]{3,2,1,0:T(8,128)(2,1)S(1)} %collective-permute-done.2.b.a1), channel_id=1, source_target_pairs={{0,4},{4,0},{1,5},{5,1},{2,6},{6,2},{3,7},{7,3},{8,12},{12,8},{9,1... | collective-permute-start | bytes 688136 | tf_op jit(solution)/shard_map/ppermute | solution.py:54
  15.0 2.7 %collective-permute-start.5 = (bf16[2,2,32,896]{3,2,1,0:T(8,128)(2,1)S(1)}, bf16[2,2,32,896]{3,2,1,0:T(8,128)(2,1)S(1)}, u32[]{:S(2)}, u32[]{:S(2)}) collective-permute-start(bf16[2,2,32,896]{3,2,1,0:T(8,128)(2,1)S(1)} %collective-permute-done.a.a2), channel_id=1, source_target_pairs={{0,4},{4,0},{1,5},{5,1},{2,6},{6,2},{3,7},{7,3},{8,12},{12,8},{9,1... | collective-permute-start | bytes 688136 | tf_op jit(solution)/shard_map/ppermute | solution.py:54
  16.4 1.5 %collective-permute-start.6 = (bf16[2,2,32,896]{3,2,1,0:T(8,128)(2,1)S(1)}, bf16[2,2,32,896]{3,2,1,0:T(8,128)(2,1)S(1)}, u32[]{:S(2)}, u32[]{:S(2)}) collective-permute-start(bf16[2,2,32,896]{3,2,1,0:T(8,128)(2,1)S(1)} %collective-permute-done.1.b.a3), channel_id=1, source_target_pairs={{0,4},{4,0},{1,5},{5,1},{2,6},{6,2},{3,7},{7,3},{8,12},{12,8},{9,1... | collective-permute-start | bytes 688136 | tf_op jit(solution)/shard_map/ppermute | solution.py:54
  21.3 2.7 %collective-permute-start.7 = (bf16[512,1024]{1,0:T(8,128)(2,1)S(1)}, bf16[512,1024]{1,0:T(8,128)(2,1)S(1)}, u32[]{:S(2)}, u32[]{:S(2)}) collective-permute-start(bf16[512,1024]{1,0:T(8,128)(2,1)S(1)} %get-tuple-element.117.send), channel_id=1, source_target_pairs={{0,4},{4,0},{1,5},{5,1},{2,6},{6,2},{3,7},{7,3},{8,12},{12,8},{9,1... | collective-permute-start | bytes 3145736 | tf_op jit(solution)/shard_map/ppermute | solution.py:54
  24.9 9.5 %collective-permute-start.8 = (bf16[224,1024]{1,0:T(8,128)(2,1)S(1)}, bf16[224,1024]{1,0:T(8,128)(2,1)S(1)}, u32[]{:S(2)}, u32[]{:S(2)}) collective-permute-start(bf16[224,1024]{1,0:T(8,128)(2,1)S(1)} %shard_map.106), channel_id=1, source_target_pairs={{0,64},{64,128},{128,192},{192,0},{4,196},{68,4},{132,68},{196,132... | collective-permute-start | bytes 1376264 | tf_op jit(solution)/shard_map/ppermute | solution.py:50
  31.8 10.4 %collective-permute-start.13 = (bf16[224,1024]{1,0:T(8,128)(2,1)S(1)}, bf16[224,1024]{1,0:T(8,128)(2,1)S(1)}, u32[]{:S(2)}, u32[]{:S(2)}) collective-permute-start(bf16[224,1024]{1,0:T(8,128)(2,1)S(1)} %get-tuple-element.142), channel_id=1, source_target_pairs={{0,192},{64,0},{128,64},{192,128},{4,68},{68,132},{132,196},{196,4... | collective-permute-start | bytes 1376264 | tf_op jit(solution)/shard_map/ppermute | solution.py:50
  35.3 11.4 %collective-permute-start.9 = (bf16[5,32,1024]{2,1,0:T(8,128)(2,1)S(1)}, bf16[5,32,1024]{2,1,0:T(8,128)(2,1)S(1)}, u32[]{:S(2)}, u32[]{:S(2)}) collective-permute-start(bf16[5,32,1024]{2,1,0:T(8,128)(2,1)S(1)} %get-tuple-element.136), channel_id=1, source_target_pairs={{0,64},{64,128},{128,192},{192,0},{4,196},{68,4},{132,68},{196,132... | collective-permute-start | bytes 983048 | tf_op jit(solution)/shard_map/ppermute | solution.py:50
  38.0 8.7 %collective-permute-start.11 = (bf16[2,2,32,896]{3,2,1,0:T(8,128)(2,1)S(1)}, bf16[2,2,32,896]{3,2,1,0:T(8,128)(2,1)S(1)}, u32[]{:S(2)}, u32[]{:S(2)}) collective-permute-start(bf16[2,2,32,896]{3,2,1,0:T(8,128)(2,1)S(1)} %get-tuple-element.138), channel_id=1, source_target_pairs={{0,1},{1,2},{2,3},{3,0},{4,7},{5,4},{6,5},{7,6},{8,9},{9,10},{10,1... | collective-permute-start | bytes 688136 | tf_op jit(solution)/shard_map/ppermute | solution.py:50
  40.4 6.3 %collective-permute-start.12 = (bf16[2,2,32,896]{3,2,1,0:T(8,128)(2,1)S(1)}, bf16[2,2,32,896]{3,2,1,0:T(8,128)(2,1)S(1)}, u32[]{:S(2)}, u32[]{:S(2)}) collective-permute-start(bf16[2,2,32,896]{3,2,1,0:T(8,128)(2,1)S(1)} %get-tuple-element.139), channel_id=1, source_target_pairs={{0,3},{1,0},{2,1},{3,2},{4,5},{5,6},{6,7},{7,4},{8,11},{9,8},{10,9... | collective-permute-start | bytes 688136 | tf_op jit(solution)/shard_map/ppermute | solution.py:50
  40.4 6.3 %collective-permute-start.10 = (bf16[3,32,1024]{2,1,0:T(8,128)(2,1)S(1)}, bf16[3,32,1024]{2,1,0:T(8,128)(2,1)S(1)}, u32[]{:S(2)}, u32[]{:S(2)}) collective-permute-start(bf16[3,32,1024]{2,1,0:T(8,128)(2,1)S(1)} %get-tuple-element.137), channel_id=1, source_target_pairs={{0,68},{64,132},{128,196},{192,4},{4,192},{68,0},{132,64},{196,128... | collective-permute-start | bytes 589832 | tf_op jit(solution)/shard_map/ppermute | solution.py:50
  43.0 3.6 %collective-permute-start.14 = (bf16[3,32,1024]{2,1,0:T(8,128)(2,1)S(1)}, bf16[3,32,1024]{2,1,0:T(8,128)(2,1)S(1)}, u32[]{:S(2)}, u32[]{:S(2)}) collective-permute-start(bf16[3,32,1024]{2,1,0:T(8,128)(2,1)S(1)} %get-tuple-element.145), channel_id=1, source_target_pairs={{0,4},{4,0},{1,5},{5,1},{2,6},{6,2},{3,7},{7,3},{8,12},{12,8},{9,1... | collective-permute-start | bytes 589832 | tf_op jit(solution)/shard_map/ppermute | solution.py:54
  46.8 8.8 %collective-permute-start.15 = (bf16[3,32,1024]{2,1,0:T(8,128)(2,1)S(1)}, bf16[3,32,1024]{2,1,0:T(8,128)(2,1)S(1)}, u32[]{:S(2)}, u32[]{:S(2)}) collective-permute-start(bf16[3,32,1024]{2,1,0:T(8,128)(2,1)S(1)} %get-tuple-element.148), channel_id=1, source_target_pairs={{0,8},{8,16},{16,24},{24,32},{32,40},{40,48},{48,56},{56,0},{4,60}... | collective-permute-start | bytes 589832 | tf_op jit(solution)/shard_map/ppermute | solution.py:50
  52.5 8.4 %collective-permute-start.17 = (bf16[2,32,1024]{2,1,0:T(8,128)(2,1)S(1)}, bf16[2,32,1024]{2,1,0:T(8,128)(2,1)S(1)}, u32[]{:S(2)}, u32[]{:S(2)}) collective-permute-start(bf16[2,32,1024]{2,1,0:T(8,128)(2,1)S(1)} %get-tuple-element.153), channel_id=1, source_target_pairs={{0,16},{8,24},{16,32},{24,40},{32,48},{40,56},{48,0},{56,8},{4,52}... | collective-permute-start | bytes 393224 | tf_op jit(solution)/shard_map/ppermute | solution.py:50
  55.7 8.8 %collective-permute-start.18 = (bf16[2,32,1024]{2,1,0:T(8,128)(2,1)S(1)}, bf16[2,32,1024]{2,1,0:T(8,128)(2,1)S(1)}, u32[]{:S(2)}, u32[]{:S(2)}) collective-permute-start(bf16[2,32,1024]{2,1,0:T(8,128)(2,1)S(1)} %shard_map.113), channel_id=1, source_target_pairs={{0,24},{8,32},{16,40},{24,48},{32,56},{40,0},{48,8},{56,16},{4,44}... | collective-permute-start | bytes 393224 | tf_op jit(solution)/shard_map/ppermute | solution.py:50
  58.1 8.4 %collective-permute-start.16 = (bf16[2,2,32,896]{3,2,1,0:T(8,128)(2,1)S(1)}, bf16[2,2,32,896]{3,2,1,0:T(8,128)(2,1)S(1)}, u32[]{:S(2)}, u32[]{:S(2)}) collective-permute-start(bf16[2,2,32,896]{3,2,1,0:T(8,128)(2,1)S(1)} %shard_map.114), channel_id=1, source_target_pairs={{0,1},{1,2},{2,3},{3,0},{4,7},{5,4},{6,5},{7,6},{8,9},{9,10},{10,1... | collective-permute-start | bytes 688136 | tf_op jit(solution)/shard_map/ppermute | solution.py:50
  65.1 2.3 %collective-permute-start.19 = (f32[2,14,1024]{2,1,0:T(8,128)S(1)}, f32[2,14,1024]{2,1,0:T(8,128)S(1)}, u32[]{:S(2)}, u32[]{:S(2)}) collective-permute-start(f32[2,14,1024]{2,1,0:T(8,128)S(1)} %get-tuple-element.156), channel_id=1, source_target_pairs={{0,4},{4,0},{1,5},{5,1},{2,6},{6,2},{3,7},{7,3},{8,12},{12,8},{9,1... | collective-permute-start | bytes 344072 | tf_op jit(solution)/shard_map/ppermute | solution.py:54

commit v6 on v5

--- a/solution.py
+++ b/solution.py
@@ -37,6 +37,12 @@
 
 def cost(flops, moved):
     return pl.CostEstimate(flops=flops, bytes_accessed=moved, transcendentals=0)
+
+
+def position():
+    y, z, core = lax.axis_index("y"), lax.axis_index("z"), lax.axis_index("c")
+    sign = 1 - 2 * core
+    return [y] + [lax.rem(y + 4 + by, 4) for by in (2, -sign, sign)] + [z, core]
 
 
 def hop(value, axis, size, step, cross=False):
@@ -182,8 +188,8 @@
     )(flags, *near_by(k1, v1, k2, v2, queries, cotangent))
 
 
-def passage_add(flags, keep, send, total, columns, weights):
-    first = flags[0] == 0
+def passage_add(keep, send, total, columns, weights):
+    first = lax.axis_index("c") == 0
     for (key_w, value_w), start in zip(weights, columns):
         a, b = keep[:, start : start + PART], send[:, start : start + PART]
         total = total + dot(jnp.where(first, a, b), key_w[...], NT)
@@ -191,7 +197,7 @@
     return total
 
 
-def passage_open_body(flags, keep, send, key_hbm, value_hbm, partial, *refs):
+def passage_open_body(keep, send, key_hbm, value_hbm, partial, *refs):
     parts = keep.shape[1] // PART
     rest, (key_w, value_w, sems) = refs[: 2 * parts - 2], refs[2 * parts - 2 :]
     targets = (key_w, value_w) + rest
@@ -205,18 +211,18 @@
         load.start()
     for load in loads[:2]:
         load.wait()
-    partial[...] = passage_add(flags, keep, send, 0.0, (0,), ((key_w, value_w),))
+    partial[...] = passage_add(keep, send, 0.0, (0,), ((key_w, value_w),))
     for load in loads[2:]:
         load.wait()
 
 
-def passage_open(flags, keep, send, key_w, value_w):
+def passage_open(keep, send, key_w, value_w):
     enc, width = key_w.shape
     rest = 2 * (width // PART) - 2
     far = [pltpu.with_memory_space_constraint(a, pltpu.HBM) for a in (key_w, value_w)]
     return pl.pallas_call(
         passage_open_body,
-        in_specs=[SMEM] + [VMEM] * 2 + [HBM] * 2,
+        in_specs=[VMEM] * 2 + [HBM] * 2,
         out_specs=[VMEM] * (1 + rest),
         out_shape=[shape((keep.shape[0], enc), F32)] + [shape((enc, PART), BF)] * rest,
         scratch_shapes=[
@@ -226,14 +232,14 @@
         ],
         compiler_params=params(),
         cost_estimate=cost(2 * 10**9, 5 * 10**6),
-    )(flags, *near_by(keep, send), *far)
-
-
-def passage_close_body(flags, keep, send, partial, *refs):
+    )(*near_by(keep, send), *far)
+
+
+def passage_close_body(keep, send, partial, *refs):
     rest, outs = refs[:-4], refs[-4:]
     pairs = list(zip(rest[::2], rest[1::2]))
     columns = range(PART, keep.shape[1], PART)
-    total = passage_add(flags, keep, send, partial[...], columns, pairs)
+    total = passage_add(keep, send, partial[...], columns, pairs)
     stretches, neigh, group, _ = outs[0].shape
     start = 0
     for c in range(stretches):
@@ -243,15 +249,15 @@
                 start += group
 
 
-def passage_close(flags, keep, send, partial, rest, slab):
+def passage_close(keep, send, partial, rest, slab):
     return pl.pallas_call(
         passage_close_body,
-        in_specs=[SMEM] + [VMEM] * (3 + len(rest)),
+        in_specs=[VMEM] * (3 + len(rest)),
         out_specs=[VMEM] * 4,
         out_shape=[shape(slab, d) for d in (F32, BF, BF, F32)],
         compiler_params=params(),
         cost_estimate=cost(2 * 10**9, 5 * 10**6),
-    )(flags, *near_by(keep, send, partial, *rest))
+    )(*near_by(keep, send, partial, *rest))
 
 
 def weight_body(a0, a1, a2, a3, b0, b1, b2, b3, grads, out, turned, rows):
@@ -275,7 +281,8 @@
     )(*near_by(*slabs, *slabs_other, grads))
 
 
-def split_body(which, place, turned, grads, partial, *outs):
+def split_body(which, turned, grads, partial, *outs):
+    place = position()
     for i, out in zip(which, outs):
         height = out.shape[0]
         here = pl.ds(pl.multiple_of(place[i] * height, 32), height)
@@ -283,16 +290,16 @@
         out[...] = total.astype(out.dtype)
 
 
-def weight_split(place, turned, grads, partial, parts, which, dtypes):
+def weight_split(turned, grads, partial, parts, which, dtypes):
     enc, width = partial.shape
     return pl.pallas_call(
         lambda *refs: split_body(which, *refs),
-        in_specs=[SMEM] + [VMEM] * 3,
+        in_specs=[VMEM] * 3,
         out_specs=[VMEM] * len(which),
         out_shape=[shape((enc // parts, width), d) for d in dtypes],
         compiler_params=params(),
         cost_estimate=cost(10**9, 5 * 10**6),
-    )(place, *near_by(turned, grads, partial))
+    )(*near_by(turned, grads, partial))
 
 
 def add_body(a, b, out):
@@ -309,8 +316,8 @@
     )(*near_by(a, b))
 
 
-def deal_body(place, a, b, ours, theirs):
-    z, core = place[4], place[5]
+def deal_body(a, b, ours, theirs):
+    z, core = position()[4:]
     total = a[...] + b[...].astype(F32)
     height = total.shape[0] // 8
     pad = jnp.zeros((PAD - height, total.shape[1]), F32)
@@ -327,16 +334,16 @@
             theirs[7 - slot] = piece.astype(theirs.dtype)
 
 
-def deal(place, a, b, dtype):
+def deal(a, b, dtype):
     width = a.shape[1]
     return pl.pallas_call(
         deal_body,
-        in_specs=[SMEM] + [VMEM] * 2,
+        in_specs=[VMEM] * 2,
         out_specs=[VMEM] * 2,
         out_shape=[shape((5, PAD, width), dtype), shape((3, PAD, width), BF)],
         compiler_params=params(),
         cost_estimate=cost(0, 0),
-    )(place, *near_by(a, b))
+    )(*near_by(a, b))
 
 
 def fold_body(base, front, cross, front_cross, own, one, two, three):
@@ -383,8 +390,8 @@
     )(*near_by(three, arrived))
 
 
-def finish_body(place, own, one, two, three, stay, give):
-    first = place[5] == 0
+def finish_body(own, one, two, three, stay, give):
+    first = lax.axis_index("c") == 0
     height = own.shape[0]
     half = height // 2
     for k in range(2):
@@ -397,31 +404,29 @@
         give[k] = jnp.where(first, high, low)
 
 
-def finish(place, own, one, two, three):
+def finish(own, one, two, three):
     height, width = own.shape
     dims = (2, height // 2, width)
     return pl.pallas_call(
         finish_body,
-        in_specs=[SMEM] + [VMEM] * 4,
+        in_specs=[VMEM] * 4,
         out_specs=[VMEM] * 2,
         out_shape=[shape(dims, F32)] * 2,
         compiler_params=params(),
         cost_estimate=pl.CostEstimate(flops=2 * 10**10, bytes_accessed=4 * 10**7, transcendentals=0),
-    )(place, *near_by(own, one, two, three))
+    )(*near_by(own, one, two, three))
 
 
 def shards(queries, cotangent, neighbours, present, key_weight, value_weight):
     ny, nz, nx = 4, 8, 4
-    y, z, core = lax.axis_index("y"), lax.axis_index("z"), lax.axis_index("c")
+    core = lax.axis_index("c")
     first = core == 0
-    sign = 1 - 2 * core
-    place = jnp.stack([y, (y + 2) % ny, (y - sign) % ny, (y + sign) % ny, z, core])
     flags = jnp.concatenate([core[None], present.reshape(-1)]).astype(jnp.int32)
     tie = lax.optimization_barrier
 
     own = neighbours
     opposite, behind, ahead = (hop(own, "x", nx, step) for step in (2, 1, -1))
-    flags, place, start = tie((flags, place, own))
+    flags, start = tie((flags, own))
     key_w, value_w, q, g, own = load(key_weight, value_weight, queries, cotangent, start)
     opposite, own = tie((opposite, own))
     k1, v1 = project((own, opposite), key_w, value_w)
@@ -436,23 +441,23 @@
     received = swap(send)
     partial, turned = weight_grad(slabs, others, keep)
     received, partial = tie((received, partial))
-    (far,) = weight_split(place, turned, received, partial, ny, (1,), (BF,))
+    (far,) = weight_split(turned, received, partial, ny, (1,), (BF,))
     far_in = hop(far, "y", ny, 1)
     far, partial = tie((far, partial))
     mine, back, front = weight_split(
-        place, turned, received, partial, ny, (0, 2, 3), (F32, BF, F32)
+        turned, received, partial, ny, (0, 2, 3), (F32, BF, F32)
     )
     keep, send, front = tie((keep, send, front))
-    part, *rest = passage_open(flags, keep, send, key_weight, value_weight)
+    part, *rest = passage_open(keep, send, key_weight, value_weight)
     back, part = tie((back, part))
     back_in = hop(back, "y", ny, -1)
-    p0, p3, p1, p2 = passage_close(flags, keep, send, part, rest, own.shape)
+    p0, p3, p1, p2 = passage_close(keep, send, part, rest, own.shape)
     far_in, p1, p2, p3 = tie((far_in, p1, p2, p3))
-    front, front_cross = deal(place, front, far_in, BF)
+    front, front_cross = deal(front, far_in, BF)
     front, front_cross, mine = tie((front, front_cross, mine))
     front_in = hop(front, "y", ny, 1)
     cross_in = hop(front_cross, "y", ny, 1, cross=True)
-    base, cross = deal(place, mine, back_in, F32)
+    base, cross = deal(mine, back_in, F32)
     cross = swap(cross)
     p1_in = hop(p1, "x", nx, -1)
     front_in, cross_in, beyond, p1_in = tie((front_in, cross_in, hop(p3, "x", nx, 1), p1_in))
@@ -464,7 +469,7 @@
     three, share = tie((relay(three, one_in), share))
     three_in = hop(three, "z", nz, 3)
     returned = [p1_in, hop(share, "x", nx, 1)]
-    stay, give = finish(place, here, one_in, two_in, three_in)
+    stay, give = finish(here, one_in, two_in, three_in)
     other = swap(give)
     neighbour_grad = p0
     for r in returned:

time: 68.4 us -> 66.9 us (0.978)
  Pallas kernels: 19.1 us -> 15.3 us
  starting transfers between devices: 35.1 us -> 36.5 us
  waiting for transfers between devices: 10.7 us -> 11.7 us
    pallas_call x7, Pallas kernels: 9.61 us -> 5.82 us  [the longest x1 2.11 us: passage_open(): pl.pallas_call(passage_open_body, in_specs=[VMEM] * 2 + [HBM] * 2, out_sp...]
    ppermute x13, starting transfers between devices: 28.4 us -> 29.5 us  [hop(): return lax.ppermute(value, ('c', axis) if inner else (axis, 'c'), pairs)]
    ppermute x13, waiting for transfers between devices: 9.22 us -> 10.3 us  [hop(): return lax.ppermute(value, ('c', axis) if inner else (axis, 'c'), pairs)]
  transfers between devices with their start and end apart: 20 -> 20, of which waited for: 7 -> 8; matrix products, arithmetic and copies ran while one was open for 3% -> 2% of each run, Pallas kernels for 22% -> 17%
where the time goes in v6:
time: 66.9 us; the launch traced here: 66.7 us
  starting transfers between devices  36.5 us (55%)
  Pallas kernels  15.3 us (23%)
  waiting for transfers between devices  11.7 us (17%)
  other arithmetic  1.58 us (2%)
  between operations  0.79 us (1%)
  local copies, waits for them, and re-layouts  0.76 us (1%)
    ppermute x13, starting transfers between devices, hop(): return lax.ppermute(value, ('c', axis) if inner else (axis, 'c'), pairs)  29.5 us
    ppermute x13, waiting for transfers between devices, hop(): return lax.ppermute(value, ('c', axis) if inner else (axis, 'c'), pairs)  10.3 us
    ppermute x7, starting transfers between devices, swap(): return lax.ppermute(value, 'c', [(0, 1), (1, 0)])  6.96 us
    pallas_call x1, Pallas kernels, attend(): pl.pallas_call(lambda *refs: attend_body(group, *refs), in_specs=[SMEM] +...  3.42 us
    pallas_call x2, Pallas kernels, project(): pl.pallas_call(project_body, in_specs=[VMEM] * 4, out_specs=[VMEM] * 2, o...  2.49 us
    pallas_call x1, Pallas kernels, load(): pl.pallas_call(load_body, in_specs=[HBM] * len(arrays), out_specs=[VMEM]...  2.24 us
    pallas_call x1, Pallas kernels, passage_open(): pl.pallas_call(passage_open_body, in_specs=[VMEM] * 2 + [HBM] * 2, out_sp...  2.11 us
    pallas_call x1, Pallas kernels, passage_close(): pl.pallas_call(passage_close_body, in_specs=[VMEM] * (3 + len(rest)), out...  1.83 us
  transfers between devices with their start and end apart: 20, of which 8 were waited for; matrix products, arithmetic and copies ran while one was open for 2% of the time, Pallas kernels for 17%

profile of v6, /device:TPU:1, one launch (start us, length us, event | category | flops | bytes accessed | tf_op | source)
XLA Modules:
  0.0 66.7 jit_solution(15832974486383933747)
XLA Ops:
  0.6 3.7 %collective-permute-start.2 = (bf16[2,2,32,896]{3,2,1,0:T(8,128)(2,1)}, bf16[2,2,32,896]{3,2,1,0:T(8,128)(2,1)S(1)}, u32[]{:S(2)}, u32[]{:S(2)}) collective-permute-start(bf16[2,2,32,896]{3,2,1,0:T(8,128)(2,1)} %refs_4_), channel_id=1, source_target_pairs={{0,2},{1,3},{2,0},{3,1},{4,6},{5,7},{6,4},{7,5},{8,10},{9,11},{10,... | collective-permute-start | bytes 688136 | tf_op jit(solution)/shard_map/ppermute | solution.py:56
  4.3 0.3 collective-permute-start.1
  4.6 2.4 %collective-permute-start = (bf16[2,2,32,896]{3,2,1,0:T(8,128)(2,1)}, bf16[2,2,32,896]{3,2,1,0:T(8,128)(2,1)S(1)}, u32[]{:S(2)}, u32[]{:S(2)}) collective-permute-start(bf16[2,2,32,896]{3,2,1,0:T(8,128)(2,1)} %refs_4_), channel_id=1, source_target_pairs={{0,1},{1,2},{2,3},{3,0},{4,7},{5,4},{6,5},{7,6},{8,9},{9,10},{10,1... | collective-permute-start | bytes 688136 | tf_op jit(solution)/shard_map/ppermute | solution.py:56
  7.3 0.8 %reshape.19 = s32[4]{0:T(128)S(1)} reshape(s32[2,2]{1,0:T(2,128)} %param.9) | data formatting | bytes 32 | tf_op jit(solution)/shard_map/reshape | solution.py:424
  8.1 2.2 %shard_map.101 = (bf16[896,1024]{1,0:T(8,128)(2,1)S(1)}, bf16[896,1024]{1,0:T(8,128)(2,1)S(1)}, bf16[128,1024]{1,0:T(8,128)(2,1)S(1)}, bf16[128,1024]{1,0:T(8,128)(2,1)S(1)}, bf16[2,2,32,896]{3,2,1,0:T(8,128)(2,1)S(1)}) custom-call(bf16[896,1024]{1,0:T(8,128)(2,1)} %key_hbm.1, bf16[896,1024]{1,0:T(8,128)(2,1)} %value_hbm.1, bf16[128,1024]{1,0:T(8,128)(2,1)} %refs_2_.1, ...), custom_call_target="tpu_custom_call" | custom-call | tf_op jit(solution)/shard_map/pallas_call | solution.py:111
  10.4 3.3 %collective-permute-start.4 = (bf16[2,2,32,896]{3,2,1,0:T(8,128)(2,1)S(1)}, bf16[2,2,32,896]{3,2,1,0:T(8,128)(2,1)S(1)}, u32[]{:S(2)}, u32[]{:S(2)}) collective-permute-start(bf16[2,2,32,896]{3,2,1,0:T(8,128)(2,1)S(1)} %collective-permute-done.2.b.a1), channel_id=1, source_target_pairs={{0,4},{4,0},{1,5},{5,1},{2,6},{6,2},{3,7},{7,3},{8,12},{12,8},{9,1... | collective-permute-start | bytes 688136 | tf_op jit(solution)/shard_map/ppermute | solution.py:60
  13.6 1.2 %shard_map.102 = (bf16[2,128,1024]{2,1,0:T(8,128)(2,1)S(1)}, bf16[2,128,1024]{2,1,0:T(8,128)(2,1)S(1)}) custom-call(bf16[2,2,32,896]{3,2,1,0:T(8,128)(2,1)S(1)} %get-tuple-element.83.a.a0, bf16[2,2,32,896]{3,2,1,0:T(8,128)(2,1)S(1)} %collective-permute-done.2.b.a1, bf16[896,1024]{1,0:T(8,128)(2,1)S(1)} %get-tuple-element.85.key_w, ...), custom_call_target="tpu_custom_call" | custom-call | tf_op jit(solution)/shard_map/pallas_call | solution.py:134
  15.0 1.4 %collective-permute-start.5 = (bf16[2,2,32,896]{3,2,1,0:T(8,128)(2,1)S(1)}, bf16[2,2,32,896]{3,2,1,0:T(8,128)(2,1)S(1)}, u32[]{:S(2)}, u32[]{:S(2)}) collective-permute-start(bf16[2,2,32,896]{3,2,1,0:T(8,128)(2,1)S(1)} %collective-permute-done.a.a2), channel_id=1, source_target_pairs={{0,4},{4,0},{1,5},{5,1},{2,6},{6,2},{3,7},{7,3},{8,12},{12,8},{9,1... | collective-permute-start | bytes 688136 | tf_op jit(solution)/shard_map/ppermute | solution.py:60
  16.5 1.2 %shard_map.103 = (bf16[2,128,1024]{2,1,0:T(8,128)(2,1)S(1)}, bf16[2,128,1024]{2,1,0:T(8,128)(2,1)S(1)}) custom-call(bf16[2,2,32,896]{3,2,1,0:T(8,128)(2,1)S(1)} %collective-permute-done.a.a2, bf16[2,2,32,896]{3,2,1,0:T(8,128)(2,1)S(1)} %collective-permute-done.1.b.a3, bf16[896,1024]{1,0:T(8,128)(2,1)S(1)} %get-tuple-element.85.key_w, ...), custom_call_target="tpu_custom_call" | custom-call | tf_op jit(solution)/shard_map/pallas_call | solution.py:134
  17.9 3.4 %shard_map.104 = (bf16[128,1024]{1,0:T(8,128)(2,1)}, bf16[128,1024]{1,0:T(8,128)(2,1)}, bf16[512,1024]{1,0:T(8,128)(2,1)S(1)}, bf16[512,1024]{1,0:T(8,128)(2,1)S(1)}) custom-call(s32[5]{0:T(128)S(1)} %pad_add_fusion.refs_0_, bf16[2,128,1024]{2,1,0:T(8,128)(2,1)S(1)} %get-tuple-element.89.refs_1_, bf16[2,128,1024]{2,1,0:T(8,128)(2,1)S(1)} %get-tuple-element.90.refs_2_, ...), custom_call_target="tpu_custom_call" | custom-call | tf_op jit(solution)/shard_map/pallas_call | solution.py:181
  21.3 0.3 collective-permute-start.7
  21.6 1.2 %shard_map.105 = (f32[896,1024]{1,0:T(8,128)S(1)}, bf16[896,512]{1,0:T(8,128)(2,1)S(1)}) custom-call(bf16[2,2,32,896]{3,2,1,0:T(8,128)(2,1)S(1)} %get-tuple-element.83.a.a0, bf16[2,2,32,896]{3,2,1,0:T(8,128)(2,1)S(1)} %collective-permute-done.2.b.a1, bf16[2,2,32,896]{3,2,1,0:T(8,128)(2,1)S(1)} %collective-permute-done.a.a2, ...), custom_call_target="tpu_custom_call" | custom-call | flops 2000000000 | bytes 5000000 | tf_op jit(solution)/shard_map/pallas_call | solution.py:273
  22.8 1.2 %collective-permute-done.7.refs_1_ = bf16[512,1024]{1,0:T(8,128)(2,1)S(1)} collective-permute-done((bf16[512,1024]{1,0:T(8,128)(2,1)S(1)}, bf16[512,1024]{1,0:T(8,128)(2,1)S(1)}, u32[]{:S(2)}, u32[]{:S(2)}) %collective-permute-start.7) | collective-permute-done | bytes 1048608 | tf_op jit(solution)/shard_map/ppermute | solution.py:60
  24.0 0.4 shard_map.106
  24.4 2.8 %collective-permute-start.8 = (bf16[224,1024]{1,0:T(8,128)(2,1)S(1)}, bf16[224,1024]{1,0:T(8,128)(2,1)S(1)}, u32[]{:S(2)}, u32[]{:S(2)}) collective-permute-start(bf16[224,1024]{1,0:T(8,128)(2,1)S(1)} %shard_map.106), channel_id=1, source_target_pairs={{0,64},{64,128},{128,192},{192,0},{4,196},{68,4},{132,68},{196,132... | collective-permute-start | bytes 1376264 | tf_op jit(solution)/shard_map/ppermute | solution.py:56
  27.2 0.9 %shard_map.107 = (f32[224,1024]{1,0:T(8,128)S(1)}, bf16[224,1024]{1,0:T(8,128)(2,1)S(1)}, f32[224,1024]{1,0:T(8,128)S(1)}) custom-call(bf16[896,512]{1,0:T(8,128)(2,1)S(1)} %get-tuple-element.108.refs_0_, bf16[512,1024]{1,0:T(8,128)(2,1)S(1)} %collective-permute-done.7.refs_1_, f32[896,1024]{1,0:T(8,128)S(1)} %get-tuple-element.112.refs_2_), custom_call_target="tpu_custom_call" | custom-call | flops 1000000000 | bytes 5000000 | tf_op jit(solution)/shard_map/pallas_call | solution.py:295
  28.1 2.1 %shard_map.108 = (f32[512,896]{1,0:T(8,128)S(1)}, bf16[896,256]{1,0:T(8,128)(2,1)S(1)}, bf16[896,256]{1,0:T(8,128)(2,1)S(1)}, bf16[896,256]{1,0:T(8,128)(2,1)S(1...) custom-call(bf16[512,1024]{1,0:T(8,128)(2,1)S(1)} %get-tuple-element.114.grads.keep, ...), custom_call_target="tpu_custom_call" | custom-call | flops 2000000000 | bytes 5000000 | tf_op jit(solution)/shard_map/pallas_call | solution.py:223
  30.5 1.8 %shard_map.109 = (f32[2,2,32,896]{3,2,1,0:T(8,128)S(1)}, bf16[2,2,32,896]{3,2,1,0:T(8,128)(2,1)S(1)}, bf16[2,2,32,896]{3,2,1,0:T(8,128)(2,1)S(1)}, f32[2,2,32,896]{3,2,1,0:T(8,128)S(1)}) custom-call(bf16[512,1024]{1,0:T(8,128)(2,1)S(1)} %get-tuple-element.114.grads.keep, bf16[512,1024]{1,0:T(8,128)(2,1)S(1)} %get-tuple-element.115.send, ...), custom_call_target="tpu_custom_call" | custom-call | flops 2000000000 | bytes 5000000 | tf_op jit(solution)/shard_map/pallas_call | solution.py:253
  32.3 0.9 %collective-permute-done.8.b = bf16[224,1024]{1,0:T(8,128)(2,1)S(1)} collective-permute-done((bf16[224,1024]{1,0:T(8,128)(2,1)S(1)}, bf16[224,1024]{1,0:T(8,128)(2,1)S(1)}, u32[]{:S(2)}, u32[]{:S(2)}) %collective-permute-start.8) | collective-permute-done | bytes 458784 | tf_op jit(solution)/shard_map/ppermute | solution.py:56
  33.4 3.5 %collective-permute-start.9 = (bf16[5,32,1024]{2,1,0:T(8,128)(2,1)S(1)}, bf16[5,32,1024]{2,1,0:T(8,128)(2,1)S(1)}, u32[]{:S(2)}, u32[]{:S(2)}) collective-permute-start(bf16[5,32,1024]{2,1,0:T(8,128)(2,1)S(1)} %get-tuple-element.134), channel_id=1, source_target_pairs={{0,64},{64,128},{128,192},{192,0},{4,196},{68,4},{132,68},{196,132... | collective-permute-start | bytes 983048 | tf_op jit(solution)/shard_map/ppermute | solution.py:56
  36.9 2.4 %collective-permute-start.11 = (bf16[2,2,32,896]{3,2,1,0:T(8,128)(2,1)S(1)}, bf16[2,2,32,896]{3,2,1,0:T(8,128)(2,1)S(1)}, u32[]{:S(2)}, u32[]{:S(2)}) collective-permute-start(bf16[2,2,32,896]{3,2,1,0:T(8,128)(2,1)S(1)} %get-tuple-element.136), channel_id=1, source_target_pairs={{0,1},{1,2},{2,3},{3,0},{4,7},{5,4},{6,5},{7,6},{8,9},{9,10},{10,1... | collective-permute-start | bytes 688136 | tf_op jit(solution)/shard_map/ppermute | solution.py:56
  39.3 2.2 %collective-permute-start.10 = (bf16[3,32,1024]{2,1,0:T(8,128)(2,1)S(1)}, bf16[3,32,1024]{2,1,0:T(8,128)(2,1)S(1)}, u32[]{:S(2)}, u32[]{:S(2)}) collective-permute-start(bf16[3,32,1024]{2,1,0:T(8,128)(2,1)S(1)} %get-tuple-element.135), channel_id=1, source_target_pairs={{0,68},{64,132},{128,196},{192,4},{4,192},{68,0},{132,64},{196,128... | collective-permute-start | bytes 589832 | tf_op jit(solution)/shard_map/ppermute | solution.py:56
  41.8 3.8 %collective-permute-done.10.front_cross = bf16[3,32,1024]{2,1,0:T(8,128)(2,1)S(1)} collective-permute-done((bf16[3,32,1024]{2,1,0:T(8,128)(2,1)S(1)}, bf16[3,32,1024]{2,1,0:T(8,128)(2,1)S(1)}, u32[]{:S(2)}, u32[]{:S(2)}) %collective-permute-start.10) | collective-permute-done | bytes 196640 | tf_op jit(solution)/shard_map/ppermute | solution.py:56
  45.7 5.6 %collective-permute-start.15 = (bf16[3,32,1024]{2,1,0:T(8,128)(2,1)S(1)}, bf16[3,32,1024]{2,1,0:T(8,128)(2,1)S(1)}, u32[]{:S(2)}, u32[]{:S(2)}) collective-permute-start(bf16[3,32,1024]{2,1,0:T(8,128)(2,1)S(1)} %get-tuple-element.146), channel_id=1, source_target_pairs={{0,8},{8,16},{16,24},{24,32},{32,40},{40,48},{48,56},{56,0},{4,60}... | collective-permute-start | bytes 589832 | tf_op jit(solution)/shard_map/ppermute | solution.py:56
  51.4 1.2 %collective-permute-start.17 = (bf16[2,32,1024]{2,1,0:T(8,128)(2,1)S(1)}, bf16[2,32,1024]{2,1,0:T(8,128)(2,1)S(1)}, u32[]{:S(2)}, u32[]{:S(2)}) collective-permute-start(bf16[2,32,1024]{2,1,0:T(8,128)(2,1)S(1)} %get-tuple-element.151), channel_id=1, source_target_pairs={{0,16},{8,24},{16,32},{24,40},{32,48},{40,56},{48,0},{56,8},{4,52}... | collective-permute-start | bytes 393224 | tf_op jit(solution)/shard_map/ppermute | solution.py:56
  52.6 1.9 %collective-permute-done.15.arrived.one = bf16[3,32,1024]{2,1,0:T(8,128)(2,1)S(1)} collective-permute-done((bf16[3,32,1024]{2,1,0:T(8,128)(2,1)S(1)}, bf16[3,32,1024]{2,1,0:T(8,128)(2,1)S(1)}, u32[]{:S(2)}, u32[]{:S(2)}) %collective-permute-start.15) | collective-permute-done | bytes 196640 | tf_op jit(solution)/shard_map/ppermute | solution.py:56
  54.6 2.6 %collective-permute-start.18 = (bf16[2,32,1024]{2,1,0:T(8,128)(2,1)S(1)}, bf16[2,32,1024]{2,1,0:T(8,128)(2,1)S(1)}, u32[]{:S(2)}, u32[]{:S(2)}) collective-permute-start(bf16[2,32,1024]{2,1,0:T(8,128)(2,1)S(1)} %shard_map.113), channel_id=1, source_target_pairs={{0,24},{8,32},{16,40},{24,48},{32,56},{40,0},{48,8},{56,16},{4,44}... | collective-permute-start | bytes 393224 | tf_op jit(solution)/shard_map/ppermute | solution.py:56
  57.1 2.7 %collective-permute-start.16 = (bf16[2,2,32,896]{3,2,1,0:T(8,128)(2,1)S(1)}, bf16[2,2,32,896]{3,2,1,0:T(8,128)(2,1)S(1)}, u32[]{:S(2)}, u32[]{:S(2)}) collective-permute-start(bf16[2,2,32,896]{3,2,1,0:T(8,128)(2,1)S(1)} %shard_map.114), channel_id=1, source_target_pairs={{0,1},{1,2},{2,3},{3,0},{4,7},{5,4},{6,5},{7,6},{8,9},{9,10},{10,1... | collective-permute-start | bytes 688136 | tf_op jit(solution)/shard_map/ppermute | solution.py:56
  59.9 3.5 %collective-permute-done.18.three = bf16[2,32,1024]{2,1,0:T(8,128)(2,1)S(1)} collective-permute-done((bf16[2,32,1024]{2,1,0:T(8,128)(2,1)S(1)}, bf16[2,32,1024]{2,1,0:T(8,128)(2,1)S(1)}, u32[]{:S(2)}, u32[]{:S(2)}) %collective-permute-start.18) | collective-permute-done | bytes 131104 | tf_op jit(solution)/shard_map/ppermute | solution.py:56
  63.5 1.5 %collective-permute-start.19 = (f32[2,14,1024]{2,1,0:T(8,128)S(1)}, f32[2,14,1024]{2,1,0:T(8,128)S(1)}, u32[]{:S(2)}, u32[]{:S(2)}) collective-permute-start(f32[2,14,1024]{2,1,0:T(8,128)S(1)} %get-tuple-element.154), channel_id=1, source_target_pairs={{0,4},{4,0},{1,5},{5,1},{2,6},{6,2},{3,7},{7,3},{8,12},{12,8},{9,1... | collective-permute-start | bytes 344072 | tf_op jit(solution)/shard_map/ppermute | solution.py:60
  65.0 0.8 %convert_add_fusion = f32[2,2,32,896]{3,2,1,0:T(8,128)} fusion(bf16[2,2,32,896]{3,2,1,0:T(8,128)(2,1)S(1)} %collective-permute-done.16, f32[2,2,32,896]{3,2,1,0:T(8,128)S(1)} %get-tuple-element.125, bf16[2,2,32,896]{3,2,1,0:T(8,128)(2,1)S(1)} %collective-permute-done.12), kind=kLoop, calls=%fused_computation | loop fusion | flops 458752 | bytes 1376256 | tf_op jit(solution)/shard_map/add | solution.py:476
  66.0 0.7 %select_bitcast_fusion = (f32[14,1024]{1,0:T(8,128)}, f32[14,1024]{1,0:T(8,128)}) fusion(pred[]{:T(512)S(6)} %eq.3, f32[2,14,1024]{2,1,0:T(8,128)S(1)} %collective-permute-done.19, f32[2,14,1024]{2,1,0:T(8,128)S(1)} %get-tuple-element.153), kind=kLoop, calls=%fused_computation.3 | loop fusion | flops 57344 | bytes 344065 | tf_op jit(solution)/shard_map/jit(_where)/select_n | solution.py:483
  (27 shorter events, 2.0 us)
Async XLA Ops:
  0.6 9.7 %collective-permute-start.2 = (bf16[2,2,32,896]{3,2,1,0:T(8,128)(2,1)}, bf16[2,2,32,896]{3,2,1,0:T(8,128)(2,1)S(1)}, u32[]{:S(2)}, u32[]{:S(2)}) collective-permute-start(bf16[2,2,32,896]{3,2,1,0:T(8,128)(2,1)} %refs_4_), channel_id=1, source_target_pairs={{0,2},{1,3},{2,0},{3,1},{4,6},{5,7},{6,4},{7,5},{8,10},{9,11},{10,... | collective-permute-start | bytes 688136 | tf_op jit(solution)/shard_map/ppermute | solution.py:56
  4.3 10.6 %collective-permute-start.1 = (bf16[2,2,32,896]{3,2,1,0:T(8,128)(2,1)}, bf16[2,2,32,896]{3,2,1,0:T(8,128)(2,1)S(1)}, u32[]{:S(2)}, u32[]{:S(2)}) collective-permute-start(bf16[2,2,32,896]{3,2,1,0:T(8,128)(2,1)} %refs_4_), channel_id=1, source_target_pairs={{0,3},{1,0},{2,1},{3,2},{4,5},{5,6},{6,7},{7,4},{8,11},{9,8},{10,9... | collective-permute-start | bytes 688136 | tf_op jit(solution)/shard_map/ppermute | solution.py:56
  4.6 10.4 %collective-permute-start = (bf16[2,2,32,896]{3,2,1,0:T(8,128)(2,1)}, bf16[2,2,32,896]{3,2,1,0:T(8,128)(2,1)S(1)}, u32[]{:S(2)}, u32[]{:S(2)}) collective-permute-start(bf16[2,2,32,896]{3,2,1,0:T(8,128)(2,1)} %refs_4_), channel_id=1, source_target_pairs={{0,1},{1,2},{2,3},{3,0},{4,7},{5,4},{6,5},{7,6},{8,9},{9,10},{10,1... | collective-permute-start | bytes 688136 | tf_op jit(solution)/shard_map/ppermute | solution.py:56
  7.0 8.0 %collective-permute-start.3 = (bf16[2,2,32,896]{3,2,1,0:T(8,128)(2,1)}, bf16[2,2,32,896]{3,2,1,0:T(8,128)(2,1)S(1)}, u32[]{:S(2)}, u32[]{:S(2)}) collective-permute-start(bf16[2,2,32,896]{3,2,1,0:T(8,128)(2,1)} %refs_4_), channel_id=1, source_target_pairs={{0,4},{4,0},{1,5},{5,1},{2,6},{6,2},{3,7},{7,3},{8,12},{12,8},{9,1... | collective-permute-start | bytes 688136 | tf_op jit(solution)/shard_map/ppermute | solution.py:60
  10.4 4.6 %collective-permute-start.4 = (bf16[2,2,32,896]{3,2,1,0:T(8,128)(2,1)S(1)}, bf16[2,2,32,896]{3,2,1,0:T(8,128)(2,1)S(1)}, u32[]{:S(2)}, u32[]{:S(2)}) collective-permute-start(bf16[2,2,32,896]{3,2,1,0:T(8,128)(2,1)S(1)} %collective-permute-done.2.b.a1), channel_id=1, source_target_pairs={{0,4},{4,0},{1,5},{5,1},{2,6},{6,2},{3,7},{7,3},{8,12},{12,8},{9,1... | collective-permute-start | bytes 688136 | tf_op jit(solution)/shard_map/ppermute | solution.py:60
  15.0 2.7 %collective-permute-start.5 = (bf16[2,2,32,896]{3,2,1,0:T(8,128)(2,1)S(1)}, bf16[2,2,32,896]{3,2,1,0:T(8,128)(2,1)S(1)}, u32[]{:S(2)}, u32[]{:S(2)}) collective-permute-start(bf16[2,2,32,896]{3,2,1,0:T(8,128)(2,1)S(1)} %collective-permute-done.a.a2), channel_id=1, source_target_pairs={{0,4},{4,0},{1,5},{5,1},{2,6},{6,2},{3,7},{7,3},{8,12},{12,8},{9,1... | collective-permute-start | bytes 688136 | tf_op jit(solution)/shard_map/ppermute | solution.py:60
  16.4 1.5 %collective-permute-start.6 = (bf16[2,2,32,896]{3,2,1,0:T(8,128)(2,1)S(1)}, bf16[2,2,32,896]{3,2,1,0:T(8,128)(2,1)S(1)}, u32[]{:S(2)}, u32[]{:S(2)}) collective-permute-start(bf16[2,2,32,896]{3,2,1,0:T(8,128)(2,1)S(1)} %collective-permute-done.1.b.a3), channel_id=1, source_target_pairs={{0,4},{4,0},{1,5},{5,1},{2,6},{6,2},{3,7},{7,3},{8,12},{12,8},{9,1... | collective-permute-start | bytes 688136 | tf_op jit(solution)/shard_map/ppermute | solution.py:60
  21.3 2.7 %collective-permute-start.7 = (bf16[512,1024]{1,0:T(8,128)(2,1)S(1)}, bf16[512,1024]{1,0:T(8,128)(2,1)S(1)}, u32[]{:S(2)}, u32[]{:S(2)}) collective-permute-start(bf16[512,1024]{1,0:T(8,128)(2,1)S(1)} %get-tuple-element.115.send), channel_id=1, source_target_pairs={{0,4},{4,0},{1,5},{5,1},{2,6},{6,2},{3,7},{7,3},{8,12},{12,8},{9,1... | collective-permute-start | bytes 3145736 | tf_op jit(solution)/shard_map/ppermute | solution.py:60
  24.4 8.8 %collective-permute-start.8 = (bf16[224,1024]{1,0:T(8,128)(2,1)S(1)}, bf16[224,1024]{1,0:T(8,128)(2,1)S(1)}, u32[]{:S(2)}, u32[]{:S(2)}) collective-permute-start(bf16[224,1024]{1,0:T(8,128)(2,1)S(1)} %shard_map.106), channel_id=1, source_target_pairs={{0,64},{64,128},{128,192},{192,0},{4,196},{68,4},{132,68},{196,132... | collective-permute-start | bytes 1376264 | tf_op jit(solution)/shard_map/ppermute | solution.py:56
  30.2 11.3 %collective-permute-start.13 = (bf16[224,1024]{1,0:T(8,128)(2,1)S(1)}, bf16[224,1024]{1,0:T(8,128)(2,1)S(1)}, u32[]{:S(2)}, u32[]{:S(2)}) collective-permute-start(bf16[224,1024]{1,0:T(8,128)(2,1)S(1)} %get-tuple-element.140), channel_id=1, source_target_pairs={{0,192},{64,0},{128,64},{192,128},{4,68},{68,132},{132,196},{196,4... | collective-permute-start | bytes 1376264 | tf_op jit(solution)/shard_map/ppermute | solution.py:56
  33.4 12.2 %collective-permute-start.9 = (bf16[5,32,1024]{2,1,0:T(8,128)(2,1)S(1)}, bf16[5,32,1024]{2,1,0:T(8,128)(2,1)S(1)}, u32[]{:S(2)}, u32[]{:S(2)}) collective-permute-start(bf16[5,32,1024]{2,1,0:T(8,128)(2,1)S(1)} %get-tuple-element.134), channel_id=1, source_target_pairs={{0,64},{64,128},{128,192},{192,0},{4,196},{68,4},{132,68},{196,132... | collective-permute-start | bytes 983048 | tf_op jit(solution)/shard_map/ppermute | solution.py:56
  36.9 8.7 %collective-permute-start.11 = (bf16[2,2,32,896]{3,2,1,0:T(8,128)(2,1)S(1)}, bf16[2,2,32,896]{3,2,1,0:T(8,128)(2,1)S(1)}, u32[]{:S(2)}, u32[]{:S(2)}) collective-permute-start(bf16[2,2,32,896]{3,2,1,0:T(8,128)(2,1)S(1)} %get-tuple-element.136), channel_id=1, source_target_pairs={{0,1},{1,2},{2,3},{3,0},{4,7},{5,4},{6,5},{7,6},{8,9},{9,10},{10,1... | collective-permute-start | bytes 688136 | tf_op jit(solution)/shard_map/ppermute | solution.py:56
  39.3 6.3 %collective-permute-start.12 = (bf16[2,2,32,896]{3,2,1,0:T(8,128)(2,1)S(1)}, bf16[2,2,32,896]{3,2,1,0:T(8,128)(2,1)S(1)}, u32[]{:S(2)}, u32[]{:S(2)}) collective-permute-start(bf16[2,2,32,896]{3,2,1,0:T(8,128)(2,1)S(1)} %get-tuple-element.137), channel_id=1, source_target_pairs={{0,3},{1,0},{2,1},{3,2},{4,5},{5,6},{6,7},{7,4},{8,11},{9,8},{10,9... | collective-permute-start | bytes 688136 | tf_op jit(solution)/shard_map/ppermute | solution.py:56
  39.3 6.3 %collective-permute-start.10 = (bf16[3,32,1024]{2,1,0:T(8,128)(2,1)S(1)}, bf16[3,32,1024]{2,1,0:T(8,128)(2,1)S(1)}, u32[]{:S(2)}, u32[]{:S(2)}) collective-permute-start(bf16[3,32,1024]{2,1,0:T(8,128)(2,1)S(1)} %get-tuple-element.135), channel_id=1, source_target_pairs={{0,68},{64,132},{128,196},{192,4},{4,192},{68,0},{132,64},{196,128... | collective-permute-start | bytes 589832 | tf_op jit(solution)/shard_map/ppermute | solution.py:56
  41.7 3.9 %collective-permute-start.14 = (bf16[3,32,1024]{2,1,0:T(8,128)(2,1)S(1)}, bf16[3,32,1024]{2,1,0:T(8,128)(2,1)S(1)}, u32[]{:S(2)}, u32[]{:S(2)}) collective-permute-start(bf16[3,32,1024]{2,1,0:T(8,128)(2,1)S(1)} %get-tuple-element.143), channel_id=1, source_target_pairs={{0,4},{4,0},{1,5},{5,1},{2,6},{6,2},{3,7},{7,3},{8,12},{12,8},{9,1... | collective-permute-start | bytes 589832 | tf_op jit(solution)/shard_map/ppermute | solution.py:60
  45.7 8.8 %collective-permute-start.15 = (bf16[3,32,1024]{2,1,0:T(8,128)(2,1)S(1)}, bf16[3,32,1024]{2,1,0:T(8,128)(2,1)S(1)}, u32[]{:S(2)}, u32[]{:S(2)}) collective-permute-start(bf16[3,32,1024]{2,1,0:T(8,128)(2,1)S(1)} %get-tuple-element.146), channel_id=1, source_target_pairs={{0,8},{8,16},{16,24},{24,32},{32,40},{40,48},{48,56},{56,0},{4,60}... | collective-permute-start | bytes 589832 | tf_op jit(solution)/shard_map/ppermute | solution.py:56
  51.4 8.5 %collective-permute-start.17 = (bf16[2,32,1024]{2,1,0:T(8,128)(2,1)S(1)}, bf16[2,32,1024]{2,1,0:T(8,128)(2,1)S(1)}, u32[]{:S(2)}, u32[]{:S(2)}) collective-permute-start(bf16[2,32,1024]{2,1,0:T(8,128)(2,1)S(1)} %get-tuple-element.151), channel_id=1, source_target_pairs={{0,16},{8,24},{16,32},{24,40},{32,48},{40,56},{48,0},{56,8},{4,52}... | collective-permute-start | bytes 393224 | tf_op jit(solution)/shard_map/ppermute | solution.py:56
  54.6 8.8 %collective-permute-start.18 = (bf16[2,32,1024]{2,1,0:T(8,128)(2,1)S(1)}, bf16[2,32,1024]{2,1,0:T(8,128)(2,1)S(1)}, u32[]{:S(2)}, u32[]{:S(2)}) collective-permute-start(bf16[2,32,1024]{2,1,0:T(8,128)(2,1)S(1)} %shard_map.113), channel_id=1, source_target_pairs={{0,24},{8,32},{16,40},{24,48},{32,56},{40,0},{48,8},{56,16},{4,44}... | collective-permute-start | bytes 393224 | tf_op jit(solution)/shard_map/ppermute | solution.py:56
  57.1 7.9 %collective-permute-start.16 = (bf16[2,2,32,896]{3,2,1,0:T(8,128)(2,1)S(1)}, bf16[2,2,32,896]{3,2,1,0:T(8,128)(2,1)S(1)}, u32[]{:S(2)}, u32[]{:S(2)}) collective-permute-start(bf16[2,2,32,896]{3,2,1,0:T(8,128)(2,1)S(1)} %shard_map.114), channel_id=1, source_target_pairs={{0,1},{1,2},{2,3},{3,0},{4,7},{5,4},{6,5},{7,6},{8,9},{9,10},{10,1... | collective-permute-start | bytes 688136 | tf_op jit(solution)/shard_map/ppermute | solution.py:56
  63.5 2.5 %collective-permute-start.19 = (f32[2,14,1024]{2,1,0:T(8,128)S(1)}, f32[2,14,1024]{2,1,0:T(8,128)S(1)}, u32[]{:S(2)}, u32[]{:S(2)}) collective-permute-start(f32[2,14,1024]{2,1,0:T(8,128)S(1)} %get-tuple-element.154), channel_id=1, source_target_pairs={{0,4},{4,0},{1,5},{5,1},{2,6},{6,2},{3,7},{7,3},{8,12},{12,8},{9,1... | collective-permute-start | bytes 344072 | tf_op jit(solution)/shard_map/ppermute | solution.py:60
